TPU v7x, 32 devices: a whole 2x2x4 slice. The times are simulated.
32 devices in a mesh: dp: 8 (over z, x), head: 4 (over y, core).
Axes of the slice: x: 2, y: 2, z: 4, core: 2. Of those that a mesh axis runs over, the one named last changes fastest.
Arguments:
- radar: bfloat16 [256, 136, 768], P(('dp', 'head')), may hold values from -6 to 6
- optical: bfloat16 [256, 136, 768], P(('dp', 'head')), may hold values from -6 to 6
- cotangent: bfloat16 [256, 136, 768], P(('dp', 'head')), may hold values from -6 to 6
- radar_ratio: int32 [256], P('dp'), may hold values from 40 to 90
- optical_ratio: int32 [256], P('dp'), may hold values from 40 to 90
- radar_patches: int32 [256, 136], P('dp'), may hold values from 0 to 224, as said below
- optical_patches: int32 [256, 136], P('dp'), may hold values from 0 to 224, as said below
- pairing: int32 [256], P('dp'), may hold values from 0 to 31, as said below
- norm_gain: bfloat16 [3, 768], replicated, may hold values from 0.5 to 1.5
- norm_bias: bfloat16 [3, 768], replicated, may hold values from -1.75 to 1.75
- self_qkv: bfloat16 [768, 2304], replicated, may hold values from -0.21875 to 0.21875
- self_out: bfloat16 [768, 768], replicated, may hold values from -0.875 to 0.875
- cross_q: bfloat16 [768, 768], replicated, may hold values from -0.21875 to 0.21875
- cross_kv: bfloat16 [768, 1536], replicated, may hold values from -0.21875 to 0.21875
- cross_out: bfloat16 [768, 768], replicated, may hold values from -0.875 to 0.875
- mlp_in: bfloat16 [768, 3072], replicated, may hold values from -0.21875 to 0.21875
- mlp_in_bias: bfloat16 [3072], replicated, may hold values from -3 to 3
- mlp_out: bfloat16 [3072, 768], replicated, may hold values from -0.109375 to 0.109375
- mlp_out_bias: bfloat16 [768], replicated, may hold values from -1.75 to 1.75
Outputs:
- mixed: bfloat16 [256, 136, 768], P(('dp', 'head'))
- radar_grad: bfloat16 [256, 136, 768], P(('dp', 'head'))
- optical_grad: bfloat16 [256, 136, 768], P(('dp', 'head'))
- norm_gain_grad: bfloat16 [3, 768], replicated
- norm_bias_grad: bfloat16 [3, 768], replicated
- self_qkv_grad: bfloat16 [768, 2304], replicated
- self_out_grad: bfloat16 [768, 768], replicated
- cross_q_grad: bfloat16 [768, 768], replicated
- cross_kv_grad: bfloat16 [768, 1536], replicated
- cross_out_grad: bfloat16 [768, 768], replicated
- mlp_in_grad: bfloat16 [768, 3072], replicated
- mlp_in_bias_grad: bfloat16 [3072], replicated
- mlp_out_grad: bfloat16 [3072, 768], replicated
- mlp_out_bias_grad: bfloat16 [768], replicated
Inputs may be any that keep to these rules, and one draw needn't show every extreme that they name: `radar_patches`: each row holds distinct patch numbers of the 15 x 15 grid in row-major order; slot a holds a visible patch when a is below the image's visible count. `optical_patches`: each row holds distinct patch numbers of the 15 x 15 grid in row-major order; slot a holds a visible patch when a is below the image's visible count. Within each aligned block of 32 images the values are a permutation of the block's places: radar image b is paired with optical image 32 * (b // 32) + pairing[b].
All inputs are finite; a program needn't handle non-finite values.
Results may differ from a plain program's by a relative error of at most 0.019.
Values may be sent and summed in bfloat16 or wider, within the bound.
No kernel may reach another device: no remote copies, remote signals or barrier semaphores. Data moves between devices by JAX's collectives and lax.ppermute only.
A program may use at most 320 MiB of HBM per device.

v0:
```python
from functools import partial
import math

import jax
import jax.numpy as jnp
from jax import lax
from jax.sharding import PartitionSpec as P

HEADS = 12
GRID = 15


def visible_count(ratio):
    return GRID * GRID * (100 - ratio) // 100


def head_slopes():
    return 2.0 ** (-8.0 * (jnp.arange(HEADS, dtype=jnp.float32) + 1.0) / HEADS)


def patch_distance(query_patch, key_patch):
    query_row = (query_patch // GRID).astype(jnp.float32)
    query_column = (query_patch % GRID).astype(jnp.float32)
    key_row = (key_patch // GRID).astype(jnp.float32)
    key_column = (key_patch % GRID).astype(jnp.float32)
    delta_row = query_row[..., :, None] - key_row[..., None, :]
    delta_column = query_column[..., :, None] - key_column[..., None, :]
    return jnp.sqrt(delta_row * delta_row + delta_column * delta_column)


def matmul(left, right):
    return jnp.dot(left, right, preferred_element_type=jnp.float32)


def transposed_product(left, right):
    return lax.dot_general(
        left, right, (((left.ndim - 1,), (1,)), ((), ())), preferred_element_type=jnp.float32
    )


def row_product(left, right):
    left_rows = left.reshape(-1, left.shape[-1])
    right_rows = right.reshape(-1, right.shape[-1])
    return lax.dot_general(
        left_rows, right_rows, (((0,), (0,)), ((), ())), preferred_element_type=jnp.float32
    )


def norm_forward(values, gain, shift):
    centre = values - jnp.mean(values, axis=-1, keepdims=True)
    inverse = lax.rsqrt(jnp.mean(centre * centre, axis=-1, keepdims=True) + 1e-06)
    scaled = centre * inverse
    return (scaled * gain + shift, scaled, inverse)


def norm_backward(grad_normed, scaled, inverse, gain):
    weighted = grad_normed * gain
    grad_input = inverse * (
        weighted
        - jnp.mean(weighted, axis=-1, keepdims=True)
        - scaled * jnp.mean(weighted * scaled, axis=-1, keepdims=True)
    )
    width = grad_normed.shape[-1]
    gain_term = jnp.sum((grad_normed * scaled).reshape(-1, width), axis=0)
    shift_term = jnp.sum(grad_normed.reshape(-1, width), axis=0)
    return (grad_input, gain_term, shift_term)


def attention_scores(query, keys, bias, live_keys):
    scale = 1.0 / math.sqrt(query.shape[-1])
    scores = (
        jnp.einsum("bqhd,bkhd->bhqk", query, keys, preferred_element_type=jnp.float32) * scale
        + bias
    )
    return jnp.where(live_keys[:, None, None, :], scores, -1e30)


def attention_forward(query, keys, values, bias, live_keys):
    scores = attention_scores(query, keys, bias, live_keys)
    log_total = jax.nn.logsumexp(scores, axis=-1, keepdims=True)
    weights = jnp.exp(scores - log_total).astype(jnp.bfloat16)
    mixed_heads = jnp.einsum("bhqk,bkhd->bqhd", weights, values, preferred_element_type=jnp.float32)
    return (mixed_heads.astype(jnp.bfloat16), log_total)


def attention_backward(query, keys, values, bias, live_keys, log_total, grad_mixed):
    scale = 1.0 / math.sqrt(query.shape[-1])
    weights = jnp.exp(attention_scores(query, keys, bias, live_keys) - log_total)
    grad_values = jnp.einsum(
        "bhqk,bqhd->bkhd",
        weights.astype(jnp.bfloat16),
        grad_mixed,
        preferred_element_type=jnp.float32,
    ).astype(jnp.bfloat16)
    grad_weights = jnp.einsum(
        "bqhd,bkhd->bhqk", grad_mixed, values, preferred_element_type=jnp.float32
    )
    grad_scores = weights * (grad_weights - jnp.sum(weights * grad_weights, axis=-1, keepdims=True))
    grad_scores = grad_scores.astype(jnp.bfloat16)
    grad_query = (
        jnp.einsum("bhqk,bkhd->bqhd", grad_scores, keys, preferred_element_type=jnp.float32) * scale
    ).astype(jnp.bfloat16)
    grad_keys = (
        jnp.einsum("bhqk,bqhd->bkhd", grad_scores, query, preferred_element_type=jnp.float32)
        * scale
    ).astype(jnp.bfloat16)
    return (grad_query, grad_keys, grad_values)


def body(
    radar,
    optical,
    cotangent,
    radar_ratio,
    optical_ratio,
    radar_patches,
    optical_patches,
    pairing,
    norm_gain,
    norm_bias,
    self_qkv,
    self_out,
    cross_q,
    cross_kv,
    cross_out,
    mlp_in,
    mlp_in_bias,
    mlp_out,
    mlp_out_bias,
):
    images, slots, width = radar.shape
    head_size = width // HEADS
    head_groups = lax.axis_size("head")
    local_heads = HEADS // head_groups
    local_width = local_heads * head_size
    group_images = images * head_groups
    start = lax.axis_index("head") * images
    slopes = head_slopes()
    gains = norm_gain.astype(jnp.float32)
    shifts = norm_bias.astype(jnp.float32)
    slot_ids = jnp.arange(slots, dtype=jnp.int32)
    radar_visible = visible_count(radar_ratio)
    optical_visible = visible_count(optical_ratio)
    own_live = slot_ids[None, :] < lax.dynamic_slice_in_dim(radar_visible, start, images)[:, None]
    own_patches = lax.dynamic_slice_in_dim(radar_patches, start, images, 0)
    radar_input = radar.astype(jnp.float32)
    normed_first, scaled_first, inverse_first = norm_forward(radar_input, gains[0], shifts[0])
    normed_first = normed_first.astype(jnp.bfloat16)
    packed = (
        matmul(normed_first, self_qkv)
        .astype(jnp.bfloat16)
        .reshape(images, slots, 3, HEADS, head_size)
    )
    self_bias = -slopes[None, :, None, None] * patch_distance(own_patches, own_patches)[:, None]
    self_mixed, self_total = attention_forward(
        packed[:, :, 0], packed[:, :, 1], packed[:, :, 2], self_bias, own_live
    )
    self_mixed = self_mixed.reshape(images, slots, width)
    first = radar_input + matmul(self_mixed, self_out)
    normed_second, scaled_second, inverse_second = norm_forward(first, gains[1], shifts[1])
    normed_second = normed_second.astype(jnp.bfloat16)
    query_cross = matmul(normed_second, cross_q).astype(jnp.bfloat16)

    def to_heads(values):
        return values.reshape(images, slots, head_groups, local_width)

    def unfold(values):
        return values.reshape(group_images, slots, local_heads, head_size)

    def fold_back(values):
        return values.reshape(group_images, slots, 1, local_width)

    keys_cross = matmul(optical, cross_kv[:, :width]).astype(jnp.bfloat16)
    values_cross = matmul(optical, cross_kv[:, width:]).astype(jnp.bfloat16)
    query_heads, keys_heads, values_heads = (
        lax.all_to_all(to_heads(query_cross), "head", split_axis=2, concat_axis=0, tiled=True),
        lax.all_to_all(to_heads(keys_cross), "head", split_axis=2, concat_axis=0, tiled=True),
        lax.all_to_all(to_heads(values_cross), "head", split_axis=2, concat_axis=0, tiled=True),
    )
    query_heads = unfold(query_heads)
    keys_paired = unfold(keys_heads)[pairing]
    values_paired = unfold(values_heads)[pairing]
    local_slopes = lax.dynamic_slice_in_dim(
        slopes, lax.axis_index("head") * local_heads, local_heads
    )
    cross_bias = (
        -local_slopes[None, :, None, None]
        * patch_distance(radar_patches, optical_patches[pairing])[:, None]
    )
    cross_live = slot_ids[None, :] < optical_visible[pairing][:, None]
    cross_mixed, cross_total = attention_forward(
        query_heads, keys_paired, values_paired, cross_bias, cross_live
    )
    cross_back = lax.all_to_all(
        fold_back(cross_mixed), "head", split_axis=0, concat_axis=2, tiled=True
    ).reshape(images, slots, width)
    second = first + matmul(cross_back, cross_out)
    normed_third, scaled_third, inverse_third = norm_forward(second, gains[2], shifts[2])
    normed_third = normed_third.astype(jnp.bfloat16)
    inner = matmul(normed_third, mlp_in) + mlp_in_bias.astype(jnp.float32)
    activated = jax.nn.gelu(inner, approximate=False).astype(jnp.bfloat16)
    output = second + (matmul(activated, mlp_out) + mlp_out_bias.astype(jnp.float32))
    mixed = jnp.where(own_live[:, :, None], output, 0.0).astype(jnp.bfloat16)
    grad_output = jnp.where(own_live[:, :, None], cotangent.astype(jnp.float32), 0.0)
    grad_branch = grad_output.astype(jnp.bfloat16)
    grad_mlp_out_bias = jnp.sum(grad_branch.reshape(-1, width), axis=0, dtype=jnp.float32)
    grad_mlp_out = row_product(activated, grad_branch)
    grad_activated = transposed_product(grad_branch, mlp_out).astype(jnp.bfloat16)
    unused_value, gelu_back = jax.vjp(partial(jax.nn.gelu, approximate=False), inner)
    grad_inner = gelu_back(grad_activated.astype(jnp.float32))[0].astype(jnp.bfloat16)
    grad_mlp_in_bias = jnp.sum(
        grad_inner.reshape(-1, grad_inner.shape[-1]), axis=0, dtype=jnp.float32
    )
    grad_mlp_in = row_product(normed_third, grad_inner)
    grad_third, gain_third, shift_third = norm_backward(
        transposed_product(grad_inner, mlp_in), scaled_third, inverse_third, gains[2]
    )
    grad_second = grad_output + grad_third
    grad_cross_branch = grad_second.astype(jnp.bfloat16)
    grad_cross_out = row_product(cross_back, grad_cross_branch)
    grad_cross_mixed = transposed_product(grad_cross_branch, cross_out).astype(jnp.bfloat16)
    grad_heads = lax.all_to_all(
        to_heads(grad_cross_mixed), "head", split_axis=2, concat_axis=0, tiled=True
    )
    grad_query_heads, grad_keys_paired, grad_values_paired = attention_backward(
        query_heads,
        keys_paired,
        values_paired,
        cross_bias,
        cross_live,
        cross_total,
        unfold(grad_heads),
    )
    inverse_pairing = jnp.argsort(pairing)
    grad_query_cross, grad_keys_cross, grad_values_cross = (
        lax.all_to_all(
            fold_back(grad_query_heads), "head", split_axis=0, concat_axis=2, tiled=True
        ),
        lax.all_to_all(
            fold_back(grad_keys_paired[inverse_pairing]),
            "head",
            split_axis=0,
            concat_axis=2,
            tiled=True,
        ),
        lax.all_to_all(
            fold_back(grad_values_paired[inverse_pairing]),
            "head",
            split_axis=0,
            concat_axis=2,
            tiled=True,
        ),
    )
    grad_query_cross = grad_query_cross.reshape(images, slots, width)
    grad_keys_cross = grad_keys_cross.reshape(images, slots, width)
    grad_values_cross = grad_values_cross.reshape(images, slots, width)
    grad_cross_kv = jnp.concatenate(
        (row_product(optical, grad_keys_cross), row_product(optical, grad_values_cross)), axis=1
    )
    optical_grad = (
        transposed_product(grad_keys_cross, cross_kv[:, :width])
        + transposed_product(grad_values_cross, cross_kv[:, width:])
    ).astype(jnp.bfloat16)
    grad_cross_q = row_product(normed_second, grad_query_cross)
    grad_second_norm, gain_second, shift_second = norm_backward(
        transposed_product(grad_query_cross, cross_q), scaled_second, inverse_second, gains[1]
    )
    grad_first = grad_second + grad_second_norm
    grad_self_branch = grad_first.astype(jnp.bfloat16)
    grad_self_out = row_product(self_mixed, grad_self_branch)
    grad_self_mixed = transposed_product(grad_self_branch, self_out).astype(jnp.bfloat16)
    grad_self_mixed = grad_self_mixed.reshape(images, slots, HEADS, head_size)
    grad_query, grad_keys, grad_values = attention_backward(
        packed[:, :, 0],
        packed[:, :, 1],
        packed[:, :, 2],
        self_bias,
        own_live,
        self_total,
        grad_self_mixed,
    )
    grad_packed = jnp.stack((grad_query, grad_keys, grad_values), axis=2).reshape(
        images, slots, 3 * width
    )
    grad_self_qkv = row_product(normed_first, grad_packed)
    grad_first_norm, gain_first, shift_first = norm_backward(
        transposed_product(grad_packed, self_qkv), scaled_first, inverse_first, gains[0]
    )
    radar_grad = (grad_first + grad_first_norm).astype(jnp.bfloat16)
    gain_grads = jnp.stack((gain_first, gain_second, gain_third))
    shift_grads = jnp.stack((shift_first, shift_second, shift_third))
    totals = lax.psum(
        (
            gain_grads,
            shift_grads,
            grad_self_qkv,
            grad_self_out,
            grad_cross_q,
            grad_cross_kv,
            grad_cross_out,
            grad_mlp_in,
            grad_mlp_in_bias,
            grad_mlp_out,
            grad_mlp_out_bias,
        ),
        ("dp", "head"),
    )
    finished = [total.astype(jnp.bfloat16) for total in totals]
    return (
        mixed,
        radar_grad,
        optical_grad,
        finished[0],
        finished[1],
        finished[2],
        finished[3],
        finished[4],
        finished[5],
        finished[6],
        finished[7],
        finished[8],
        finished[9],
        finished[10],
    )


def solution(mesh):
    placed = (
        P(("dp", "head"), None, None),
        P(("dp", "head"), None, None),
        P(("dp", "head"), None, None),
        P("dp"),
        P("dp"),
        P("dp", None),
        P("dp", None),
        P("dp"),
        P(),
        P(),
        P(),
        P(),
        P(),
        P(),
        P(),
        P(),
        P(),
        P(),
        P(),
    )
    return jax.shard_map(
        body,
        mesh=mesh,
        in_specs=placed,
        out_specs=(
            P(("dp", "head"), None, None),
            P(("dp", "head"), None, None),
            P(("dp", "head"), None, None),
            P(),
            P(),
            P(),
            P(),
            P(),
            P(),
            P(),
            P(),
            P(),
            P(),
            P(),
        ),
        check_vma=False,
    )
```

profile of v0, /device:TPU:0, one launch (start us, length us, event | category | flops | bytes accessed | tf_op | source)
XLA Modules:
  0.0 1294.0 jit_solution(2530825244425150493)
XLA Ops:
  9.9 5.7 convolution_convert_fusion
  15.6 10.9 copy.81
  28.0 12.1 fusion.90
  40.1 8.3 exponential_reduce_fusion.1
  48.6 8.5 fusion.50
  65.0 5.5 reshape.333
  82.8 5.5 reshape.335
  94.3 11.8 all-to-all-done.1
  115.0 5.5 reshape.331
  129.0 4.6 copy.90
  137.7 4.9 all-to-all-start
  142.6 4.6 copy.92
  151.6 9.9 fusion.92
  161.5 8.2 exponential_reduce_fusion
  170.5 4.6 copy.88
  179.4 9.9 convolution_convert_fusion.1
  189.3 4.6 copy.94
  193.9 4.8 all-to-all-start.3
  200.9 5.6 copy.114
  206.5 5.9 reshape_reshape.19
  213.7 12.2 all-to-all-done.3
  225.9 4.7 copy.136
  230.6 5.1 reshape.338
  240.9 11.5 fusion.42
  252.4 32.2 %multiply_convert_fusion.2 = (bf16[8,136,3072]{2,1,0:T(8,128)(2,1)}, f32[8,136,3072]{2,1,0:T(8,128)}) fusion(f32[8,136,3072]{2,1,0:T(8,128)S(1)} %get-tuple-element.108, f32[3072]{0:T(1024)S(1)} %copy-done.50, u8[136,3072]{1,0:T(8,128)(4,1)S(1)} %get-tuple-element.59, u8[136,3072]{1,0:T(8,128)(4,1)S(1)} %get-tuple-element.58), kind=kLoop, calls=%fused_computation.27 | loop fusion | flops 237305856 | bytes 34271232 | tf_op jit(solution)/shard_map/convert_element_type | solution.py:201
  284.6 18.2 %convert_reduce_fusion = (f32[3072]{0:T(1024)}, bf16[8,136,3072]{2,1,0:T(8,128)(2,1)}) fusion(f32[8,136,3072]{2,1,0:T(8,128)} %get-tuple-element.92, bf16[3072,768]{1,0:T(8,128)(2,1)} %param.36, bf16[8,136,768]{2,1,0:T(8,128)(2,1)} %param.21, pred[8,136]{1,0:T(8,128)(4,1)} %copy-done.59, f32[8,136,3072]{2,1,0:T(8,128)} %copy-done.17, ...), kind=kOutput, calls=%fused_computation.22 | convolution fusion | flops 5199836160 | bytes 39838784 | tf_op jit(solution)/shard_map/dot_general | solution.py:36
  302.8 12.7 convolution_bitcast_fusion.1
  315.6 10.9 multiply_reduce_fusion.2
  326.5 4.9 reshape_reshape.23
  340.9 5.5 reshape.339
  349.7 5.0 all-to-all-start.4
  355.9 5.3 fusion.97
  361.2 11.1 convolution_bitcast_fusion
  372.4 6.7 select_convert_fusion
  381.8 4.6 copy.97
  386.5 14.6 %multiply_reduce_fusion.1 = (f32[32,3,136]{2,1,0:T(4,128)S(1)}, f32[32,3,136,136]{2,3,1,0:T(8,128)}) fusion(f32[32,3,136,136]{2,3,1,0:T(8,128)} %get-tuple-element.105, f32[32,3,136]{2,1,0:T(4,128)} %log_add_fusion, bf16[32,136,3,64]{1,3,2,0:T(8,128)(2,1)} %bitcast.236, bf16[32,136,3,64]{1,3,2,0:T(8,128)(2,1)} %gather_fusion), kind=kOutput, calls=%fused_computation.26 | convolution fusion | flops 232592640 | bytes 17651712 | tf_op jit(solution)/shard_map/bqhd,bkhd->bhqk/dot_general | solution.py:95
  401.1 10.4 multiply_convert_fusion.1
  415.2 4.6 copy.99
  424.2 9.6 convert_bitcast_fusion
  438.2 4.6 copy.111
  442.9 7.9 fusion.45
  455.1 4.6 copy.108
  464.3 4.7 copy.135
  469.0 4.9 reshape.342
  473.9 5.9 multiply_reduce_fusion.3
  492.8 14.7 %multiply_reduce_fusion = (f32[8,12,136]{2,1,0:T(8,128)S(1)}, f32[8,12,136,136]{2,3,1,0:T(8,128)}) fusion(f32[8,12,136,136]{2,3,1,0:T(8,128)} %get-tuple-element.101, f32[8,12,136]{2,1,0:T(8,128)} %copy-done.22, bf16[8,136,12,64]{1,3,2,0:T(8,128)(2,1)} %bitcast.238, bf16[8,136,3,12,64]{1,4,3,2,0:T(8,128)(2,1)} %bitcast.231), kind=kOutput, calls=%fused_computation.24 | convolution fusion | flops 232592640 | bytes 26946560 | tf_op jit(solution)/shard_map/bqhd,bkhd->bhqk/dot_general | solution.py:95
  507.5 10.6 multiply_convert_fusion
  520.8 4.9 fusion.43
  525.7 8.7 convert_bitcast_fusion.1
  538.9 7.9 fusion.44
  546.9 9.5 pad_maximum_fusion
  556.4 9.3 copy.105
  565.7 18.5 %copy.113 = bf16[8,136,3,12,64]{1,0,4,3,2:T(8,128)(2,1)} copy(bf16[8,136,3,12,64]{1,4,3,0,2:T(8,128)(2,1)} %pad_maximum_fusion) | data formatting | bytes 10027008 | tf_op jit(solution)/shard_map/stack | solution.py:282
  584.2 4.9 reshape_reshape.20
  589.1 4.7 copy.133
  593.8 4.9 reshape_reshape.22
  598.7 4.9 reshape.348
  603.5 4.7 copy.134
  608.3 4.9 reshape_reshape.21
  613.1 5.1 reshape.346
  626.8 10.6 fusion.38
  638.7 15.1 %reshape_reshape.18 = bf16[1088,2304]{0,1:T(8,128)(2,1)} reshape(bf16[8,136,3,12,64]{1,0,4,3,2:T(8,128)(2,1)} %copy.113) | data formatting | bytes 10027008 | tf_op jit(solution)/shard_map/reshape;reshape | solution.py:43
  653.7 10.8 fusion.94
  670.9 608.8 %all-reduce.2 = (bf16[3,768]{1,0:T(4,128)(2,1)}, bf16[3,768]{1,0:T(4,128)(2,1)}, bf16[768,2304]{1,0:T(8,128)(2,1)}, bf16[768,768]{1,0:T(8,128)(2,1)}, bf16[768,7...) all-reduce(f32[3,768]{1,0:T(4,128)} %pad_maximum_fusion.2, ...), channel_id=1, replica_groups=mesh['dp'=8,'head'=4] {'dp','head'}, use_global_device_ids=true, to_apply=%region_22.23 | all-reduce | flops 9445632 | bytes 56673792 | tf_op jit(solution)/shard_map/psum | solution.py:292
  (281 shorter events, 164.5 us)
Async XLA Ops:
  0.6 9.3 copy-start
  0.7 7.4 copy-start.11
  7.5 52.5 %copy-start.57 = (f32[768]{0:T(1024)}, f32[768]{0:T(1024)S(1)}, u32[]{:S(2)}) copy-start(f32[768]{0:T(1024)S(1)} %get-tuple-element.119) | copy-start | bytes 9220
  15.6 10.9 copy-start.80
  27.5 12.7 copy-start.59
  48.5 8.5 copy-start.22
  48.5 8.5 copy-start.12
  48.6 8.5 copy-start.78
  73.8 32.3 %all-to-all-start.1 = ((bf16[8,136,4,192]{3,1,0,2:T(8,128)(2,1)}), bf16[8,136,4,192]{3,1,0,2:T(8,128)(2,1)}, u32[]{:S(2)}, u32[]{:S(2)}) async-start(bf16[8,136,4,192]{3,1,0,2:T(8,128)(2,1)} %copy.89), calls=%async_computation.1 | async-start | bytes 4456448 | tf_op jit(solution)/shard_map/all_to_all | solution.py:176
  82.7 8.8 copy-start.82
  88.3 5.3 copy-start.81
  106.1 31.6 %all-to-all-start.2 = ((bf16[8,136,4,192]{3,1,0,2:T(8,128)(2,1)}), bf16[8,136,4,192]{3,1,0,2:T(8,128)(2,1)}, u32[]{:S(2)}, u32[]{:S(2)}) async-start(bf16[8,136,4,192]{3,1,0,2:T(8,128)(2,1)} %copy.91), calls=%async_computation.2 | async-start | bytes 4456448 | tf_op jit(solution)/shard_map/all_to_all | solution.py:177
  137.7 32.7 %all-to-all-start = ((bf16[8,136,4,192]{3,1,0,2:T(8,128)(2,1)}), bf16[8,136,4,192]{3,1,0,2:T(8,128)(2,1)}, u32[]{:S(2)}, u32[]{:S(2)}) async-start(bf16[8,136,4,192]{3,1,0,2:T(8,128)(2,1)} %copy.87), calls=%async_computation | async-start | bytes 4456448 | tf_op jit(solution)/shard_map/all_to_all | solution.py:178
  193.9 4.8 copy-start.66
  193.9 5.5 copy-start.83
  193.9 32.0 %all-to-all-start.3 = ((bf16[32,136,1,192]{3,1,2,0:T(8,128)(2,1)}), bf16[32,136,1,192]{3,1,2,0:T(8,128)(2,1)}, u32[]{:S(2)}, u32[]{:S(2)}) async-start(bf16[32,136,1,192]{3,1,2,0:T(8,128)(2,1)} %copy.94), calls=%async_computation.3 | async-start | bytes 4456448 | tf_op jit(solution)/shard_map/all_to_all | solution.py:194
  206.5 5.9 copy-start.73
  240.0 12.3 copy-start.4
  240.7 92.1 %copy-start.44 = (f32[8,136]{1,0:T(8,128)}, f32[8,136]{1,0:T(8,128)S(1)}, u32[]{:S(2)}) copy-start(f32[8,136]{1,0:T(8,128)S(1)} %add_rsqrt_fusion) | copy-start | bytes 13060
  252.4 32.2 %copy-start.17 = (f32[8,136,3072]{2,1,0:T(8,128)}, f32[8,136,3072]{2,1,0:T(8,128)S(1)}, u32[]{:S(2)}) copy-start(f32[8,136,3072]{2,1,0:T(8,128)S(1)} %get-tuple-element.108) | copy-start | bytes 40108036
  302.8 12.7 copy-start.5
  302.8 12.7 copy-start.55
  302.8 12.8 copy-start.84
  332.0 4.9 copy-start.46
  332.7 5.4 copy-start.35
  349.7 5.0 copy-start.70
  349.7 5.6 copy-start.69
  349.7 32.2 %all-to-all-start.4 = ((bf16[8,136,4,192]{3,1,0,2:T(8,128)(2,1)}), bf16[8,136,4,192]{3,1,0,2:T(8,128)(2,1)}, u32[]{:S(2)}, u32[]{:S(2)}) async-start(bf16[8,136,4,192]{3,1,0,2:T(8,128)(2,1)} %copy.96), calls=%async_computation.4 | async-start | bytes 4456448 | tf_op jit(solution)/shard_map/all_to_all | solution.py:222
  355.9 5.3 copy-start.19
  355.9 5.3 copy-start.60
  355.9 16.4 %slice-start.3 = ((s8[6684672]{0:T(1024)(128)(4,1)}), s8[4194304]{0:T(1024)(128)(4,1)S(1)}, s32[]{:S(2)}) async-start(s8[6684672]{0:T(1024)(128)(4,1)} %bitcast.259), calls=%async_computation.11 | async-start | bytes 8388608
  355.9 16.4 %slice-start.5 = ((s8[4718592]{0:T(1024)(128)(4,1)}), s8[4194304]{0:T(1024)(128)(4,1)S(1)}, s32[]{:S(2)}) async-start(s8[4718592]{0:T(1024)(128)(4,1)} %bitcast.265), calls=%async_computation.13 | async-start | bytes 8388608
  361.2 11.1 copy-start.6
  361.2 11.1 slice-start.4
  361.2 11.1 copy-start.71
  361.2 11.1 slice-start.6
  386.5 14.6 %copy-start.24 = (f32[32,3,136]{2,1,0:T(4,128)S(1)}, f32[32,3,136]{2,1,0:T(4,128)}, u32[]{:S(2)}) copy-start(f32[32,3,136]{2,1,0:T(4,128)} %log_add_fusion) | copy-start | bytes 156676
  401.1 10.4 copy-start.3
  419.8 40.0 %all-to-all-start.5 = ((bf16[32,136,1,192]{3,1,2,0:T(8,128)(2,1)}), bf16[32,136,1,192]{3,1,2,0:T(8,128)(2,1)}, u32[]{:S(2)}, u32[]{:S(2)}) async-start(bf16[32,136,1,192]{3,1,2,0:T(8,128)(2,1)} %copy.99), calls=%async_computation.5 | async-start | bytes 4456448 | tf_op jit(solution)/shard_map/all_to_all | solution.py:236
  459.8 74.7 %all-to-all-start.7 = ((bf16[32,136,1,192]{3,1,2,0:T(8,128)(2,1)}), bf16[32,136,1,192]{3,1,2,0:T(8,128)(2,1)}, u32[]{:S(2)}, u32[]{:S(2)}) async-start(bf16[32,136,1,192]{3,1,2,0:T(8,128)(2,1)} %copy.111), calls=%async_computation.7 | async-start | bytes 4456448 | tf_op jit(solution)/shard_map/all_to_all | solution.py:246
  464.2 9.6 copy-start.39
  473.8 6.0 copy-start.7
  473.8 6.0 copy-start.9
  473.8 6.0 copy-start.16
  473.9 6.2 copy-start.20
  473.9 6.2 copy-start.43
  473.9 6.2 copy-start.45
  473.9 6.1 copy-start.47
  473.9 6.1 copy-start.49
  473.9 6.1 copy-start.56
  473.9 6.1 copy-start.58
  473.9 6.1 copy-start.61
  480.1 5.7 copy-start.79
  492.8 14.7 %copy-start.23 = (f32[8,12,136]{2,1,0:T(8,128)S(1)}, f32[8,12,136]{2,1,0:T(8,128)}, u32[]{:S(2)}) copy-start(f32[8,12,136]{2,1,0:T(8,128)} %copy-done.22) | copy-start | bytes 156676
  520.8 4.9 copy-start.10
  534.5 69.1 %all-to-all-start.6 = ((bf16[32,136,1,192]{3,1,2,0:T(8,128)(2,1)}), bf16[32,136,1,192]{3,1,2,0:T(8,128)(2,1)}, u32[]{:S(2)}, u32[]{:S(2)}) async-start(bf16[32,136,1,192]{3,1,2,0:T(8,128)(2,1)} %copy.108), calls=%async_computation.6 | async-start | bytes 4456448 | tf_op jit(solution)/shard_map/all_to_all | solution.py:239
  618.2 8.3 slice-start
  622.1 4.4 slice-start.1
  626.8 10.6 copy-start.68
  626.8 10.6 copy-start.63
  626.8 11.2 copy-start.67
  626.8 11.2 copy-start.62
  653.7 10.8 copy-start.28
  653.7 10.8 copy-start.31
  (36 other events, 91.0 us)
where the time goes:
time: 1300 us; the launch traced here: 1290 us
  blocking collectives  609 us (47%)
  matrix products  263 us (20%)
  local copies, waits for them, and re-layouts  237 us (18%)
  other arithmetic  115 us (9%)
  starting transfers between devices  37.1 us (3%)
  waiting for transfers between devices  30.9 us (2%)
    psum x1, blocking collectives, body(): lax.psum((gain_grads, shift_grads, grad_self_qkv, grad_self_out, grad_cro...  609 us
    dot_general x8, matrix products, transposed_product(): lax.dot_general(left, right, (((left.ndim - 1,), (1,)), ((), ())), prefer...  57.2 us
    dot_general x8, matrix products, row_product(): lax.dot_general(left_rows, right_rows, (((0,), (0,)), ((), ())), preferre...  51.9 us
    dot_general x8, matrix products, matmul(): return jnp.dot(left, right, preferred_element_type=jnp.float32)  42.1 us
    reshape x8, local copies, waits for them, and re-layouts, to_heads(): return values.reshape(images, slots, head_groups, local_width)  35.2 us
    convert_element_type x1, other arithmetic, body(): activated = jax.nn.gelu(inner, approximate=False).astype(jnp.bfloat16)  32.2 us
    another operation x4, local copies, waits for them, and re-layouts, row_product(): right_rows = right.reshape(-1, right.shape[-1])  29.7 us
    dot_general x2, matrix products, attention_backward(): jnp.einsum('bqhd,bkhd->bhqk', grad_mixed, values, preferred_element_type=...  29.2 us
  transfers between devices with their start and end apart: 8, of which 4 were waited for; matrix products, arithmetic and copies ran while one was open for 21% of the time, Pallas kernels for 0%

commit v1 on v0

v1 whole, which is shorter than its diff:
```python
from functools import partial
import math

import jax
import jax.numpy as jnp
from jax import lax
from jax.experimental import pallas as pl
from jax.experimental.pallas import tpu as pltpu
from jax.sharding import PartitionSpec as P

HEADS = 12
HEAD_DIM = 64
GRID = 15
PAIR = 2
QUAD = 4
WIDE = QUAD * HEAD_DIM
FAR = 1e15
VMEM_BYTES = 61 * 1024 * 1024
SLOPES = [2.0 ** (-8.0 * (h + 1.0) / HEADS) for h in range(HEADS)]
SCALE = 1.0 / math.sqrt(HEAD_DIM)
F32 = jnp.float32
BF16 = jnp.bfloat16
SMALL_COST = pl.CostEstimate(flops=1, bytes_accessed=1, transcendentals=0)


def mm(left, right):
    return jnp.dot(left, right, preferred_element_type=F32)


def mm_t(left, right):
    return lax.dot_general(left, right, (((1,), (1,)), ((), ())), preferred_element_type=F32)


def t_mm(left, right):
    return lax.dot_general(left, right, (((0,), (0,)), ((), ())), preferred_element_type=F32)


def rows_of(ref):
    value = ref[...].astype(F32)
    return value.reshape(value.shape[0] * value.shape[1], value.shape[2])


def put_rows(ref, value):
    slots = ref.shape[1]
    for i in range(ref.shape[0]):
        ref[i] = value[i * slots : (i + 1) * slots].astype(ref.dtype)


def norm(values):
    centre = values - jnp.mean(values, axis=-1, keepdims=True)
    inverse = lax.rsqrt(jnp.mean(centre * centre, axis=-1, keepdims=True) + 1e-6)
    return centre * inverse, inverse


def norm_back(grad, scaled, inverse, gain):
    weighted = grad * gain
    return inverse * (
        weighted
        - jnp.mean(weighted, axis=-1, keepdims=True)
        - scaled * jnp.mean(weighted * scaled, axis=-1, keepdims=True)
    )


def column_sum(values):
    return jnp.sum(values, axis=0, keepdims=True)


def head_masks(dtype):
    lane = lax.broadcasted_iota(jnp.int32, (1, WIDE), 1) // HEAD_DIM
    return [(lane == h).astype(F32).astype(dtype) for h in range(QUAD)]


def as_column(row, slots):
    n = row.shape[1]
    same = lax.broadcasted_iota(jnp.int32, (slots, n), 0) == lax.broadcasted_iota(
        jnp.int32, (slots, n), 1
    )
    return jnp.sum(jnp.where(same, jnp.broadcast_to(row, (slots, n)), 0.0), axis=1, keepdims=True)


def distances(query_pos, key_pos, slots, keys):
    delta_row = as_column(query_pos[0:1], slots) - key_pos[0:1, :keys]
    delta_column = as_column(query_pos[1:2], slots) - key_pos[1:2, :keys]
    return jnp.sqrt(delta_row * delta_row + delta_column * delta_column)


def stacked(block, keys, masks):
    slots = block.shape[0]
    if keys <= slots:
        part = block[:keys]
    else:
        part = jnp.concatenate(
            (block.astype(F32), jnp.zeros((keys - slots, block.shape[1]), F32)), axis=0
        ).astype(BF16)
    return jnp.concatenate([part * m for m in masks], axis=0)


def attend(i, keys, q_of, k_of, v_of, query_pos, key_pos, p_ref, o_ref):
    slots = o_ref.shape[1]
    dist = distances(query_pos, key_pos, slots, keys)
    masks = head_masks(BF16)
    for g in range(HEADS // QUAD):
        q = q_of(g) * jnp.asarray(SCALE, BF16)
        scores = mm_t(q, stacked(k_of(g), keys, masks))
        parts = []
        for h in range(QUAD):
            s = scores[:, h * keys : (h + 1) * keys] - SLOPES[g * QUAD + h] * dist
            e = jnp.exp(s - jnp.max(s, axis=1, keepdims=True))
            parts.append((e * (1.0 / jnp.sum(e, axis=1, keepdims=True))).astype(BF16))
        p = jnp.concatenate(parts, axis=1)
        p_ref[i, :, g * QUAD * keys : (g + 1) * QUAD * keys] = p
        o_ref[i, :, g * WIDE : (g + 1) * WIDE] = mm(p, stacked(v_of(g), keys, masks)).astype(BF16)


def attend_back(i, keys, q_of, k_of, v_of, do_of, p_ref, put_dq, put_dk, put_dv, slots):
    masks = head_masks(BF16)
    wide_masks = head_masks(F32)

    def gathered(product):
        total = sum(product[h * keys : (h + 1) * keys] * wide_masks[h] for h in range(QUAD))
        if keys >= slots:
            return total[:slots]
        return jnp.concatenate((total, jnp.zeros((slots - keys, WIDE), F32)), axis=0)

    for g in range(HEADS // QUAD):
        q, do = q_of(g), do_of(g)
        keys_stack = stacked(k_of(g), keys, masks)
        dp = mm_t(do, stacked(v_of(g), keys, masks))
        p = p_ref[i, :, g * QUAD * keys : (g + 1) * QUAD * keys]
        parts = []
        for h in range(QUAD):
            ph = p[:, h * keys : (h + 1) * keys].astype(F32)
            t = ph * dp[:, h * keys : (h + 1) * keys]
            parts.append((t - ph * jnp.sum(t, axis=1, keepdims=True)).astype(BF16))
        ds = jnp.concatenate(parts, axis=1)
        put_dv(g, gathered(t_mm(p, do)).astype(BF16))
        put_dq(g, (mm(ds, keys_stack) * SCALE).astype(BF16))
        put_dk(g, (gathered(t_mm(ds, q)) * SCALE).astype(BF16))


def by_count(count, slots, work):
    small = min(slots, 128)
    pl.when(count <= small)(lambda: work(small))
    if slots > small:
        pl.when(count > small)(lambda: work(256))


def gelu_parts(u):
    size = jnp.abs(u)
    t = 1.0 / (1.0 + (0.3275911 / math.sqrt(2.0)) * size)
    poly = 0.5 * 1.061405429
    for c in (-1.453152027, 1.421413741, -0.284496736, 0.254829592):
        poly = poly * t + 0.5 * c
    bell = jnp.exp(-0.5 * (u * u))
    tail = poly * t * bell
    phi_cap = jnp.where(u >= 0.0, 1.0 - tail, tail)
    return u * phi_cap, phi_cap + u * (bell * (1.0 / math.sqrt(2.0 * math.pi)))


def live_rows(counts, slots):
    slot = lax.broadcasted_iota(jnp.int32, (slots, 1), 0)
    return jnp.concatenate([(slot < c).astype(F32) for c in counts], axis=0)


def self_forward(
    count, x_ref, pos_ref, gain_ref, shift_ref, qkv_w, out_w, q_w,
    h1_ref, qkv_ref, p_ref, o_ref, x1_ref, h2_ref, q2_ref,
):
    step = pl.program_id(0)
    pair, slots, width = x_ref.shape
    x = rows_of(x_ref)
    scaled, _ = norm(x)
    h1 = (scaled * gain_ref[0:1] + shift_ref[0:1]).astype(BF16)
    put_rows(h1_ref, h1.astype(F32))
    put_rows(qkv_ref, mm(h1, qkv_w[...]))
    for i in range(pair):

        def block(kind, i=i):
            return lambda g: qkv_ref[i, :, kind * width + g * WIDE : kind * width + (g + 1) * WIDE]

        by_count(
            count[step * pair + i],
            slots,
            lambda keys, i=i, block=block: attend(
                i, keys, block(0), block(1), block(2), pos_ref[i], pos_ref[i], p_ref, o_ref
            ),
        )
    x1 = x + mm(rows_of(o_ref).astype(BF16), out_w[...])
    put_rows(x1_ref, x1)
    scaled, _ = norm(x1)
    h2 = (scaled * gain_ref[1:2] + shift_ref[1:2]).astype(BF16)
    put_rows(h2_ref, h2.astype(F32))
    put_rows(q2_ref, mm(h2, q_w[...]))


def cross_and_mlp(
    count, other_count, x1_ref, q2_ref, opt_ref, dy_ref, pos_ref, other_pos_ref, gain_ref, shift_ref,
    kv_w, out_w, in_w, in_b, mo_w, mo_b,
    mixed_ref, kv_ref, p_ref, o_ref, h3_ref, g_ref, du_ref, dm_ref, dx2_ref, sums_ref, in_sums_ref,
):
    step = pl.program_id(0)
    pair, slots, width = x1_ref.shape
    hidden = in_w.shape[1]
    put_rows(kv_ref, mm(rows_of(opt_ref).astype(BF16), kv_w[...]))
    for i in range(pair):

        def block(ref, kind, i=i):
            return lambda g: ref[i, :, kind * width + g * WIDE : kind * width + (g + 1) * WIDE]

        by_count(
            other_count[step * pair + i],
            slots,
            lambda keys, i=i, block=block: attend(
                i, keys, block(q2_ref, 0), block(kv_ref, 0), block(kv_ref, 1),
                pos_ref[i], other_pos_ref[i], p_ref, o_ref,
            ),
        )
    x2 = rows_of(x1_ref) + mm(rows_of(o_ref).astype(BF16), out_w[...])
    scaled, inverse = norm(x2)
    gain = gain_ref[2:3]
    h3 = (scaled * gain + shift_ref[2:3]).astype(BF16)
    put_rows(h3_ref, h3.astype(F32))
    live = live_rows([count[step * pair + i] for i in range(pair)], slots)
    dy = rows_of(dy_ref) * live
    dm = dy.astype(BF16)
    put_rows(dm_ref, dy)
    chunk = 768
    g_parts, du_parts, in_sums = [], [], []
    for j in range(hidden // chunk):
        cols = slice(j * chunk, (j + 1) * chunk)
        u = mm(h3, in_w[:, cols]) + in_b[0:1, cols]
        dg = mm_t(dm, mo_w[cols, :]).astype(BF16).astype(F32)
        g, slope = gelu_parts(u)
        du = dg * slope
        for i in range(pair):
            rows = slice(i * slots, (i + 1) * slots)
            g_ref[i, :, cols] = g[rows].astype(BF16)
            du_ref[i, :, cols] = du[rows].astype(BF16)
        g_parts.append(g.astype(BF16))
        du_parts.append(du.astype(BF16))
        in_sums.append(column_sum(du.astype(BF16).astype(F32)))
    y = x2 + (mm(jnp.concatenate(g_parts, axis=1), mo_w[...]) + mo_b[0:1])
    put_rows(mixed_ref, y * live)
    dh3 = mm_t(jnp.concatenate(du_parts, axis=1), in_w[...])
    put_rows(dx2_ref, dy + norm_back(dh3, scaled, inverse, gain))
    sums = jnp.concatenate((column_sum(dh3 * scaled), column_sum(dh3), column_sum(dy)), axis=0)
    in_sums = jnp.concatenate(in_sums, axis=1)

    @pl.when(step == 0)
    def _():
        sums_ref[...] = sums
        in_sums_ref[...] = in_sums

    @pl.when(step > 0)
    def _():
        sums_ref[...] += sums
        in_sums_ref[...] += in_sums


def cross_back(
    other_count, dx2_ref, x1_ref, q2_ref, kv_ref, p_ref, gain_ref, out_w, q_w, kv_w,
    da2_ref, dq2_ref, dkv_ref, og_ref, dx1_ref, sums_ref, do_ref,
):
    step = pl.program_id(0)
    pair, slots, width = x1_ref.shape
    dx2 = rows_of(dx2_ref)
    da2 = dx2.astype(BF16)
    put_rows(da2_ref, dx2)
    put_rows(do_ref, mm_t(da2, out_w[...]))
    for i in range(pair):

        def block(ref, kind, i=i):
            return lambda g: ref[i, :, kind * width + g * WIDE : kind * width + (g + 1) * WIDE]

        def put(ref, kind, i=i):
            def store(g, value):
                ref[i, :, kind * width + g * WIDE : kind * width + (g + 1) * WIDE] = value

            return store

        by_count(
            other_count[step * pair + i],
            slots,
            lambda keys, i=i, block=block, put=put: attend_back(
                i, keys, block(q2_ref, 0), block(kv_ref, 0), block(kv_ref, 1), block(do_ref, 0),
                p_ref, put(dq2_ref, 0), put(dkv_ref, 0), put(dkv_ref, 1), slots,
            ),
        )
    put_rows(og_ref, mm_t(rows_of(dkv_ref).astype(BF16), kv_w[...]))
    dh2 = mm_t(rows_of(dq2_ref).astype(BF16), q_w[...])
    scaled, inverse = norm(rows_of(x1_ref))
    put_rows(dx1_ref, dx2 + norm_back(dh2, scaled, inverse, gain_ref[1:2]))
    sums = jnp.concatenate((column_sum(dh2 * scaled), column_sum(dh2)), axis=0)

    @pl.when(step == 0)
    def _():
        sums_ref[...] = sums

    @pl.when(step > 0)
    def _():
        sums_ref[...] += sums


def self_back(
    count, dx1_ref, x_ref, qkv_ref, p_ref, gain_ref, out_w, qkv_w,
    dqkv_ref, dx_ref, sums_ref, do_ref,
):
    step = pl.program_id(0)
    pair, slots, width = x_ref.shape
    dx1 = rows_of(dx1_ref)
    da1 = dx1.astype(BF16)
    put_rows(do_ref, mm_t(da1, out_w[...]))
    for i in range(pair):

        def block(ref, kind, i=i):
            return lambda g: ref[i, :, kind * width + g * WIDE : kind * width + (g + 1) * WIDE]

        def put(ref, kind, i=i):
            def store(g, value):
                ref[i, :, kind * width + g * WIDE : kind * width + (g + 1) * WIDE] = value

            return store

        by_count(
            count[step * pair + i],
            slots,
            lambda keys, i=i, block=block, put=put: attend_back(
                i, keys, block(qkv_ref, 0), block(qkv_ref, 1), block(qkv_ref, 2), block(do_ref, 0),
                p_ref, put(dqkv_ref, 0), put(dqkv_ref, 1), put(dqkv_ref, 2), slots,
            ),
        )
    dh1 = mm_t(rows_of(dqkv_ref).astype(BF16), qkv_w[...])
    scaled, inverse = norm(rows_of(x_ref))
    put_rows(dx_ref, dx1 + norm_back(dh1, scaled, inverse, gain_ref[0:1]))
    sums = jnp.concatenate((column_sum(dh1 * scaled), column_sum(dh1)), axis=0)

    @pl.when(step == 0)
    def _():
        sums_ref[...] = sums

    @pl.when(step > 0)
    def _():
        sums_ref[...] += sums


def take_images(source, place, *refs):
    j = pl.program_id(0)
    for r, ref in enumerate(refs[:-1]):

        @pl.when(source[j] == r)
        def _(ref=ref):
            refs[-1][...] = ref[...]


def pack_blocks(core, *refs):
    count = (len(refs) - 2) // 2
    for first, out in ((0, refs[-2]), (count, refs[-1])):
        column = 0
        for ref in refs[first : first + count]:
            out[:, column : column + ref.shape[1]] = ref[...]
            column += ref.shape[1]


def unpack_blocks(core, own, other, *outs):
    def copy(source):
        column = 0
        for out in outs:
            out[...] = source[:, column : column + out.shape[1]]
            column += out.shape[1]

    pl.when(pl.program_id(0) == core[0])(lambda: copy(own))
    pl.when(pl.program_id(0) != core[0])(lambda: copy(other))


def add_blocks(bits, *refs):
    third = len(refs) // 3
    for one, other, out in zip(refs[:third], refs[third : 2 * third], refs[2 * third :]):
        value = (one[...].astype(F32) + other[...].astype(F32)).astype(out.dtype)
        out[...] = value.reshape(out.shape)


def merge_blocks(bits, *refs):
    third = len(refs) // 3
    half = pl.program_id(0)
    for p, (one, other, out) in enumerate(zip(refs[:third], refs[third : 2 * third], refs[2 * third :])):

        @pl.when(half == bits[p])
        def _(one=one, out=out):
            out[...] = one[...].reshape(out.shape)

        @pl.when(half != bits[p])
        def _(other=other, out=out):
            out[...] = other[...].reshape(out.shape)


def images_call(kernel, scalars, arrays, whole, outs, sums, scratch, flops, name):
    images = arrays[0].shape[0]
    pair = PAIR if images % PAIR == 0 else 1

    def split_spec(shape):
        rank = len(shape)
        return pl.BlockSpec((pair,) + tuple(shape[1:]), lambda i, *s: (i,) + (0,) * (rank - 1))

    def whole_spec(shape):
        rank = len(shape)
        return pl.BlockSpec(tuple(shape), lambda i, *s: (0,) * rank, pipeline_mode=pl.Buffered(1))

    out_shapes = [jax.ShapeDtypeStruct((images,) + tail, dtype) for tail, dtype in outs]
    sum_shapes = [jax.ShapeDtypeStruct(shape, F32) for shape in sums]
    moved = sum(x.size * x.dtype.itemsize for x in (*arrays, *whole, *out_shapes))
    return pl.pallas_call(
        kernel,
        grid_spec=pltpu.PrefetchScalarGridSpec(
            num_scalar_prefetch=len(scalars),
            grid=(images // pair,),
            in_specs=[split_spec(a.shape) for a in arrays] + [whole_spec(a.shape) for a in whole],
            out_specs=[split_spec(o.shape) for o in out_shapes]
            + [pl.BlockSpec(s.shape, lambda i, *_: (0, 0)) for s in sum_shapes],
            scratch_shapes=[pltpu.VMEM((pair,) + tail, dtype) for tail, dtype in scratch],
        ),
        out_shape=out_shapes + sum_shapes,
        compiler_params=pltpu.CompilerParams(vmem_limit_bytes=VMEM_BYTES),
        cost_estimate=SMALL_COST,
        name=name,
    )(*scalars, *arrays, *whole)


def take_call(source, place, sources):
    shape = sources[0].shape
    block = (1,) + shape[1:]

    def spec(r):
        return pl.BlockSpec(block, lambda j, source, place: (jnp.where(source[j] == r, place[j], 0), 0, 0))

    return pl.pallas_call(
        take_images,
        grid_spec=pltpu.PrefetchScalarGridSpec(
            num_scalar_prefetch=2,
            grid=(shape[0],),
            in_specs=[spec(r) for r in range(len(sources))],
            out_specs=pl.BlockSpec(block, lambda j, source, place: (j, 0, 0)),
        ),
        out_shape=jax.ShapeDtypeStruct(shape, sources[0].dtype),
        cost_estimate=SMALL_COST,
        name="take_images",
    )(source, place, *sources)


def plain_call(kernel, scalars, grid, ins, outs, name):
    shapes = [jax.ShapeDtypeStruct(shape, BF16) for shape, _, _ in outs]
    moved = 2 * (sum(math.prod(s.shape) for s in shapes) * 3)
    return pl.pallas_call(
        kernel,
        grid_spec=pltpu.PrefetchScalarGridSpec(
            num_scalar_prefetch=1,
            grid=(grid,),
            in_specs=[pl.BlockSpec(block, index) for _, block, index in ins],
            out_specs=[pl.BlockSpec(block, index) for _, block, index in outs],
        ),
        out_shape=shapes,
        compiler_params=pltpu.CompilerParams(vmem_limit_bytes=VMEM_BYTES),
        cost_estimate=SMALL_COST,
        name=name,
    )(scalars, *[a for a, _, _ in ins])


def bit_of(axis_name, bit):
    return (lax.axis_index(axis_name) // bit) % 2


PARTS = 3


def sum_levels():
    head, dp = lax.axis_size("head"), lax.axis_size("dp")
    links = [("head", 2**i) for i in reversed(range(1, head.bit_length() - 1))]
    links += [("dp", 2**i) for i in range(dp.bit_length() - 1)]
    turn = links[:PARTS] if len(links) >= PARTS else []
    levels = [[turn[(p + k) % PARTS] for p in range(PARTS)] for k in range(len(turn))]
    return levels + [[link] * PARTS for link in links[len(turn) :]]


def total_by_halves(mats):
    rows = mats[0].shape[0]
    widths = [m.shape[1] for m in mats]
    wide = sum(widths)
    levels = sum_levels()
    n = 2 ** len(levels)
    part_rows = rows // (2 * PARTS)
    r = part_rows // n
    core = bit_of("head", 1)[None].astype(jnp.int32)

    def mine(p, core):
        return (core[0] * PARTS + p, 0)

    def theirs(p, core):
        return ((1 - core[0]) * PARTS + p, 0)

    send, keep = plain_call(
        pack_blocks,
        core,
        PARTS,
        [(m, (part_rows, m.shape[1]), theirs) for m in mats] + [(m, (part_rows, m.shape[1]), mine) for m in mats],
        [((PARTS * part_rows, wide), (part_rows, wide), lambda p, core: (p, 0))] * 2,
        "pack_blocks",
    )
    got = [flip(send.reshape(PARTS, n, r, wide), "head", 1)]
    keep = [keep.reshape(PARTS, n, r, wide)]

    def is_stacked(arrays):
        return len(arrays) == 1

    def split_step(keep, got, bits, same, n):
        half = n // 2
        chunk = min(half, 2)

        def reader(arrays, p, other):
            def index(i, bits):
                b = 1 - bits[p] if other else bits[p]
                return b * (half // chunk) + i

            if is_stacked(arrays):
                return (arrays[0], (1, chunk, r, wide), lambda i, bits: (p, index(i, bits), 0, 0))
            return (arrays[p], (chunk, r, wide), lambda i, bits: (index(i, bits), 0, 0))

        order = [(p, other) for other in (True, False) for p in range(PARTS)]
        ones = [reader(keep, p, other) for p, other in order]
        others = [reader(got, p, other) for p, other in order]
        outs = [((half, r, wide), (chunk, r, wide), lambda i, bits: (i, 0, 0))] * (2 * PARTS)
        done = plain_call(add_blocks, bits, half // chunk, ones + others, outs, "add_blocks")
        return list(done[:PARTS]), list(done[PARTS:])

    def level_bits(level):
        return jnp.stack([bit_of(*link) for link in level]).astype(jnp.int32)

    for level in levels:
        send, keep = split_step(keep, got, level_bits(level), False, n)
        n //= 2
        got = [flip(x, *link) for x, link in zip(send, level)]
    ones = [(x, (1, r, wide), lambda i, bits: (0, 0, 0)) for x in keep]
    others = [(x, (1, r, wide), lambda i, bits: (0, 0, 0)) for x in got]
    have = plain_call(
        add_blocks, core, 1, ones + others, [((1, r, wide), (1, r, wide), lambda i, bits: (0, 0, 0))] * PARTS, "add_blocks"
    )
    for k, level in enumerate(reversed(levels)):
        got = [flip(x, *link) for x, link in zip(have, level)]
        ins = [(x, (n, r, wide), lambda i, bits: (0, 0, 0)) for x in (*have, *got)]
        outs = [((2 * n, r, wide), (n, r, wide), lambda i, bits: (i, 0, 0))] * PARTS
        have = plain_call(merge_blocks, level_bits(level), 2, ins, outs, "merge_blocks")
        n *= 2
    whole = jnp.stack(have)
    other = flip(whole, "head", 1)
    whole, other = (x.reshape(PARTS * part_rows, wide) for x in (whole, other))
    return plain_call(
        unpack_blocks,
        core,
        2,
        [(x, (PARTS * part_rows, wide), lambda i, core: (0, 0)) for x in (whole, other)],
        [((rows, w), (rows // 2, w), lambda i, core: (i, 0)) for w in widths],
        "unpack_blocks",
    )


def positions(patches, count):
    slots = patches.shape[1]
    live = jnp.arange(slots, dtype=jnp.int32)[None, :] < count[:, None]
    row = jnp.where(live, (patches // GRID).astype(F32), FAR)
    column = (patches % GRID).astype(F32)
    pos = jnp.stack((row, column), axis=1)
    return jnp.pad(pos, ((0, 0), (0, 0), (0, 256 - slots)), constant_values=FAR)


def flip(values, axis_name, bit):
    size = lax.axis_size(axis_name)
    return lax.ppermute(values, axis_name, [(i, i ^ bit) for i in range(size)])


def gather_group(values, after):
    size = lax.axis_size("head")
    reach = {0: values}
    bit = size // 2
    while bit:
        sent = dict(reach)
        for r in sent:
            if r:
                sent[r], after = lax.optimization_barrier((sent[r], after))
            reach[r ^ bit] = flip(sent[r], "head", bit)
        bit //= 2
    return [reach[r] for r in range(size)], after


def row_product(left, right):
    return lax.dot_general(
        left.reshape(-1, left.shape[-1]),
        right.reshape(-1, right.shape[-1]),
        (((0,), (0,)), ((), ())),
        preferred_element_type=F32,
    )


def total(values):
    return lax.psum(values, ("dp", "head"))


def body(
    radar, optical, cotangent, radar_ratio, optical_ratio, radar_patches, optical_patches, pairing,
    norm_gain, norm_bias, self_qkv, self_out, cross_q, cross_kv, cross_out,
    mlp_in, mlp_in_bias, mlp_out, mlp_out_bias,
):
    images, slots, width = radar.shape
    hidden = mlp_in.shape[1]
    me = lax.axis_index("head")
    start = me * images
    gains, shifts = norm_gain.astype(F32), norm_bias.astype(F32)

    def own(values):
        return lax.dynamic_slice_in_dim(values, start, images, 0)


    radar_count = GRID * GRID * (100 - own(radar_ratio)) // 100
    partner = own(pairing)
    other_count = (GRID * GRID * (100 - optical_ratio) // 100)[partner]
    pos = positions(own(radar_patches), radar_count)
    other_pos = positions(optical_patches[partner], other_count)

    rows = images * slots
    wide_p = HEADS * 256 if slots > 128 else HEADS * slots
    attention = 2 * images * HEADS * slots * 256 * HEAD_DIM
    h1, qkv, p1, o1, x1, h2, q2 = images_call(
        self_forward,
        (radar_count,),
        (radar, pos),
        (gains, shifts, self_qkv, self_out, cross_q),
        [
            ((slots, width), BF16),
            ((slots, 3 * width), BF16),
            ((slots, wide_p), BF16),
            ((slots, width), BF16),
            ((slots, width), F32),
            ((slots, width), BF16),
            ((slots, width), BF16),
        ],
        [],
        [],
        2 * rows * width * width * 5 + 2 * attention,
        "self_forward",
    )
    optical_blocks, x1 = gather_group(optical, x1)
    paired = take_call(partner // images ^ me, partner % images, optical_blocks)
    mixed, kv, p2, o2, h3, g, du, dm, dx2, sums3, in_sums = images_call(
        cross_and_mlp,
        (radar_count, other_count),
        (x1, q2, paired, cotangent, pos, other_pos),
        (
            gains, shifts, cross_kv, cross_out, mlp_in, mlp_in_bias.astype(F32)[None],
            mlp_out, mlp_out_bias.astype(F32)[None],
        ),
        [
            ((slots, width), BF16),
            ((slots, 2 * width), BF16),
            ((slots, wide_p), BF16),
            ((slots, width), BF16),
            ((slots, width), BF16),
            ((slots, hidden), BF16),
            ((slots, hidden), BF16),
            ((slots, width), BF16),
            ((slots, width), F32),
        ],
        [(3, width), (1, hidden)],
        [],
        2 * rows * width * (3 * width + 4 * hidden) + 2 * attention,
        "cross_and_mlp",
    )
    grad_mlp_out, grad_mlp_in = row_product(g, dm).astype(BF16), row_product(h3, du).astype(BF16)
    grad_mlp_out, grad_mlp_in, dx2 = lax.optimization_barrier((grad_mlp_out, grad_mlp_in, dx2))
    grad_mlp_out, grad_mlp_in = total((grad_mlp_out, grad_mlp_in))
    da2, dq2, dkv, og, dx1, sums2 = images_call(
        cross_back,
        (other_count,),
        (dx2, x1, q2, kv, p2),
        (gains, cross_out, cross_q, cross_kv),
        [
            ((slots, width), BF16),
            ((slots, width), BF16),
            ((slots, 2 * width), BF16),
            ((slots, width), BF16),
            ((slots, width), F32),
        ],
        [(2, width)],
        [((slots, width), BF16)],
        2 * rows * width * width * 4 + 4 * attention,
        "cross_back",
    )
    first_group = (
        row_product(o2, da2).astype(BF16),
        row_product(h2, dq2).astype(BF16),
        row_product(paired, dkv).astype(BF16),
        row_product(o1, dx1.astype(BF16)).astype(BF16),
    )
    first_group, dx1 = lax.optimization_barrier((first_group, dx1))
    grad_cross_out, grad_cross_q, grad_cross_kv, grad_self_out = total_by_halves(first_group)
    dqkv, radar_grad, sums1 = images_call(
        self_back,
        (radar_count,),
        (dx1, radar, qkv, p1),
        (gains, self_out, self_qkv),
        [((slots, 3 * width), BF16), ((slots, width), BF16)],
        [(2, width)],
        [((slots, width), BF16)],
        2 * rows * width * width * 4 + 4 * attention,
        "self_back",
    )
    og_blocks, dqkv = gather_group(og, dqkv)
    inverse_pairing = own(jnp.argsort(pairing))
    optical_grad = take_call(inverse_pairing // images ^ me, inverse_pairing % images, og_blocks)
    grad_self_qkv = row_product(h1, dqkv).astype(BF16)
    small = jnp.concatenate((sums1, sums2, sums3, in_sums.reshape(-1, width)), axis=0)
    count = small.shape[0]
    small = jnp.pad(small.astype(BF16).T, ((0, 0), (0, 128 - count)))
    grad_self_qkv, small = total_by_halves((grad_self_qkv, small))
    small = small[:, :count].T
    gain_grads = jnp.stack((small[0], small[2], small[4]))
    shift_grads = jnp.stack((small[1], small[3], small[5]))
    grad_mlp_in_bias, grad_mlp_out_bias = small[7:].reshape(hidden), small[6]
    return (
        mixed, radar_grad, optical_grad, gain_grads.astype(BF16), shift_grads.astype(BF16),
        grad_self_qkv, grad_self_out, grad_cross_q, grad_cross_kv, grad_cross_out,
        grad_mlp_in, grad_mlp_in_bias.astype(BF16), grad_mlp_out, grad_mlp_out_bias.astype(BF16),
    )


def solution(mesh):
    split, group, copied = P(("dp", "head"), None, None), P("dp"), P()
    return jax.shard_map(
        body,
        mesh=mesh,
        in_specs=(split,) * 3 + (group,) * 5 + (copied,) * 11,
        out_specs=(split,) * 3 + (copied,) * 11,
        check_vma=False,
    )
```

time: 1300 us -> 506 us (0.39)
  blocking collectives: 609 us -> 0 us
  Pallas kernels: 0 us -> 220 us
  matrix products: 263 us -> 43.5 us
  local copies, waits for them, and re-layouts: 237 us -> 34.4 us
  other arithmetic: 115 us -> 18.7 us
  waiting for transfers between devices: 30.9 us -> 107 us
  starting transfers between devices: 37.1 us -> 60.1 us
  between operations: 1.98 us -> 15 us
    psum x1 -> x0, blocking collectives: 609 us -> none  [body(): lax.psum((gain_grads, shift_grads, grad_self_qkv, grad_self_out, grad_cro...]
    pallas_call x0 -> x28, Pallas kernels: none -> 220 us  [the longest x4 129 us: images_call(): pl.pallas_call(kernel, grid_spec=pltpu.PrefetchScalarGridSpec(num_scalar_...]
    dot_general x36 -> x7, matrix products: 263 us -> 43.5 us  [row_product(): lax.dot_general(left.reshape(-1, left.shape[-1]), right.reshape(-1, right...]
    ppermute x0 -> x58, waiting for transfers between devices: none -> 79.7 us  [flip(): return lax.ppermute(values, axis_name, [(i, i ^ bit) for i in range(size)])]
    reshape x16 -> x2, local copies, waits for them, and re-layouts: 73.5 us -> 0.65 us  [the longest x1 0.63 us: body(): grad_mlp_in_bias, grad_mlp_out_bias = (small[7:].reshape(hidden), small[6])]
    another operation x14 -> x1, local copies, waits for them, and re-layouts: 69.5 us -> 0.54 us  [level_bits(): return jnp.stack([bit_of(*link) for link in level]).astype(jnp.int32)]
    convert_element_type x14 -> x3, other arithmetic: 69.8 us -> 2.62 us  [the longest x2 2.6 us: body(): gains, shifts = (norm_gain.astype(F32), norm_bias.astype(F32))]
    ppermute x0 -> x58, starting transfers between devices: none -> 60 us  [flip(): return lax.ppermute(values, axis_name, [(i, i ^ bit) for i in range(size)])]
  transfers between devices with their start and end apart: 8 -> 59, of which waited for: 4 -> 25; matrix products, arithmetic and copies ran while one was open for 21% -> 11% of each run, Pallas kernels for 0% -> 27%
where the time goes in v1:
time: 506 us; the launch traced here: 498 us
  Pallas kernels  220 us (43%)
  waiting for transfers between devices  107 us (21%)
  starting transfers between devices  60.1 us (12%)
  matrix products  43.5 us (9%)
  local copies, waits for them, and re-layouts  34.4 us (7%)
  other arithmetic  18.7 us (4%)
  between operations  15 us (3%)
    pallas_call x4, Pallas kernels, images_call(): pl.pallas_call(kernel, grid_spec=pltpu.PrefetchScalarGridSpec(num_scalar_...  129 us
    ppermute x58, waiting for transfers between devices, flip(): return lax.ppermute(values, axis_name, [(i, i ^ bit) for i in range(size)])  79.7 us
    pallas_call x22, Pallas kernels, plain_call(): pl.pallas_call(kernel, grid_spec=pltpu.PrefetchScalarGridSpec(num_scalar_...  77.2 us
    ppermute x58, starting transfers between devices, flip(): return lax.ppermute(values, axis_name, [(i, i ^ bit) for i in range(size)])  60 us
    dot_general x7, matrix products, row_product(): lax.dot_general(left.reshape(-1, left.shape[-1]), right.reshape(-1, right...  43.5 us
    psum x1, waiting for transfers between devices, total(): return lax.psum(values, ('dp', 'head'))  27.2 us
    unnamed x145, local copies, waits for them, and re-layouts  21.4 us
    pallas_call x2, Pallas kernels, take_call(): pl.pallas_call(take_images, grid_spec=pltpu.PrefetchScalarGridSpec(num_sc...  13.3 us
  transfers between devices with their start and end apart: 59, of which 25 were waited for; matrix products, arithmetic and copies ran while one was open for 11% of the time, Pallas kernels for 27%

profile of v1, /device:TPU:0, one launch (start us, length us, event | category | flops | bytes accessed | tf_op | source)
XLA Modules:
  0.0 498.4 jit_solution(7525978581634422119)
XLA Ops:
  7.2 3.0 collective-permute-start
  15.8 25.5 %self_forward.1 = (bf16[8,136,768]{2,1,0:T(8,128)(2,1)}, bf16[8,136,2304]{2,1,0:T(8,128)(2,1)}, bf16[8,136,3072]{2,1,0:T(8,128)(2,1)}, bf16[8,136,768]{2,1,0:T(8...) custom-call(s32[8]{0:T(128)} %copy-done.54, ...), custom_call_target="tpu_custom_call" | custom-call | flops 1 | bytes 1 | tf_op jit(solution)/shard_map/self_forward/pallas_call | solution.py:411
  41.3 5.7 %collective-permute-done.refs_2_ = bf16[8,136,768]{2,1,0:T(8,128)(2,1)S(1)} collective-permute-done((bf16[8,136,768]{2,1,0:T(8,128)(2,1)}, bf16[8,136,768]{2,1,0:T(8,128)(2,1)S(1)}, u32[]{:S(2)}, u32[]{:S(2)}) %collective-permute-start) | collective-permute-done | bytes 1671200 | tf_op jit(solution)/shard_map/ppermute | solution.py:575
  51.4 6.3 %take_images.2.opt_ref = bf16[8,136,768]{2,1,0:T(8,128)(2,1)} custom-call(s32[8]{0:T(128)} %get-tuple-element.313.source, s32[8]{0:T(128)} %get-tuple-element.302.place, bf16[8,136,768]{2,1,0:T(8,128)(2,1)} %refs_0_.1, bf16[8,136,768]{2,1,0:T(8,128)(2,1)} %collective-permute-done.1.refs_1_, bf16[8,136,768]{2,1,0:T(8,128)(2,1)} %copy-done.9, ...), custom_call_target="tpu_custom_call" | custom-call | flops 1 | bytes 1 | tf_op jit(solution)/shard_map/take_images/pallas_call | solution.py:435
  57.8 53.0 %cross_and_mlp.1 = (bf16[8,136,768]{2,1,0:T(8,128)(2,1)}, bf16[8,136,1536]{2,1,0:T(8,128)(2,1)}, bf16[8,136,3072]{2,1,0:T(8,128)(2,1)}, bf16[8,136,768]{2,1,0:T(...) custom-call(s32[8]{0:T(128)} %copy-done.54, ...), custom_call_target="tpu_custom_call" | custom-call | flops 1 | bytes 1 | tf_op jit(solution)/shard_map/cross_and_mlp/pallas_call | solution.py:411
  110.7 11.0 %bitcast_convert_fusion.1 = bf16[3072,768]{1,0:T(8,128)(2,1)} fusion(bf16[8,136,3072]{2,1,0:T(8,128)(2,1)} %get-tuple-element.148, bf16[8,136,768]{2,1,0:T(8,128)(2,1)} %get-tuple-element.149), kind=kOutput, calls=%fused_computation.3 | convolution fusion | flops 5136187392 | bytes 13074432 | tf_op jit(solution)/shard_map/dot_general | solution.py:593
  121.8 7.9 %bitcast_convert_fusion = bf16[768,3072]{1,0:T(8,128)(2,1)} fusion(bf16[8,136,768]{2,1,0:T(8,128)(2,1)S(1)} %copy-done.67, bf16[8,136,3072]{2,1,0:T(8,128)(2,1)S(1)} %copy-done.60), kind=kOutput, calls=%fused_computation.2 | convolution fusion | flops 5136187392 | bytes 13074432 | tf_op jit(solution)/shard_map/dot_general | solution.py:593
  129.7 25.4 %cross_back.1 = (bf16[8,136,768]{2,1,0:T(8,128)(2,1)}, bf16[8,136,768]{2,1,0:T(8,128)(2,1)}, bf16[8,136,1536]{2,1,0:T(8,128)(2,1)}, bf16[8,136,768]{2,1,0:T(8,12...) custom-call(s32[8]{0:T(128)} %copy-done.55, f32[8,136,768]{2,1,0:T(8,128)} %get-tuple-element.153.dx2_ref, ...), custom_call_target="tpu_custom_call" | custom-call | flops 1 | bytes 1 | tf_op jit(solution)/shard_map/cross_back/pallas_call | solution.py:411
  155.1 2.2 collective-permute-start.4
  157.4 4.9 bitcast_convert_fusion.4.refs_3_.refs_7_
  162.2 2.8 bitcast_convert_fusion.5.refs_1_.refs_5_
  165.1 2.8 bitcast_convert_fusion.6.refs_0_.refs_4_
  167.8 4.5 bitcast_convert_fusion.3.refs_2_.refs_6_
  172.4 6.2 %pack_blocks.3 = (bf16[384,3840]{1,0:T(8,128)(2,1)}, bf16[384,3840]{1,0:T(8,128)(2,1)}) custom-call(s32[1]{0:T(128)} %bitcast.10.core.bits, bf16[768,768]{1,0:T(8,128)(2,1)} %bitcast_convert_fusion.6.refs_0_.refs_4_, bf16[768,768]{1,0:T(8,128)(2,1)} %bitcast_convert_fusion.5.refs_1_.refs_5_, bf16[768,1536]{1,0:T(8,128)(2,1)} %bitcast_convert_fusion.3.refs_2_.refs_6_, ...), custom_call_target="tpu_custom_call" | custom-call | flops 1 | bytes 1 | tf_op jit(solution)/shard_map/pack_blocks/pallas_call | solution.py:452
  180.0 25.5 %self_back.1 = (bf16[8,136,2304]{2,1,0:T(8,128)(2,1)}, bf16[8,136,768]{2,1,0:T(8,128)(2,1)}, f32[2,768]{1,0:T(2,128)}) custom-call(s32[8]{0:T(128)} %copy-done.54, f32[8,136,768]{2,1,0:T(8,128)} %get-tuple-element.162.dx1_ref, bf16[8,136,768]{2,1,0:T(8,128)(2,1)} %x_ref.3, bf16[8,136,2304]{2,1,0:T(8,128)(2,1)} %get-tuple-element.163.qkv_ref, ...), custom_call_target="tpu_custom_call" | custom-call | flops 1 | bytes 1 | tf_op jit(solution)/shard_map/self_back/pallas_call | solution.py:411
  207.2 9.5 %bitcast_convert_fusion.2.refs_0_.refs_2_ = bf16[768,2304]{1,0:T(8,128)(2,1)} fusion(bf16[8,136,768]{2,1,0:T(8,128)(2,1)} %get-tuple-element.170, bf16[8,136,2304]{2,1,0:T(8,128)(2,1)} %get-tuple-element.171), kind=kOutput, calls=%fused_computation.4 | convolution fusion | flops 3852140544 | bytes 10223616 | tf_op jit(solution)/shard_map/dot_general | solution.py:593
  216.8 4.7 pack_blocks.2
  223.7 5.6 %add_blocks.15 = (bf16[8,8,3840]{2,1,0:T(8,128)(2,1)}, bf16[8,8,3840]{2,1,0:T(8,128)(2,1)}, bf16[8,8,3840]{2,1,0:T(8,128)(2,1)}, bf16[8,8,3840]{2,1,0:T(8,128)(2...) custom-call(s32[3]{0:T(128)} %pad_add_fusion.bits, bf16[3,16,8,3840]{3,2,1,0:T(8,128)(2,1)} %bitcast.55, ...), custom_call_target="tpu_custom_call" | custom-call | flops 1 | bytes 1 | tf_op jit(solution)/shard_map/add_blocks/pallas_call | solution.py:452
  230.6 3.9 collective-permute-start.35
  235.1 8.1 %collective-permute-done.33.refs_6_.refs_9_ = bf16[8,8,3840]{2,1,0:T(8,128)(2,1)S(1)} collective-permute-done((bf16[8,8,3840]{2,1,0:T(8,128)(2,1)}, bf16[8,8,3840]{2,1,0:T(8,128)(2,1)S(1)}, u32[]{:S(2)}, u32[]{:S(2)}) %collective-permute-start.33) | collective-permute-done | bytes 491552 | tf_op jit(solution)/shard_map/ppermute | solution.py:575
  244.0 2.3 collective-permute-done.35.refs_8_.refs_11_
  247.0 3.7 add_blocks.16
  251.1 1.9 collective-permute-start.37
  254.6 4.8 add_blocks.10
  263.1 3.1 add_blocks.17
  272.4 2.1 collective-permute-done.40.refs_7_.refs_10_
  274.5 4.6 collective-permute-done.41.refs_8_.refs_11_
  279.8 2.6 add_blocks.18
  282.8 2.5 collective-permute-start.43
  286.6 3.2 add_blocks.11
  290.7 3.4 collective-permute-done.43.refs_4_
  294.2 2.6 collective-permute-done.44.refs_5_
  299.1 2.9 collective-permute-start.46
  303.1 4.2 collective-permute-done.45.refs_3_
  310.0 2.0 collective-permute-done.47.refs_5_
  312.6 2.5 merge_blocks.12
  317.8 2.7 add_blocks.12
  320.5 2.0 collective-permute-start.13
  324.8 2.8 merge_blocks.13
  331.7 4.4 collective-permute-done.14.refs_7_.refs_10_
  336.7 2.4 add_blocks.13
  342.1 2.2 collective-permute-done.16.refs_3_
  346.5 3.4 collective-permute-done.18.refs_5_
  352.9 2.1 collective-permute-start.20
  357.2 3.4 merge_blocks.14
  364.9 2.3 merge_blocks.8
  368.7 7.5 %collective-permute-done.22.refs_3_ = bf16[2,8,2432]{2,1,0:T(8,128)(2,1)S(1)} collective-permute-done((bf16[2,8,2432]{2,1,0:T(8,128)(2,1)}, bf16[2,8,2432]{2,1,0:T(8,128)(2,1)S(1)}, u32[]{:S(2)}, u32[]{:S(2)}) %collective-permute-start.22) | collective-permute-done | bytes 77856 | tf_op jit(solution)/shard_map/ppermute | solution.py:575
  377.3 3.6 collective-permute-done.24.refs_5_
  381.5 2.9 merge_blocks.9
  386.3 3.5 collective-permute-done.25.refs_3_
  391.3 8.4 %collective-permute-done.27.refs_5_ = bf16[4,8,2432]{2,1,0:T(8,128)(2,1)S(1)} collective-permute-done((bf16[4,8,2432]{2,1,0:T(8,128)(2,1)}, bf16[4,8,2432]{2,1,0:T(8,128)(2,1)S(1)}, u32[]{:S(2)}, u32[]{:S(2)}) %collective-permute-start.27) | collective-permute-done | bytes 155680 | tf_op jit(solution)/shard_map/ppermute | solution.py:575
  400.3 3.0 merge_blocks.10
  407.4 4.2 merge_blocks.15
  411.5 2.3 pad_maximum_fusion
  414.0 3.7 merge_blocks.11
  417.7 2.9 pad_maximum_fusion.1
  424.2 3.0 collective-permute-done.3.refs_1_
  427.2 2.4 collective-permute-done.5.refs_3_
  429.6 7.0 %take_images.3 = bf16[8,136,768]{2,1,0:T(8,128)(2,1)} custom-call(s32[8]{0:T(128)} %fusion.11.source, s32[8]{0:T(128)} %get-tuple-element.300.place, bf16[8,136,768]{2,1,0:T(8,128)(2,1)} %get-tuple-element.167.refs_0_, bf16[8,136,768]{2,1,0:T(8,128)(2,1)} %collective-permute-done.3.refs_1_, bf16[8,136,768]{2,1,0:T(8,128)(2,1)} %collective-permute-done.4.refs_2_, ...), custom_call_target="tpu_custom_call" | custom-call | flops 1 | bytes 1 | tf_op jit(solution)/shard_map/take_images/pallas_call | solution.py:435
  436.6 4.6 unpack_blocks.2
  451.0 5.7 %unpack_blocks.3 = (bf16[768,768]{1,0:T(8,128)(2,1)}, bf16[768,768]{1,0:T(8,128)(2,1)}, bf16[768,1536]{1,0:T(8,128)(2,1)}, bf16[768,768]{1,0:T(8,128)(2,1)}) custom-call(s32[1]{0:T(128)} %bitcast.10.core.bits, bf16[384,3840]{1,0:T(8,128)(2,1)} %bitcast.67, bf16[384,3840]{1,0:T(8,128)(2,1)} %bitcast.30.other), custom_call_target="tpu_custom_call" | custom-call | flops 1 | bytes 1 | tf_op jit(solution)/shard_map/unpack_blocks/pallas_call | solution.py:452
  456.7 27.2 %all-reduce.6.cloned.1.call-done = (bf16[768,3072]{1,0:T(8,128)(2,1)}, bf16[3072,768]{1,0:T(8,128)(2,1)}) async-done(((bf16[768,3072]{1,0:T(8,128)(2,1)}, bf16[3072,768]{1,0:T(8,128)(2,1)}), (bf16[768,3072]{1,0:T(8,128)(2,1)}, bf16[3072,768]{1,0:T(8,128)(2,1)})) %all-reduce.6.cloned.1.call-update) | async-done | bytes 9437200 | tf_op jit(solution)/shard_map/psum | solution.py:602
  483.9 5.0 %copy.70 = bf16[768,3072]{1,0:T(8,128)(2,1)} copy(bf16[768,3072]{1,0:T(8,128)(2,1)} %get-tuple-element.327) | data formatting | bytes 9437184
  488.9 2.2 copy.71
  (285 shorter events, 89.6 us)
Async XLA Ops:
  7.2 42.3 %copy-start = (s32[32,136]{1,0:T(8,128)S(1)}, s32[32,136]{1,0:T(8,128)}, u32[]{:S(2)}) copy-start(s32[32,136]{1,0:T(8,128)} %param.25) | copy-start | bytes 52228
  7.2 476.7 %all-reduce.6.cloned.1.call-start = ((), (), s32[]{:S(2)}) async-start(), calls=%async_computation | async-start | bytes 18874368 | tf_op jit(solution)/shard_map/psum | solution.py:602
  7.2 39.7 %collective-permute-start = (bf16[8,136,768]{2,1,0:T(8,128)(2,1)}, bf16[8,136,768]{2,1,0:T(8,128)(2,1)S(1)}, u32[]{:S(2)}, u32[]{:S(2)}) collective-permute-start(bf16[8,136,768]{2,1,0:T(8,128)(2,1)} %refs_0_.1), channel_id=1, source_target_pairs={{0,2},{1,3},{2,0},{3,1},{4,6},{5,7},{6,4},{7,5},{8,10},{9,11},{10,... | collective-permute-start | bytes 5013512 | tf_op jit(solution)/shard_map/ppermute | solution.py:575
  10.3 41.2 %collective-permute-start.1 = (bf16[8,136,768]{2,1,0:T(8,128)(2,1)}, bf16[8,136,768]{2,1,0:T(8,128)(2,1)}, u32[]{:S(2)}, u32[]{:S(2)}) collective-permute-start(bf16[8,136,768]{2,1,0:T(8,128)(2,1)} %refs_0_.1), channel_id=1, source_target_pairs={{0,1},{1,0},{2,3},{3,2},{4,5},{5,4},{6,7},{7,6},{8,9},{9,8},{10,11... | collective-permute-start | bytes 5013512 | tf_op jit(solution)/shard_map/ppermute | solution.py:575
  15.8 31.2 %copy-start.58 = (bf16[768]{0:T(1024)(128)(2,1)S(1)}, bf16[768]{0:T(1024)(128)(2,1)}, u32[]{:S(2)}) copy-start(bf16[768]{0:T(1024)(128)(2,1)} %param.37) | copy-start | bytes 4612
  15.8 31.9 %copy-start.59 = (s32[32]{0:T(128)S(1)}, s32[32]{0:T(128)}, u32[]{:S(2)}) copy-start(s32[32]{0:T(128)} %param.26) | copy-start | bytes 388
  15.8 33.1 %copy-start.70 = (s32[32]{0:T(128)S(1)}, s32[32]{0:T(128)}, u32[]{:S(2)}) copy-start(s32[32]{0:T(128)} %param.23) | copy-start | bytes 388
  15.8 34.3 %copy-start.57 = (bf16[3072]{0:T(1024)(128)(2,1)S(1)}, bf16[3072]{0:T(1024)(128)(2,1)}, u32[]{:S(2)}) copy-start(bf16[3072]{0:T(1024)(128)(2,1)} %param.35) | copy-start | bytes 18436
  47.0 4.4 collective-permute-start.2
  155.1 52.1 %collective-permute-start.4 = (bf16[8,136,768]{2,1,0:T(8,128)(2,1)}, bf16[8,136,768]{2,1,0:T(8,128)(2,1)}, u32[]{:S(2)}, u32[]{:S(2)}) collective-permute-start(bf16[8,136,768]{2,1,0:T(8,128)(2,1)} %get-tuple-element.167.refs_0_), channel_id=1, source_target_pairs={{0,2},{1,3},{2,0},{3,1},{4,6},{5,7},{6,4},{7,5},{8,10},{9,11},{10,... | collective-permute-start | bytes 5013512 | tf_op jit(solution)/shard_map/ppermute | solution.py:575
  178.6 43.5 %collective-permute-start.32 = (bf16[3,16,8,3840]{3,2,1,0:T(8,128)(2,1)}, bf16[3,16,8,3840]{3,2,1,0:T(8,128)(2,1)S(1)}, u32[]{:S(2)}, u32[]{:S(2)}) collective-permute-start(bf16[3,16,8,3840]{3,2,1,0:T(8,128)(2,1)} %bitcast.76), channel_id=1, source_target_pairs={{0,1},{1,0},{2,3},{3,2},{4,5},{5,4},{6,7},{7,6},{8,9},{9,8},{10,11... | collective-permute-start | bytes 8847368 | tf_op jit(solution)/shard_map/ppermute | solution.py:575
  221.5 33.1 %collective-permute-start.6 = (bf16[3,16,8,2432]{3,2,1,0:T(8,128)(2,1)}, bf16[3,16,8,2432]{3,2,1,0:T(8,128)(2,1)}, u32[]{:S(2)}, u32[]{:S(2)}) collective-permute-start(bf16[3,16,8,2432]{3,2,1,0:T(8,128)(2,1)} %bitcast.77), channel_id=1, source_target_pairs={{0,1},{1,0},{2,3},{3,2},{4,5},{5,4},{6,7},{7,6},{8,9},{9,8},{10,11... | collective-permute-start | bytes 5603336 | tf_op jit(solution)/shard_map/ppermute | solution.py:575
  229.3 13.9 %collective-permute-start.33 = (bf16[8,8,3840]{2,1,0:T(8,128)(2,1)}, bf16[8,8,3840]{2,1,0:T(8,128)(2,1)S(1)}, u32[]{:S(2)}, u32[]{:S(2)}) collective-permute-start(bf16[8,8,3840]{2,1,0:T(8,128)(2,1)} %get-tuple-element.228), channel_id=1, source_target_pairs={{0,2},{1,3},{2,0},{3,1},{4,6},{5,7},{6,4},{7,5},{8,10},{9,11},{10,... | collective-permute-start | bytes 1474568 | tf_op jit(solution)/shard_map/ppermute | solution.py:575
  230.4 13.6 %collective-permute-start.34 = (bf16[8,8,3840]{2,1,0:T(8,128)(2,1)}, bf16[8,8,3840]{2,1,0:T(8,128)(2,1)S(1)}, u32[]{:S(2)}, u32[]{:S(2)}) collective-permute-start(bf16[8,8,3840]{2,1,0:T(8,128)(2,1)} %get-tuple-element.229), channel_id=1, source_target_pairs={{0,4},{4,0},{8,12},{12,8},{16,20},{20,16},{24,28},{28,24},{1,5},{5... | collective-permute-start | bytes 1474568 | tf_op jit(solution)/shard_map/ppermute | solution.py:575
  230.6 15.7 %collective-permute-start.35 = (bf16[8,8,3840]{2,1,0:T(8,128)(2,1)}, bf16[8,8,3840]{2,1,0:T(8,128)(2,1)S(1)}, u32[]{:S(2)}, u32[]{:S(2)}) collective-permute-start(bf16[8,8,3840]{2,1,0:T(8,128)(2,1)} %get-tuple-element.230), channel_id=1, source_target_pairs={{0,8},{4,12},{8,0},{12,4},{16,24},{20,28},{24,16},{28,20},{1,9},{5... | collective-permute-start | bytes 1474568 | tf_op jit(solution)/shard_map/ppermute | solution.py:575
  250.7 10.8 %collective-permute-start.36 = (bf16[4,8,3840]{2,1,0:T(8,128)(2,1)}, bf16[4,8,3840]{2,1,0:T(8,128)(2,1)S(1)}, u32[]{:S(2)}, u32[]{:S(2)}) collective-permute-start(bf16[4,8,3840]{2,1,0:T(8,128)(2,1)} %get-tuple-element.234), channel_id=1, source_target_pairs={{0,4},{4,0},{8,12},{12,8},{16,20},{20,16},{24,28},{28,24},{1,5},{5... | collective-permute-start | bytes 737288 | tf_op jit(solution)/shard_map/ppermute | solution.py:575
  251.1 11.2 %collective-permute-start.37 = (bf16[4,8,3840]{2,1,0:T(8,128)(2,1)}, bf16[4,8,3840]{2,1,0:T(8,128)(2,1)S(1)}, u32[]{:S(2)}, u32[]{:S(2)}) collective-permute-start(bf16[4,8,3840]{2,1,0:T(8,128)(2,1)} %get-tuple-element.235), channel_id=1, source_target_pairs={{0,8},{4,12},{8,0},{12,4},{16,24},{20,28},{24,16},{28,20},{1,9},{5... | collective-permute-start | bytes 737288 | tf_op jit(solution)/shard_map/ppermute | solution.py:575
  253.0 9.3 %collective-permute-start.38 = (bf16[4,8,3840]{2,1,0:T(8,128)(2,1)}, bf16[4,8,3840]{2,1,0:T(8,128)(2,1)S(1)}, u32[]{:S(2)}, u32[]{:S(2)}) collective-permute-start(bf16[4,8,3840]{2,1,0:T(8,128)(2,1)} %get-tuple-element.236), channel_id=1, source_target_pairs={{0,2},{1,3},{2,0},{3,1},{4,6},{5,7},{6,4},{7,5},{8,10},{9,11},{10,... | collective-permute-start | bytes 737288 | tf_op jit(solution)/shard_map/ppermute | solution.py:575
  259.4 25.8 %collective-permute-start.7 = (bf16[8,8,2432]{2,1,0:T(8,128)(2,1)}, bf16[8,8,2432]{2,1,0:T(8,128)(2,1)S(1)}, u32[]{:S(2)}, u32[]{:S(2)}) collective-permute-start(bf16[8,8,2432]{2,1,0:T(8,128)(2,1)} %get-tuple-element.181), channel_id=1, source_target_pairs={{0,2},{1,3},{2,0},{3,1},{4,6},{5,7},{6,4},{7,5},{8,10},{9,11},{10,... | collective-permute-start | bytes 933896 | tf_op jit(solution)/shard_map/ppermute | solution.py:575
  260.0 25.8 %collective-permute-start.8 = (bf16[8,8,2432]{2,1,0:T(8,128)(2,1)}, bf16[8,8,2432]{2,1,0:T(8,128)(2,1)S(1)}, u32[]{:S(2)}, u32[]{:S(2)}) collective-permute-start(bf16[8,8,2432]{2,1,0:T(8,128)(2,1)} %get-tuple-element.182), channel_id=1, source_target_pairs={{0,4},{4,0},{8,12},{12,8},{16,20},{20,16},{24,28},{28,24},{1,5},{5... | collective-permute-start | bytes 933896 | tf_op jit(solution)/shard_map/ppermute | solution.py:575
  261.5 24.3 %collective-permute-start.9 = (bf16[8,8,2432]{2,1,0:T(8,128)(2,1)}, bf16[8,8,2432]{2,1,0:T(8,128)(2,1)S(1)}, u32[]{:S(2)}, u32[]{:S(2)}) collective-permute-start(bf16[8,8,2432]{2,1,0:T(8,128)(2,1)} %get-tuple-element.183), channel_id=1, source_target_pairs={{0,8},{4,12},{8,0},{12,4},{16,24},{20,28},{24,16},{28,20},{1,9},{5... | collective-permute-start | bytes 933896 | tf_op jit(solution)/shard_map/ppermute | solution.py:575
  266.2 5.4 %collective-permute-start.39 = (bf16[2,8,3840]{2,1,0:T(8,128)(2,1)}, bf16[2,8,3840]{2,1,0:T(8,128)(2,1)S(1)}, u32[]{:S(2)}, u32[]{:S(2)}) collective-permute-start(bf16[2,8,3840]{2,1,0:T(8,128)(2,1)} %get-tuple-element.240), channel_id=1, source_target_pairs={{0,8},{4,12},{8,0},{12,4},{16,24},{20,28},{24,16},{28,20},{1,9},{5... | collective-permute-start | bytes 368648 | tf_op jit(solution)/shard_map/ppermute | solution.py:575
  268.0 6.5 %collective-permute-start.40 = (bf16[2,8,3840]{2,1,0:T(8,128)(2,1)S(1)}, bf16[2,8,3840]{2,1,0:T(8,128)(2,1)S(1)}, u32[]{:S(2)}, u32[]{:S(2)}) collective-permute-start(bf16[2,8,3840]{2,1,0:T(8,128)(2,1)S(1)} %copy-done.69), channel_id=1, source_target_pairs={{0,2},{1,3},{2,0},{3,1},{4,6},{5,7},{6,4},{7,5},{8,10},{9,11},{10,... | collective-permute-start | bytes 368648 | tf_op jit(solution)/shard_map/ppermute | solution.py:575
  271.6 7.5 %collective-permute-start.41 = (bf16[2,8,3840]{2,1,0:T(8,128)(2,1)S(1)}, bf16[2,8,3840]{2,1,0:T(8,128)(2,1)S(1)}, u32[]{:S(2)}, u32[]{:S(2)}) collective-permute-start(bf16[2,8,3840]{2,1,0:T(8,128)(2,1)S(1)} %copy-done.68), channel_id=1, source_target_pairs={{0,4},{4,0},{8,12},{12,8},{16,20},{20,16},{24,28},{28,24},{1,5},{5... | collective-permute-start | bytes 368648 | tf_op jit(solution)/shard_map/ppermute | solution.py:575
  282.3 8.4 %collective-permute-start.42 = (bf16[1,8,3840]{2,1,0:T(8,128)(2,1)}, bf16[1,8,3840]{2,1,0:T(8,128)(2,1)S(1)}, u32[]{:S(2)}, u32[]{:S(2)}) collective-permute-start(bf16[1,8,3840]{2,1,0:T(8,128)(2,1)} %get-tuple-element.246), channel_id=1, source_target_pairs={{0,16},{4,20},{8,24},{12,28},{16,0},{20,4},{24,8},{28,12},{1,17},{... | collective-permute-start | bytes 184328 | tf_op jit(solution)/shard_map/ppermute | solution.py:575
  282.8 11.4 %collective-permute-start.43 = (bf16[1,8,3840]{2,1,0:T(8,128)(2,1)}, bf16[1,8,3840]{2,1,0:T(8,128)(2,1)S(1)}, u32[]{:S(2)}, u32[]{:S(2)}) collective-permute-start(bf16[1,8,3840]{2,1,0:T(8,128)(2,1)} %get-tuple-element.247), channel_id=1, source_target_pairs={{0,16},{4,20},{8,24},{12,28},{16,0},{20,4},{24,8},{28,12},{1,17},{... | collective-permute-start | bytes 184328 | tf_op jit(solution)/shard_map/ppermute | solution.py:575
  285.3 11.5 %collective-permute-start.44 = (bf16[1,8,3840]{2,1,0:T(8,128)(2,1)}, bf16[1,8,3840]{2,1,0:T(8,128)(2,1)S(1)}, u32[]{:S(2)}, u32[]{:S(2)}) collective-permute-start(bf16[1,8,3840]{2,1,0:T(8,128)(2,1)} %get-tuple-element.248), channel_id=1, source_target_pairs={{0,16},{4,20},{8,24},{12,28},{16,0},{20,4},{24,8},{28,12},{1,17},{... | collective-permute-start | bytes 184328 | tf_op jit(solution)/shard_map/ppermute | solution.py:575
  289.8 26.6 %collective-permute-start.10 = (bf16[4,8,2432]{2,1,0:T(8,128)(2,1)}, bf16[4,8,2432]{2,1,0:T(8,128)(2,1)S(1)}, u32[]{:S(2)}, u32[]{:S(2)}) collective-permute-start(bf16[4,8,2432]{2,1,0:T(8,128)(2,1)} %get-tuple-element.187), channel_id=1, source_target_pairs={{0,4},{4,0},{8,12},{12,8},{16,20},{20,16},{24,28},{28,24},{1,5},{5... | collective-permute-start | bytes 466952 | tf_op jit(solution)/shard_map/ppermute | solution.py:575
  299.1 8.2 %collective-permute-start.45 = (bf16[1,8,3840]{2,1,0:T(8,128)(2,1)}, bf16[1,8,3840]{2,1,0:T(8,128)(2,1)S(1)}, u32[]{:S(2)}, u32[]{:S(2)}) collective-permute-start(bf16[1,8,3840]{2,1,0:T(8,128)(2,1)} %get-tuple-element.249.refs_0_), channel_id=1, source_target_pairs={{0,16},{4,20},{8,24},{12,28},{16,0},{20,4},{24,8},{28,12},{1,17},{... | collective-permute-start | bytes 184328 | tf_op jit(solution)/shard_map/ppermute | solution.py:575
  299.1 10.9 %collective-permute-start.46 = (bf16[1,8,3840]{2,1,0:T(8,128)(2,1)}, bf16[1,8,3840]{2,1,0:T(8,128)(2,1)S(1)}, u32[]{:S(2)}, u32[]{:S(2)}) collective-permute-start(bf16[1,8,3840]{2,1,0:T(8,128)(2,1)} %get-tuple-element.250.refs_1_), channel_id=1, source_target_pairs={{0,16},{4,20},{8,24},{12,28},{16,0},{20,4},{24,8},{28,12},{1,17},{... | collective-permute-start | bytes 184328 | tf_op jit(solution)/shard_map/ppermute | solution.py:575
  302.0 10.0 %collective-permute-start.47 = (bf16[1,8,3840]{2,1,0:T(8,128)(2,1)}, bf16[1,8,3840]{2,1,0:T(8,128)(2,1)S(1)}, u32[]{:S(2)}, u32[]{:S(2)}) collective-permute-start(bf16[1,8,3840]{2,1,0:T(8,128)(2,1)} %get-tuple-element.251.refs_2_), channel_id=1, source_target_pairs={{0,16},{4,20},{8,24},{12,28},{16,0},{20,4},{24,8},{28,12},{1,17},{... | collective-permute-start | bytes 184328 | tf_op jit(solution)/shard_map/ppermute | solution.py:575
  302.1 15.0 %collective-permute-start.11 = (bf16[4,8,2432]{2,1,0:T(8,128)(2,1)}, bf16[4,8,2432]{2,1,0:T(8,128)(2,1)S(1)}, u32[]{:S(2)}, u32[]{:S(2)}) collective-permute-start(bf16[4,8,2432]{2,1,0:T(8,128)(2,1)} %get-tuple-element.188), channel_id=1, source_target_pairs={{0,8},{4,12},{8,0},{12,4},{16,24},{20,28},{24,16},{28,20},{1,9},{5... | collective-permute-start | bytes 466952 | tf_op jit(solution)/shard_map/ppermute | solution.py:575
  307.3 9.8 %collective-permute-start.12 = (bf16[4,8,2432]{2,1,0:T(8,128)(2,1)}, bf16[4,8,2432]{2,1,0:T(8,128)(2,1)S(1)}, u32[]{:S(2)}, u32[]{:S(2)}) collective-permute-start(bf16[4,8,2432]{2,1,0:T(8,128)(2,1)} %get-tuple-element.189), channel_id=1, source_target_pairs={{0,2},{1,3},{2,0},{3,1},{4,6},{5,7},{6,4},{7,5},{8,10},{9,11},{10,... | collective-permute-start | bytes 466952 | tf_op jit(solution)/shard_map/ppermute | solution.py:575
  315.1 8.4 %collective-permute-start.48 = (bf16[2,8,3840]{2,1,0:T(8,128)(2,1)}, bf16[2,8,3840]{2,1,0:T(8,128)(2,1)S(1)}, u32[]{:S(2)}, u32[]{:S(2)}) collective-permute-start(bf16[2,8,3840]{2,1,0:T(8,128)(2,1)} %get-tuple-element.252.refs_0_), channel_id=1, source_target_pairs={{0,8},{4,12},{8,0},{12,4},{16,24},{20,28},{24,16},{28,20},{1,9},{5... | collective-permute-start | bytes 368648 | tf_op jit(solution)/shard_map/ppermute | solution.py:575
  315.1 8.4 %collective-permute-start.49 = (bf16[2,8,3840]{2,1,0:T(8,128)(2,1)}, bf16[2,8,3840]{2,1,0:T(8,128)(2,1)S(1)}, u32[]{:S(2)}, u32[]{:S(2)}) collective-permute-start(bf16[2,8,3840]{2,1,0:T(8,128)(2,1)} %get-tuple-element.253.refs_1_), channel_id=1, source_target_pairs={{0,2},{1,3},{2,0},{3,1},{4,6},{5,7},{6,4},{7,5},{8,10},{9,11},{10,... | collective-permute-start | bytes 368648 | tf_op jit(solution)/shard_map/ppermute | solution.py:575
  316.4 7.1 %collective-permute-start.50 = (bf16[2,8,3840]{2,1,0:T(8,128)(2,1)}, bf16[2,8,3840]{2,1,0:T(8,128)(2,1)S(1)}, u32[]{:S(2)}, u32[]{:S(2)}) collective-permute-start(bf16[2,8,3840]{2,1,0:T(8,128)(2,1)} %get-tuple-element.254.refs_2_), channel_id=1, source_target_pairs={{0,4},{4,0},{8,12},{12,8},{16,20},{20,16},{24,28},{28,24},{1,5},{5... | collective-permute-start | bytes 368648 | tf_op jit(solution)/shard_map/ppermute | solution.py:575
  320.5 10.3 %collective-permute-start.13 = (bf16[2,8,2432]{2,1,0:T(8,128)(2,1)}, bf16[2,8,2432]{2,1,0:T(8,128)(2,1)S(1)}, u32[]{:S(2)}, u32[]{:S(2)}) collective-permute-start(bf16[2,8,2432]{2,1,0:T(8,128)(2,1)} %get-tuple-element.193), channel_id=1, source_target_pairs={{0,8},{4,12},{8,0},{12,4},{16,24},{20,28},{24,16},{28,20},{1,9},{5... | collective-permute-start | bytes 233480 | tf_op jit(solution)/shard_map/ppermute | solution.py:575
  327.6 27.4 %collective-permute-start.51 = (bf16[4,8,3840]{2,1,0:T(8,128)(2,1)}, bf16[4,8,3840]{2,1,0:T(8,128)(2,1)S(1)}, u32[]{:S(2)}, u32[]{:S(2)}) collective-permute-start(bf16[4,8,3840]{2,1,0:T(8,128)(2,1)} %get-tuple-element.255.refs_0_), channel_id=1, source_target_pairs={{0,4},{4,0},{8,12},{12,8},{16,20},{20,16},{24,28},{28,24},{1,5},{5... | collective-permute-start | bytes 737288 | tf_op jit(solution)/shard_map/ppermute | solution.py:575
  328.8 27.0 %collective-permute-start.52 = (bf16[4,8,3840]{2,1,0:T(8,128)(2,1)}, bf16[4,8,3840]{2,1,0:T(8,128)(2,1)S(1)}, u32[]{:S(2)}, u32[]{:S(2)}) collective-permute-start(bf16[4,8,3840]{2,1,0:T(8,128)(2,1)} %get-tuple-element.256.refs_1_), channel_id=1, source_target_pairs={{0,8},{4,12},{8,0},{12,4},{16,24},{20,28},{24,16},{28,20},{1,9},{5... | collective-permute-start | bytes 737288 | tf_op jit(solution)/shard_map/ppermute | solution.py:575
  328.8 27.0 %collective-permute-start.53 = (bf16[4,8,3840]{2,1,0:T(8,128)(2,1)}, bf16[4,8,3840]{2,1,0:T(8,128)(2,1)S(1)}, u32[]{:S(2)}, u32[]{:S(2)}) collective-permute-start(bf16[4,8,3840]{2,1,0:T(8,128)(2,1)} %get-tuple-element.257.refs_2_), channel_id=1, source_target_pairs={{0,2},{1,3},{2,0},{3,1},{4,6},{5,7},{6,4},{7,5},{8,10},{9,11},{10,... | collective-permute-start | bytes 737288 | tf_op jit(solution)/shard_map/ppermute | solution.py:575
  329.9 6.1 %collective-permute-start.14 = (bf16[2,8,2432]{2,1,0:T(8,128)(2,1)}, bf16[2,8,2432]{2,1,0:T(8,128)(2,1)S(1)}, u32[]{:S(2)}, u32[]{:S(2)}) collective-permute-start(bf16[2,8,2432]{2,1,0:T(8,128)(2,1)} %get-tuple-element.194), channel_id=1, source_target_pairs={{0,2},{1,3},{2,0},{3,1},{4,6},{5,7},{6,4},{7,5},{8,10},{9,11},{10,... | collective-permute-start | bytes 233480 | tf_op jit(solution)/shard_map/ppermute | solution.py:575
  330.9 5.2 %collective-permute-start.15 = (bf16[2,8,2432]{2,1,0:T(8,128)(2,1)}, bf16[2,8,2432]{2,1,0:T(8,128)(2,1)S(1)}, u32[]{:S(2)}, u32[]{:S(2)}) collective-permute-start(bf16[2,8,2432]{2,1,0:T(8,128)(2,1)} %get-tuple-element.195), channel_id=1, source_target_pairs={{0,4},{4,0},{8,12},{12,8},{16,20},{20,16},{24,28},{28,24},{1,5},{5... | collective-permute-start | bytes 233480 | tf_op jit(solution)/shard_map/ppermute | solution.py:575
  339.1 5.1 %collective-permute-start.16 = (bf16[1,8,2432]{2,1,0:T(8,128)(2,1)}, bf16[1,8,2432]{2,1,0:T(8,128)(2,1)S(1)}, u32[]{:S(2)}, u32[]{:S(2)}) collective-permute-start(bf16[1,8,2432]{2,1,0:T(8,128)(2,1)} %get-tuple-element.199), channel_id=1, source_target_pairs={{0,16},{4,20},{8,24},{12,28},{16,0},{20,4},{24,8},{28,12},{1,17},{... | collective-permute-start | bytes 116744 | tf_op jit(solution)/shard_map/ppermute | solution.py:575
  340.4 6.1 %collective-permute-start.17 = (bf16[1,8,2432]{2,1,0:T(8,128)(2,1)}, bf16[1,8,2432]{2,1,0:T(8,128)(2,1)S(1)}, u32[]{:S(2)}, u32[]{:S(2)}) collective-permute-start(bf16[1,8,2432]{2,1,0:T(8,128)(2,1)} %get-tuple-element.200), channel_id=1, source_target_pairs={{0,16},{4,20},{8,24},{12,28},{16,0},{20,4},{24,8},{28,12},{1,17},{... | collective-permute-start | bytes 116744 | tf_op jit(solution)/shard_map/ppermute | solution.py:575
  344.2 5.7 %collective-permute-start.18 = (bf16[1,8,2432]{2,1,0:T(8,128)(2,1)}, bf16[1,8,2432]{2,1,0:T(8,128)(2,1)S(1)}, u32[]{:S(2)}, u32[]{:S(2)}) collective-permute-start(bf16[1,8,2432]{2,1,0:T(8,128)(2,1)} %get-tuple-element.201), channel_id=1, source_target_pairs={{0,16},{4,20},{8,24},{12,28},{16,0},{20,4},{24,8},{28,12},{1,17},{... | collective-permute-start | bytes 116744 | tf_op jit(solution)/shard_map/ppermute | solution.py:575
  352.1 11.0 %collective-permute-start.19 = (bf16[1,8,2432]{2,1,0:T(8,128)(2,1)}, bf16[1,8,2432]{2,1,0:T(8,128)(2,1)S(1)}, u32[]{:S(2)}, u32[]{:S(2)}) collective-permute-start(bf16[1,8,2432]{2,1,0:T(8,128)(2,1)} %get-tuple-element.202.refs_0_), channel_id=1, source_target_pairs={{0,16},{4,20},{8,24},{12,28},{16,0},{20,4},{24,8},{28,12},{1,17},{... | collective-permute-start | bytes 116744 | tf_op jit(solution)/shard_map/ppermute | solution.py:575
  352.9 10.7 %collective-permute-start.20 = (bf16[1,8,2432]{2,1,0:T(8,128)(2,1)}, bf16[1,8,2432]{2,1,0:T(8,128)(2,1)S(1)}, u32[]{:S(2)}, u32[]{:S(2)}) collective-permute-start(bf16[1,8,2432]{2,1,0:T(8,128)(2,1)} %get-tuple-element.203.refs_1_), channel_id=1, source_target_pairs={{0,16},{4,20},{8,24},{12,28},{16,0},{20,4},{24,8},{28,12},{1,17},{... | collective-permute-start | bytes 116744 | tf_op jit(solution)/shard_map/ppermute | solution.py:575
  355.0 8.6 %collective-permute-start.21 = (bf16[1,8,2432]{2,1,0:T(8,128)(2,1)}, bf16[1,8,2432]{2,1,0:T(8,128)(2,1)S(1)}, u32[]{:S(2)}, u32[]{:S(2)}) collective-permute-start(bf16[1,8,2432]{2,1,0:T(8,128)(2,1)} %get-tuple-element.204.refs_2_), channel_id=1, source_target_pairs={{0,16},{4,20},{8,24},{12,28},{16,0},{20,4},{24,8},{28,12},{1,17},{... | collective-permute-start | bytes 116744 | tf_op jit(solution)/shard_map/ppermute | solution.py:575
  360.6 43.3 %collective-permute-start.54 = (bf16[8,8,3840]{2,1,0:T(8,128)(2,1)}, bf16[8,8,3840]{2,1,0:T(8,128)(2,1)S(1)}, u32[]{:S(2)}, u32[]{:S(2)}) collective-permute-start(bf16[8,8,3840]{2,1,0:T(8,128)(2,1)} %get-tuple-element.258.refs_0_), channel_id=1, source_target_pairs={{0,2},{1,3},{2,0},{3,1},{4,6},{5,7},{6,4},{7,5},{8,10},{9,11},{10,... | collective-permute-start | bytes 1474568 | tf_op jit(solution)/shard_map/ppermute | solution.py:575
  361.5 44.2 %collective-permute-start.55 = (bf16[8,8,3840]{2,1,0:T(8,128)(2,1)}, bf16[8,8,3840]{2,1,0:T(8,128)(2,1)S(1)}, u32[]{:S(2)}, u32[]{:S(2)}) collective-permute-start(bf16[8,8,3840]{2,1,0:T(8,128)(2,1)} %get-tuple-element.259.refs_1_), channel_id=1, source_target_pairs={{0,4},{4,0},{8,12},{12,8},{16,20},{20,16},{24,28},{28,24},{1,5},{5... | collective-permute-start | bytes 1474568 | tf_op jit(solution)/shard_map/ppermute | solution.py:575
  363.1 42.7 %collective-permute-start.56 = (bf16[8,8,3840]{2,1,0:T(8,128)(2,1)}, bf16[8,8,3840]{2,1,0:T(8,128)(2,1)S(1)}, u32[]{:S(2)}, u32[]{:S(2)}) collective-permute-start(bf16[8,8,3840]{2,1,0:T(8,128)(2,1)} %get-tuple-element.260.refs_2_), channel_id=1, source_target_pairs={{0,8},{4,12},{8,0},{12,4},{16,24},{20,28},{24,16},{28,20},{1,9},{5... | collective-permute-start | bytes 1474568 | tf_op jit(solution)/shard_map/ppermute | solution.py:575
  367.2 9.1 %collective-permute-start.22 = (bf16[2,8,2432]{2,1,0:T(8,128)(2,1)}, bf16[2,8,2432]{2,1,0:T(8,128)(2,1)S(1)}, u32[]{:S(2)}, u32[]{:S(2)}) collective-permute-start(bf16[2,8,2432]{2,1,0:T(8,128)(2,1)} %get-tuple-element.205.refs_0_), channel_id=1, source_target_pairs={{0,8},{4,12},{8,0},{12,4},{16,24},{20,28},{24,16},{28,20},{1,9},{5... | collective-permute-start | bytes 233480 | tf_op jit(solution)/shard_map/ppermute | solution.py:575
  368.7 8.6 %collective-permute-start.23 = (bf16[2,8,2432]{2,1,0:T(8,128)(2,1)}, bf16[2,8,2432]{2,1,0:T(8,128)(2,1)S(1)}, u32[]{:S(2)}, u32[]{:S(2)}) collective-permute-start(bf16[2,8,2432]{2,1,0:T(8,128)(2,1)} %get-tuple-element.206.refs_1_), channel_id=1, source_target_pairs={{0,2},{1,3},{2,0},{3,1},{4,6},{5,7},{6,4},{7,5},{8,10},{9,11},{10,... | collective-permute-start | bytes 233480 | tf_op jit(solution)/shard_map/ppermute | solution.py:575
  376.3 4.6 collective-permute-start.24
  384.4 5.4 %collective-permute-start.25 = (bf16[4,8,2432]{2,1,0:T(8,128)(2,1)}, bf16[4,8,2432]{2,1,0:T(8,128)(2,1)S(1)}, u32[]{:S(2)}, u32[]{:S(2)}) collective-permute-start(bf16[4,8,2432]{2,1,0:T(8,128)(2,1)} %get-tuple-element.208.refs_0_), channel_id=1, source_target_pairs={{0,4},{4,0},{8,12},{12,8},{16,20},{20,16},{24,28},{28,24},{1,5},{5... | collective-permute-start | bytes 466952 | tf_op jit(solution)/shard_map/ppermute | solution.py:575
  385.4 5.8 %collective-permute-start.26 = (bf16[4,8,2432]{2,1,0:T(8,128)(2,1)}, bf16[4,8,2432]{2,1,0:T(8,128)(2,1)S(1)}, u32[]{:S(2)}, u32[]{:S(2)}) collective-permute-start(bf16[4,8,2432]{2,1,0:T(8,128)(2,1)} %get-tuple-element.209.refs_1_), channel_id=1, source_target_pairs={{0,8},{4,12},{8,0},{12,4},{16,24},{20,28},{24,16},{28,20},{1,9},{5... | collective-permute-start | bytes 466952 | tf_op jit(solution)/shard_map/ppermute | solution.py:575
  389.8 9.8 %collective-permute-start.27 = (bf16[4,8,2432]{2,1,0:T(8,128)(2,1)}, bf16[4,8,2432]{2,1,0:T(8,128)(2,1)S(1)}, u32[]{:S(2)}, u32[]{:S(2)}) collective-permute-start(bf16[4,8,2432]{2,1,0:T(8,128)(2,1)} %get-tuple-element.210.refs_2_), channel_id=1, source_target_pairs={{0,2},{1,3},{2,0},{3,1},{4,6},{5,7},{6,4},{7,5},{8,10},{9,11},{10,... | collective-permute-start | bytes 466952 | tf_op jit(solution)/shard_map/ppermute | solution.py:575
  403.3 10.7 %collective-permute-start.28 = (bf16[8,8,2432]{2,1,0:T(8,128)(2,1)}, bf16[8,8,2432]{2,1,0:T(8,128)(2,1)}, u32[]{:S(2)}, u32[]{:S(2)}) collective-permute-start(bf16[8,8,2432]{2,1,0:T(8,128)(2,1)} %get-tuple-element.211.refs_0_), channel_id=1, source_target_pairs={{0,2},{1,3},{2,0},{3,1},{4,6},{5,7},{6,4},{7,5},{8,10},{9,11},{10,... | collective-permute-start | bytes 933896 | tf_op jit(solution)/shard_map/ppermute | solution.py:575
  403.3 10.6 %collective-permute-start.29 = (bf16[8,8,2432]{2,1,0:T(8,128)(2,1)}, bf16[8,8,2432]{2,1,0:T(8,128)(2,1)}, u32[]{:S(2)}, u32[]{:S(2)}) collective-permute-start(bf16[8,8,2432]{2,1,0:T(8,128)(2,1)} %get-tuple-element.212.refs_1_), channel_id=1, source_target_pairs={{0,4},{4,0},{8,12},{12,8},{16,20},{20,16},{24,28},{28,24},{1,5},{5... | collective-permute-start | bytes 933896 | tf_op jit(solution)/shard_map/ppermute | solution.py:575
  403.9 10.1 %collective-permute-start.30 = (bf16[8,8,2432]{2,1,0:T(8,128)(2,1)}, bf16[8,8,2432]{2,1,0:T(8,128)(2,1)}, u32[]{:S(2)}, u32[]{:S(2)}) collective-permute-start(bf16[8,8,2432]{2,1,0:T(8,128)(2,1)} %get-tuple-element.213.refs_2_), channel_id=1, source_target_pairs={{0,8},{4,12},{8,0},{12,4},{16,24},{20,28},{24,16},{28,20},{1,9},{5... | collective-permute-start | bytes 933896 | tf_op jit(solution)/shard_map/ppermute | solution.py:575
  413.9 37.2 %collective-permute-start.57 = (bf16[3,16,8,3840]{3,2,1,0:T(8,128)(2,1)S(1)}, bf16[3,16,8,3840]{3,2,1,0:T(8,128)(2,1)}, u32[]{:S(2)}, u32[]{:S(2)}) collective-permute-start(bf16[3,16,8,3840]{3,2,1,0:T(8,128)(2,1)S(1)} %pad_maximum_fusion), channel_id=1, source_target_pairs={{0,1},{1,0},{2,3},{3,2},{4,5},{5,4},{6,7},{7,6},{8,9},{9,8},{10,11... | collective-permute-start | bytes 8847368 | tf_op jit(solution)/shard_map/ppermute | solution.py:575
  420.7 16.0 %collective-permute-start.31 = (bf16[3,16,8,2432]{3,2,1,0:T(8,128)(2,1)}, bf16[3,16,8,2432]{3,2,1,0:T(8,128)(2,1)}, u32[]{:S(2)}, u32[]{:S(2)}) collective-permute-start(bf16[3,16,8,2432]{3,2,1,0:T(8,128)(2,1)} %pad_maximum_fusion.1), channel_id=1, source_target_pairs={{0,1},{1,0},{2,3},{3,2},{4,5},{5,4},{6,7},{7,6},{8,9},{9,8},{10,11... | collective-permute-start | bytes 5603336 | tf_op jit(solution)/shard_map/ppermute | solution.py:575
  420.9 6.3 %collective-permute-start.3 = (bf16[8,136,768]{2,1,0:T(8,128)(2,1)}, bf16[8,136,768]{2,1,0:T(8,128)(2,1)}, u32[]{:S(2)}, u32[]{:S(2)}) collective-permute-start(bf16[8,136,768]{2,1,0:T(8,128)(2,1)} %get-tuple-element.167.refs_0_), channel_id=1, source_target_pairs={{0,1},{1,0},{2,3},{3,2},{4,5},{5,4},{6,7},{7,6},{8,9},{9,8},{10,11... | collective-permute-start | bytes 5013512 | tf_op jit(solution)/shard_map/ppermute | solution.py:575
  421.2 8.4 %collective-permute-start.5 = (bf16[8,136,768]{2,1,0:T(8,128)(2,1)}, bf16[8,136,768]{2,1,0:T(8,128)(2,1)}, u32[]{:S(2)}, u32[]{:S(2)}) collective-permute-start(bf16[8,136,768]{2,1,0:T(8,128)(2,1)} %collective-permute-done.4.refs_2_), channel_id=1, source_target_pairs={{0,1},{1,0},{2,3},{3,2},{4,5},{5,4},{6,7},{7,6},{8,9},{9,8},{10,11... | collective-permute-start | bytes 5013512 | tf_op jit(solution)/shard_map/ppermute | solution.py:575
  (66 other events, 284.4 us)
Sparse Core Ops, SparseCore 0:
  268.1 215.7 all-reduce.5

commit v2 on v1

--- a/solution.py
+++ b/solution.py
@@ -163,14 +163,14 @@
 
 
 def self_forward(
-    count, x_ref, pos_ref, gain_ref, shift_ref, qkv_w, out_w, q_w,
+    base, count, x_ref, pos_ref, gain_ref, shift_ref, qkv_w, out_w, q_w,
     h1_ref, qkv_ref, p_ref, o_ref, x1_ref, h2_ref, q2_ref,
 ):
     step = pl.program_id(0)
     pair, slots, width = x_ref.shape
     x = rows_of(x_ref)
     scaled, _ = norm(x)
-    h1 = (scaled * gain_ref[0:1] + shift_ref[0:1]).astype(BF16)
+    h1 = (scaled * gain_ref[...].astype(F32)[0:1] + shift_ref[...].astype(F32)[0:1]).astype(BF16)
     put_rows(h1_ref, h1.astype(F32))
     put_rows(qkv_ref, mm(h1, qkv_w[...]))
     for i in range(pair):
@@ -179,7 +179,7 @@
             return lambda g: qkv_ref[i, :, kind * width + g * WIDE : kind * width + (g + 1) * WIDE]
 
         by_count(
-            count[step * pair + i],
+            count[base + step * pair + i],
             slots,
             lambda keys, i=i, block=block: attend(
                 i, keys, block(0), block(1), block(2), pos_ref[i], pos_ref[i], p_ref, o_ref
@@ -188,13 +188,13 @@
     x1 = x + mm(rows_of(o_ref).astype(BF16), out_w[...])
     put_rows(x1_ref, x1)
     scaled, _ = norm(x1)
-    h2 = (scaled * gain_ref[1:2] + shift_ref[1:2]).astype(BF16)
+    h2 = (scaled * gain_ref[...].astype(F32)[1:2] + shift_ref[...].astype(F32)[1:2]).astype(BF16)
     put_rows(h2_ref, h2.astype(F32))
     put_rows(q2_ref, mm(h2, q_w[...]))
 
 
 def cross_and_mlp(
-    count, other_count, x1_ref, q2_ref, opt_ref, dy_ref, pos_ref, other_pos_ref, gain_ref, shift_ref,
+    base, count, other_count, x1_ref, q2_ref, opt_ref, dy_ref, pos_ref, other_pos_ref, gain_ref, shift_ref,
     kv_w, out_w, in_w, in_b, mo_w, mo_b,
     mixed_ref, kv_ref, p_ref, o_ref, h3_ref, g_ref, du_ref, dm_ref, dx2_ref, sums_ref, in_sums_ref,
 ):
@@ -208,7 +208,7 @@
             return lambda g: ref[i, :, kind * width + g * WIDE : kind * width + (g + 1) * WIDE]
 
         by_count(
-            other_count[step * pair + i],
+            other_count[base + step * pair + i],
             slots,
             lambda keys, i=i, block=block: attend(
                 i, keys, block(q2_ref, 0), block(kv_ref, 0), block(kv_ref, 1),
@@ -217,10 +217,10 @@
         )
     x2 = rows_of(x1_ref) + mm(rows_of(o_ref).astype(BF16), out_w[...])
     scaled, inverse = norm(x2)
-    gain = gain_ref[2:3]
-    h3 = (scaled * gain + shift_ref[2:3]).astype(BF16)
+    gain = gain_ref[...].astype(F32)[2:3]
+    h3 = (scaled * gain + shift_ref[...].astype(F32)[2:3]).astype(BF16)
     put_rows(h3_ref, h3.astype(F32))
-    live = live_rows([count[step * pair + i] for i in range(pair)], slots)
+    live = live_rows([count[base + step * pair + i] for i in range(pair)], slots)
     dy = rows_of(dy_ref) * live
     dm = dy.astype(BF16)
     put_rows(dm_ref, dy)
@@ -258,7 +258,7 @@
 
 
 def cross_back(
-    other_count, dx2_ref, x1_ref, q2_ref, kv_ref, p_ref, gain_ref, out_w, q_w, kv_w,
+    base, other_count, dx2_ref, x1_ref, q2_ref, kv_ref, p_ref, gain_ref, out_w, q_w, kv_w,
     da2_ref, dq2_ref, dkv_ref, og_ref, dx1_ref, sums_ref, do_ref,
 ):
     step = pl.program_id(0)
@@ -279,7 +279,7 @@
             return store
 
         by_count(
-            other_count[step * pair + i],
+            other_count[base + step * pair + i],
             slots,
             lambda keys, i=i, block=block, put=put: attend_back(
                 i, keys, block(q2_ref, 0), block(kv_ref, 0), block(kv_ref, 1), block(do_ref, 0),
@@ -289,7 +289,7 @@
     put_rows(og_ref, mm_t(rows_of(dkv_ref).astype(BF16), kv_w[...]))
     dh2 = mm_t(rows_of(dq2_ref).astype(BF16), q_w[...])
     scaled, inverse = norm(rows_of(x1_ref))
-    put_rows(dx1_ref, dx2 + norm_back(dh2, scaled, inverse, gain_ref[1:2]))
+    put_rows(dx1_ref, dx2 + norm_back(dh2, scaled, inverse, gain_ref[...].astype(F32)[1:2]))
     sums = jnp.concatenate((column_sum(dh2 * scaled), column_sum(dh2)), axis=0)
 
     @pl.when(step == 0)
@@ -302,7 +302,7 @@
 
 
 def self_back(
-    count, dx1_ref, x_ref, qkv_ref, p_ref, gain_ref, out_w, qkv_w,
+    base, count, dx1_ref, x_ref, qkv_ref, p_ref, gain_ref, out_w, qkv_w,
     dqkv_ref, dx_ref, sums_ref, do_ref,
 ):
     step = pl.program_id(0)
@@ -322,7 +322,7 @@
             return store
 
         by_count(
-            count[step * pair + i],
+            count[base + step * pair + i],
             slots,
             lambda keys, i=i, block=block, put=put: attend_back(
                 i, keys, block(qkv_ref, 0), block(qkv_ref, 1), block(qkv_ref, 2), block(do_ref, 0),
@@ -331,7 +331,7 @@
         )
     dh1 = mm_t(rows_of(dqkv_ref).astype(BF16), qkv_w[...])
     scaled, inverse = norm(rows_of(x_ref))
-    put_rows(dx_ref, dx1 + norm_back(dh1, scaled, inverse, gain_ref[0:1]))
+    put_rows(dx_ref, dx1 + norm_back(dh1, scaled, inverse, gain_ref[...].astype(F32)[0:1]))
     sums = jnp.concatenate((column_sum(dh1 * scaled), column_sum(dh1)), axis=0)
 
     @pl.when(step == 0)
@@ -352,31 +352,41 @@
             refs[-1][...] = ref[...]
 
 
-def pack_blocks(core, *refs):
-    count = (len(refs) - 2) // 2
-    for first, out in ((0, refs[-2]), (count, refs[-1])):
+def split_first(core, bits, *refs):
+    outs = refs[-2 * PARTS :]
+    count = (len(refs) - 2 * PARTS) // (4 * PARTS)
+    for place, out in enumerate(outs):
         column = 0
-        for ref in refs[first : first + count]:
-            out[:, column : column + ref.shape[1]] = ref[...]
-            column += ref.shape[1]
-
-
-def unpack_blocks(core, own, other, *outs):
-    def copy(source):
-        column = 0
-        for out in outs:
-            out[...] = source[:, column : column + out.shape[1]]
-            column += out.shape[1]
-
-    pl.when(pl.program_id(0) == core[0])(lambda: copy(own))
-    pl.when(pl.program_id(0) != core[0])(lambda: copy(other))
+        for k in range(count):
+            first = (place * count + k) * 2
+            value = refs[first][...].astype(F32) + refs[first + 1][...].astype(F32)
+            chunk, r, _ = out.shape
+            for j in range(chunk):
+                out[j, :, column : column + value.shape[1]] = value[j * r : (j + 1) * r].astype(out.dtype)
+            column += value.shape[1]
 
 
 def add_blocks(bits, *refs):
     third = len(refs) // 3
     for one, other, out in zip(refs[:third], refs[third : 2 * third], refs[2 * third :]):
-        value = (one[...].astype(F32) + other[...].astype(F32)).astype(out.dtype)
-        out[...] = value.reshape(out.shape)
+        out[...] = (one[...].astype(F32) + other[...].astype(F32)).astype(out.dtype)
+
+
+def unpack_blocks(core, bits, *refs):
+    outs = refs[4 * PARTS :]
+    here = pl.program_id(0) == core[0]
+
+    for p in range(PARTS):
+        own = pl.program_id(1) == bits[p]
+        for where, first in ((here, 0), (jnp.logical_not(here), 2)):
+            for whose, second in ((own, 0), (jnp.logical_not(own), 1)):
+
+                @pl.when(jnp.logical_and(where, whose))
+                def _(source=refs[(first + second) * PARTS + p], p=p):
+                    column = 0
+                    for out in outs:
+                        out[0, p, 0] = source[:, :, column : column + out.shape[-1]]
+                        column += out.shape[-1]
 
 
 def merge_blocks(bits, *refs):
@@ -393,13 +403,34 @@
             out[...] = other[...].reshape(out.shape)
 
 
-def images_call(kernel, scalars, arrays, whole, outs, sums, scratch, flops, name):
+class Thread:
+    def __init__(self, arrays):
+        self.arrays = tuple(arrays)
+
+
+def passing(after):
+    threads = [x for x in after if isinstance(x, Thread)]
+    waits = [x for x in after if not isinstance(x, Thread)]
+    through = [x for t in threads for x in t.arrays]
+
+    def hand_back(results):
+        results = list(results)
+        for t in threads:
+            t.arrays, results = tuple(results[: len(t.arrays)]), results[len(t.arrays) :]
+
+    return waits, through, hand_back
+
+
+def images_call(kernel, scalars, arrays, whole, outs, sums, scratch, flops, name, part=(0, 1), into=None, after=()):
     images = arrays[0].shape[0]
     pair = PAIR if images % PAIR == 0 else 1
+    steps = images // pair // part[1]
+    first = part[0] * steps
+    into = into or ()
 
     def split_spec(shape):
         rank = len(shape)
-        return pl.BlockSpec((pair,) + tuple(shape[1:]), lambda i, *s: (i,) + (0,) * (rank - 1))
+        return pl.BlockSpec((pair,) + tuple(shape[1:]), lambda i, *s: (i + first,) + (0,) * (rank - 1))
 
     def whole_spec(shape):
         rank = len(shape)
@@ -407,22 +438,39 @@
 
     out_shapes = [jax.ShapeDtypeStruct((images,) + tail, dtype) for tail, dtype in outs]
     sum_shapes = [jax.ShapeDtypeStruct(shape, F32) for shape in sums]
-    moved = sum(x.size * x.dtype.itemsize for x in (*arrays, *whole, *out_shapes))
-    return pl.pallas_call(
-        kernel,
+    waits, through, hand_back = passing(after)
+    free = [*waits, *into, *through]
+    n_used = len(scalars) + len(arrays) + len(whole)
+    n_outs = len(out_shapes) + len(sum_shapes)
+    shapes = out_shapes + sum_shapes + [jax.ShapeDtypeStruct(x.shape, x.dtype) for x in through]
+
+    def run(*refs):
+        refs, rest = refs[:n_used], refs[n_used + len(free) :]
+        kernel(first * pair, *refs, *rest[:n_outs], *rest[n_outs + len(through) :])
+
+    aliases = {n_used + len(waits) + k: k for k in range(len(into))}
+    aliases |= {n_used + len(waits) + len(into) + k: n_outs + k for k in range(len(through))}
+    results = pl.pallas_call(
+        run,
         grid_spec=pltpu.PrefetchScalarGridSpec(
             num_scalar_prefetch=len(scalars),
-            grid=(images // pair,),
-            in_specs=[split_spec(a.shape) for a in arrays] + [whole_spec(a.shape) for a in whole],
+            grid=(steps,),
+            in_specs=[split_spec(a.shape) for a in arrays]
+            + [whole_spec(a.shape) for a in whole]
+            + [pl.BlockSpec(memory_space=pl.ANY)] * len(free),
             out_specs=[split_spec(o.shape) for o in out_shapes]
-            + [pl.BlockSpec(s.shape, lambda i, *_: (0, 0)) for s in sum_shapes],
+            + [pl.BlockSpec(s.shape, lambda i, *_: (0, 0)) for s in sum_shapes]
+            + [pl.BlockSpec(memory_space=pl.ANY)] * len(through),
             scratch_shapes=[pltpu.VMEM((pair,) + tail, dtype) for tail, dtype in scratch],
         ),
-        out_shape=out_shapes + sum_shapes,
+        out_shape=shapes,
+        input_output_aliases=aliases,
         compiler_params=pltpu.CompilerParams(vmem_limit_bytes=VMEM_BYTES),
         cost_estimate=SMALL_COST,
         name=name,
-    )(*scalars, *arrays, *whole)
+    )(*scalars, *arrays, *whole, *free)
+    hand_back(results[n_outs:])
+    return results[:n_outs]
 
 
 def take_call(source, place, sources):
@@ -446,119 +494,220 @@
     )(source, place, *sources)
 
 
-def plain_call(kernel, scalars, grid, ins, outs, name):
-    shapes = [jax.ShapeDtypeStruct(shape, BF16) for shape, _, _ in outs]
-    moved = 2 * (sum(math.prod(s.shape) for s in shapes) * 3)
-    return pl.pallas_call(
-        kernel,
+def plain_call(kernel, scalars, grid, ins, outs, name, after=()):
+    waits, through, hand_back = passing(after)
+    free = [*waits, *through]
+    n_used, n_outs = len(scalars) + len(ins), len(outs)
+
+    def run(*refs):
+        refs, rest = refs[:n_used], refs[n_used + len(free) :]
+        kernel(*refs, *rest[:n_outs])
+
+    results = pl.pallas_call(
+        run,
         grid_spec=pltpu.PrefetchScalarGridSpec(
-            num_scalar_prefetch=1,
-            grid=(grid,),
-            in_specs=[pl.BlockSpec(block, index) for _, block, index in ins],
-            out_specs=[pl.BlockSpec(block, index) for _, block, index in outs],
+            num_scalar_prefetch=len(scalars),
+            grid=grid,
+            in_specs=[pl.BlockSpec(block, index) for _, block, index in ins]
+            + [pl.BlockSpec(memory_space=pl.ANY)] * len(free),
+            out_specs=[pl.BlockSpec(block, index) for _, block, index in outs]
+            + [pl.BlockSpec(memory_space=pl.ANY)] * len(through),
         ),
-        out_shape=shapes,
+        out_shape=[jax.ShapeDtypeStruct(shape, BF16) for shape, _, _ in outs]
+        + [jax.ShapeDtypeStruct(x.shape, x.dtype) for x in through],
+        input_output_aliases={n_used + len(waits) + k: n_outs + k for k in range(len(through))},
         compiler_params=pltpu.CompilerParams(vmem_limit_bytes=VMEM_BYTES),
         cost_estimate=SMALL_COST,
         name=name,
-    )(scalars, *[a for a, _, _ in ins])
+    )(*scalars, *[a for a, _, _ in ins], *free)
+    hand_back(results[n_outs:])
+    return results[:n_outs]
 
 
 def bit_of(axis_name, bit):
     return (lax.axis_index(axis_name) // bit) % 2
 
 
+def own_place():
+    return lax.axis_index("chip") * 2 + lax.axis_index("core")
+
+
 PARTS = 3
 
 
+def sum_links(turn):
+    chip, dp = lax.axis_size("chip"), lax.axis_size("dp")
+    links = [("chip", 2**i) for i in reversed(range(chip.bit_length() - 1))]
+    links += [("dp", 2**i) for i in range(dp.bit_length() - 1)]
+    return links[turn:PARTS] + links[:turn] + links[PARTS:]
+
+
 def sum_levels():
-    head, dp = lax.axis_size("head"), lax.axis_size("dp")
-    links = [("head", 2**i) for i in reversed(range(1, head.bit_length() - 1))]
-    links += [("dp", 2**i) for i in range(dp.bit_length() - 1)]
-    turn = links[:PARTS] if len(links) >= PARTS else []
-    levels = [[turn[(p + k) % PARTS] for p in range(PARTS)] for k in range(len(turn))]
-    return levels + [[link] * PARTS for link in links[len(turn) :]]
-
-
-def total_by_halves(mats):
-    rows = mats[0].shape[0]
-    widths = [m.shape[1] for m in mats]
+    orders = [sum_links(p) for p in range(PARTS)]
+    return [list(level) for level in zip(*orders)]
+
+
+def take_own(refs_every, *outs):
+    one, two = outs
+    for j in range(refs_every.shape[0]):
+        r = refs_every.shape[2]
+        one[j] = refs_every[j, 0]
+        wide = two.shape[3]
+        for k in range(two.shape[1]):
+            two[j, k] = refs_every[j, 1, :, k * wide : (k + 1) * wide]
+
+
+def total_of_pieces(products):
+    core = bit_of("core", 1)
+    orders = [sum_links(0)[k:] + sum_links(0)[:k] for k in range(len(products))]
+    chip, dp = lax.axis_size("chip").bit_length() - 1, lax.axis_size("dp").bit_length() - 1
+    links = [("dp", 2**i) for i in reversed(range(dp))] + [("chip", 2**i) for i in reversed(range(chip))]
+    got = [flip(product(1 - core).astype(BF16), "core", 1) for product in products]
+    keep, shapes = [], []
+    for product, more in zip(products, got):
+        kept = (product(core) + more.astype(F32)).astype(BF16)
+        shapes.append((2 * kept.shape[0], kept.shape[1]))
+        keep.append(kept.reshape((2,) * len(links) + (kept.shape[0] // 2 ** len(links), kept.shape[1])))
+    for k in range(len(links)):
+        send = []
+        for m, order in enumerate(orders):
+            b, axis = bit_of(*order[k]), links.index(order[k])
+            send.append(lax.dynamic_slice_in_dim(keep[m], 1 - b, 1, axis))
+            keep[m] = lax.dynamic_slice_in_dim(keep[m], b, 1, axis)
+        got = [flip(x, *order[k]) for x, order in zip(send, orders)]
+        keep = yield tuple(send) + (Thread(keep),)
+        keep = [(one.astype(F32) + more.astype(F32)).astype(BF16) for one, more in zip(keep, got)]
+    (r, wide), (rows, columns) = sorted(x.shape[-2:] for x in keep)
+    parts = rows // r
+    pieces = []
+    for x in keep:
+        x = x.reshape(-1, r, x.shape[-1])
+        pieces.append(x.swapaxes(0, 1).reshape(1, r, wide))
+    pieces = jnp.stack(pieces, axis=1)
+    every = lax.all_gather(pieces, ("core", "dp", "chip"), axis=0, tiled=True)
+    yield (pieces,)
+    count = every.shape[0]
+    chunk = 4
+    tall = [m for m, x in enumerate(keep) if x.shape[-2] != r]
+    tall = tall[0] if tall else 1
+    one, two = pl.pallas_call(
+        take_own,
+        grid=(count // chunk,),
+        in_specs=[pl.BlockSpec((chunk, 2, r, wide), lambda i: (i, 0, 0, 0))],
+        out_specs=[
+            pl.BlockSpec((chunk, r, wide), lambda i: (i, 0, 0)),
+            pl.BlockSpec((chunk, parts, r, columns), lambda i: (i, 0, 0, 0)),
+        ],
+        out_shape=[
+            jax.ShapeDtypeStruct((count, r, wide), BF16),
+            jax.ShapeDtypeStruct((count, parts, r, columns), BF16),
+        ],
+        compiler_params=pltpu.CompilerParams(vmem_limit_bytes=VMEM_BYTES),
+        cost_estimate=SMALL_COST,
+        name="take_own",
+    )(every)
+    yield [one.reshape(shapes[0]), two.reshape(shapes[1])]
+
+
+def exchange(arrays, level):
+    if len(set(level)) == 1:
+        got = flip(jnp.concatenate(arrays, axis=0), *level[0])
+        return [(got, p * arrays[0].shape[0]) for p in range(len(arrays))]
+    return [(flip(x, *link), 0) for x, link in zip(arrays, level)]
+
+
+def total_by_halves(products):
+    levels = sum_levels()
+    core = bit_of("core", 1)
+
+    def scalars(level):
+        return jnp.stack([bit_of(*link) for link in level]).astype(jnp.int32)
+
+    got = [flip(product(1 - core).astype(BF16), "core", 1) for product in products]
+    keep = [product(core).astype(BF16) for product in products]
+    after = yield (keep[0],)
+    rows = 2 * keep[0].shape[0]
+    widths = [m.shape[1] for m in keep]
     wide = sum(widths)
-    levels = sum_levels()
     n = 2 ** len(levels)
-    part_rows = rows // (2 * PARTS)
-    r = part_rows // n
-    core = bit_of("head", 1)[None].astype(jnp.int32)
-
-    def mine(p, core):
-        return (core[0] * PARTS + p, 0)
-
-    def theirs(p, core):
-        return ((1 - core[0]) * PARTS + p, 0)
-
-    send, keep = plain_call(
-        pack_blocks,
-        core,
-        PARTS,
-        [(m, (part_rows, m.shape[1]), theirs) for m in mats] + [(m, (part_rows, m.shape[1]), mine) for m in mats],
-        [((PARTS * part_rows, wide), (part_rows, wide), lambda p, core: (p, 0))] * 2,
-        "pack_blocks",
+    r = rows // (2 * PARTS * n)
+    half = n // 2
+    chunk = min(half, max(1, 16 // r))
+    core = core[None].astype(jnp.int32)
+    ins = []
+    for other in (True, False):
+        for p in range(PARTS):
+            for one, more in zip(keep, got):
+
+                def index(i, core, bits, p=p, other=other):
+                    b = 1 - bits[p] if other else bits[p]
+                    return ((p * n + b * half) // chunk + i, 0)
+
+                ins += [(x, (chunk * r, x.shape[1]), index) for x in (one, more)]
+    outs = [((half, r, wide), (chunk, r, wide), lambda i, core, bits: (i, 0, 0))] * (2 * PARTS)
+    done = plain_call(split_first, (core, scalars(levels[0])), (half // chunk,), ins, outs, "split_first", after)
+    for k, level in enumerate(levels):
+        send, keep = done[:PARTS], done[PARTS:]
+        got = exchange(send, level)
+        after = yield (keep[0],)
+        n //= 2
+        if k + 1 == len(levels):
+            break
+        half = n // 2
+        chunk = min(half, max(1, 16 // r))
+        ones, others = [], []
+        for other in (True, False):
+            for p in range(PARTS):
+
+                def index(i, bits, p=p, other=other, first=0):
+                    b = 1 - bits[p] if other else bits[p]
+                    return ((first + b * half) // chunk + i, 0, 0)
+
+                ones.append((keep[p], (chunk, r, wide), index))
+                others.append((got[p][0], (chunk, r, wide), partial(index, first=got[p][1])))
+        outs = [((half, r, wide), (chunk, r, wide), lambda i, bits: (i, 0, 0))] * (2 * PARTS)
+        done = plain_call(add_blocks, (scalars(levels[k + 1]),), (half // chunk,), ones + others, outs, "add_blocks", after)
+    ins = [(x, (1, r, wide), lambda i, bits, f=f: (f, 0, 0)) for x, f in [(x, 0) for x in keep] + got]
+    have = plain_call(
+        add_blocks, (core,), (1,), ins, [((1, r, wide), (1, r, wide), lambda i, bits: (0, 0, 0))] * PARTS, "add_blocks", after
     )
-    got = [flip(send.reshape(PARTS, n, r, wide), "head", 1)]
-    keep = [keep.reshape(PARTS, n, r, wide)]
-
-    def is_stacked(arrays):
-        return len(arrays) == 1
-
-    def split_step(keep, got, bits, same, n):
-        half = n // 2
-        chunk = min(half, 2)
-
-        def reader(arrays, p, other):
-            def index(i, bits):
-                b = 1 - bits[p] if other else bits[p]
-                return b * (half // chunk) + i
-
-            if is_stacked(arrays):
-                return (arrays[0], (1, chunk, r, wide), lambda i, bits: (p, index(i, bits), 0, 0))
-            return (arrays[p], (chunk, r, wide), lambda i, bits: (index(i, bits), 0, 0))
-
-        order = [(p, other) for other in (True, False) for p in range(PARTS)]
-        ones = [reader(keep, p, other) for p, other in order]
-        others = [reader(got, p, other) for p, other in order]
-        outs = [((half, r, wide), (chunk, r, wide), lambda i, bits: (i, 0, 0))] * (2 * PARTS)
-        done = plain_call(add_blocks, bits, half // chunk, ones + others, outs, "add_blocks")
-        return list(done[:PARTS]), list(done[PARTS:])
-
-    def level_bits(level):
-        return jnp.stack([bit_of(*link) for link in level]).astype(jnp.int32)
-
-    for level in levels:
-        send, keep = split_step(keep, got, level_bits(level), False, n)
-        n //= 2
-        got = [flip(x, *link) for x, link in zip(send, level)]
-    ones = [(x, (1, r, wide), lambda i, bits: (0, 0, 0)) for x in keep]
-    others = [(x, (1, r, wide), lambda i, bits: (0, 0, 0)) for x in got]
-    have = plain_call(
-        add_blocks, core, 1, ones + others, [((1, r, wide), (1, r, wide), lambda i, bits: (0, 0, 0))] * PARTS, "add_blocks"
+    for level in reversed(levels):
+        got = exchange(have, level)
+        if level is levels[0]:
+            got = [x for x, _ in got]
+            break
+        after = yield (have[0],)
+        ins = [(x, (n, r, wide), lambda i, bits, f=f // n: (f, 0, 0)) for x, f in [(x, 0) for x in have] + got]
+        outs = [((2 * n, r, wide), (n, r, wide), lambda i, bits: (i, 0, 0))] * PARTS
+        have = plain_call(merge_blocks, (scalars(level),), (2,), ins, outs, "merge_blocks", after)
+        n *= 2
+    other_have = [flip(x, "core", 1) for x in have]
+    other_got = [flip(x, "core", 1) for x in got]
+    after = yield (have[0],)
+    sums = plain_call(
+        unpack_blocks,
+        (core, scalars(levels[0])),
+        (2, 2),
+        [(x, (n, r, wide), lambda h, b, core, bits: (0, 0, 0)) for x in (*have, *got, *other_have, *other_got)],
+        [((2, PARTS, 2, n, r, w), (1, PARTS, 1, n, r, w), lambda h, b, core, bits: (h, 0, b, 0, 0, 0)) for w in widths],
+        "unpack_blocks",
+        after,
     )
-    for k, level in enumerate(reversed(levels)):
-        got = [flip(x, *link) for x, link in zip(have, level)]
-        ins = [(x, (n, r, wide), lambda i, bits: (0, 0, 0)) for x in (*have, *got)]
-        outs = [((2 * n, r, wide), (n, r, wide), lambda i, bits: (i, 0, 0))] * PARTS
-        have = plain_call(merge_blocks, level_bits(level), 2, ins, outs, "merge_blocks")
-        n *= 2
-    whole = jnp.stack(have)
-    other = flip(whole, "head", 1)
-    whole, other = (x.reshape(PARTS * part_rows, wide) for x in (whole, other))
-    return plain_call(
-        unpack_blocks,
-        core,
-        2,
-        [(x, (PARTS * part_rows, wide), lambda i, core: (0, 0)) for x in (whole, other)],
-        [((rows, w), (rows // 2, w), lambda i, core: (i, 0)) for w in widths],
-        "unpack_blocks",
-    )
+    yield [x.reshape(rows, w) for x, w in zip(sums, widths)]
+
+
+def half_of_rows(left, right):
+    def product(half):
+        flat = left.reshape(-1, left.shape[-1])
+        wide = flat.shape[1] // 2
+        return row_product(lax.dynamic_slice_in_dim(flat, half * wide, wide, 1), right)
+
+    return product
+
+
+def half_of(values):
+    rows = values.shape[0] // 2
+    return lambda half: lax.dynamic_slice_in_dim(values, half * rows, rows, 0)
 
 
 def positions(patches, count):
@@ -575,18 +724,21 @@
     return lax.ppermute(values, axis_name, [(i, i ^ bit) for i in range(size)])
 
 
-def gather_group(values, after):
-    size = lax.axis_size("head")
+def gather_far(values):
     reach = {0: values}
-    bit = size // 2
+    bit = lax.axis_size("chip") // 2
     while bit:
-        sent = dict(reach)
-        for r in sent:
-            if r:
-                sent[r], after = lax.optimization_barrier((sent[r], after))
-            reach[r ^ bit] = flip(sent[r], "head", bit)
+        for r in list(reach):
+            reach[r ^ (2 * bit)] = flip(reach[r], "chip", bit)
         bit //= 2
-    return [reach[r] for r in range(size)], after
+    return reach
+
+
+def gather_near(reach):
+    both = {r: x for r, x in reach.items()}
+    for r, x in reach.items():
+        both[r ^ 1] = flip(x, "core", 1)
+    return [both[r] for r in range(len(both))]
 
 
 def row_product(left, right):
@@ -599,7 +751,7 @@
 
 
 def total(values):
-    return lax.psum(values, ("dp", "head"))
+    return lax.psum(values, ("dp", "chip", "core"))
 
 
 def body(
@@ -609,9 +761,9 @@
 ):
     images, slots, width = radar.shape
     hidden = mlp_in.shape[1]
-    me = lax.axis_index("head")
+    me = own_place()
     start = me * images
-    gains, shifts = norm_gain.astype(F32), norm_bias.astype(F32)
+    gains, shifts = norm_gain, norm_bias
 
     def own(values):
         return lax.dynamic_slice_in_dim(values, start, images, 0)
@@ -645,7 +797,8 @@
         2 * rows * width * width * 5 + 2 * attention,
         "self_forward",
     )
-    optical_blocks, x1 = gather_group(optical, x1)
+    far, x1 = lax.optimization_barrier((gather_far(optical), x1))
+    optical_blocks = gather_near(far)
     paired = take_call(partner // images ^ me, partner % images, optical_blocks)
     mixed, kv, p2, o2, h3, g, du, dm, dx2, sums3, in_sums = images_call(
         cross_and_mlp,
@@ -671,9 +824,8 @@
         2 * rows * width * (3 * width + 4 * hidden) + 2 * attention,
         "cross_and_mlp",
     )
-    grad_mlp_out, grad_mlp_in = row_product(g, dm).astype(BF16), row_product(h3, du).astype(BF16)
-    grad_mlp_out, grad_mlp_in, dx2 = lax.optimization_barrier((grad_mlp_out, grad_mlp_in, dx2))
-    grad_mlp_out, grad_mlp_in = total((grad_mlp_out, grad_mlp_in))
+    first = total_of_pieces((half_of_rows(h3, du), half_of_rows(g, dm)))
+    before_cross = next(first)
     da2, dq2, dkv, og, dx1, sums2 = images_call(
         cross_back,
         (other_count,),
@@ -690,34 +842,54 @@
         [((slots, width), BF16)],
         2 * rows * width * width * 4 + 4 * attention,
         "cross_back",
+        after=before_cross,
     )
-    first_group = (
-        row_product(o2, da2).astype(BF16),
-        row_product(h2, dq2).astype(BF16),
-        row_product(paired, dkv).astype(BF16),
-        row_product(o1, dx1.astype(BF16)).astype(BF16),
-    )
-    first_group, dx1 = lax.optimization_barrier((first_group, dx1))
-    grad_cross_out, grad_cross_q, grad_cross_kv, grad_self_out = total_by_halves(first_group)
-    dqkv, radar_grad, sums1 = images_call(
-        self_back,
-        (radar_count,),
-        (dx1, radar, qkv, p1),
-        (gains, self_out, self_qkv),
-        [((slots, 3 * width), BF16), ((slots, width), BF16)],
-        [(2, width)],
-        [((slots, width), BF16)],
-        2 * rows * width * width * 4 + 4 * attention,
-        "self_back",
-    )
-    og_blocks, dqkv = gather_group(og, dqkv)
+    second = [
+        half_of_rows(o2, da2), half_of_rows(h2, dq2), half_of_rows(paired, dkv), half_of_rows(o1, dx1.astype(BF16))
+    ]
+    core = lax.axis_index("core")
+    halves = [tuple(product(half).astype(BF16) for half in (1 - core, core)) for product in second]
+    og_far = gather_far(og)
+
+    def step_first(begun):
+        return first.send(begun[-1].arrays) if isinstance(begun[-1], Thread) else next(first)
+
+    begun = step_first(before_cross)
+    scalars, arrays, whole = (radar_count,), (dx1, radar, qkv, p1), (gains, self_out, self_qkv)
+    outs = [((slots, 3 * width), BF16), ((slots, width), BF16)]
+    made = None
+    for part in range(2):
+        *made, sums = images_call(
+            self_back, scalars, arrays, whole, outs, [(2, width)], [((slots, width), BF16)], 0, "self_back",
+            part=(part, 2), into=made, after=begun + (sum(halves, ()) if part == 0 else ()) + (tuple(og_far[r] for r in og_far if r) if part == 1 else ()),
+        )
+        sums1 = sums if part == 0 else sums1 + sums
+        begun = step_first(begun)
+    after = tuple(x for x in begun if not isinstance(x, Thread))
+    dqkv, radar_grad = made
+    og_blocks = gather_near(og_far)
     inverse_pairing = own(jnp.argsort(pairing))
     optical_grad = take_call(inverse_pairing // images ^ me, inverse_pairing % images, og_blocks)
-    grad_self_qkv = row_product(h1, dqkv).astype(BF16)
     small = jnp.concatenate((sums1, sums2, sums3, in_sums.reshape(-1, width)), axis=0)
     count = small.shape[0]
     small = jnp.pad(small.astype(BF16).T, ((0, 0), (0, 128 - count)))
-    grad_self_qkv, small = total_by_halves((grad_self_qkv, small))
+    ready = [iter(pair) for pair in halves]
+    second = [lambda half, pair=pair: next(pair) for pair in ready]
+    while not isinstance(begun, list):
+        begun = step_first(begun)
+    grad_mlp_in, grad_mlp_out = begun
+    last_round = 2 * len(sum_levels())
+    rest = total_by_halves((*second, half_of_rows(h1, dqkv), half_of(small)))
+    next(rest)
+    rounds = 0
+    while not isinstance(after, list):
+        rounds += 1
+        if rounds == 2:
+            after = after + (optical_grad,)
+        if rounds == last_round:
+            after = after + (grad_mlp_in,)
+        after = rest.send(after)
+    grad_cross_out, grad_cross_q, grad_cross_kv, grad_self_out, grad_self_qkv, small = after
     small = small[:, :count].T
     gain_grads = jnp.stack((small[0], small[2], small[4]))
     shift_grads = jnp.stack((small[1], small[3], small[5]))
@@ -730,7 +902,9 @@
 
 
 def solution(mesh):
-    split, group, copied = P(("dp", "head"), None, None), P("dp"), P()
+    dp, head = mesh.shape["dp"], mesh.shape["head"]
+    mesh = jax.sharding.Mesh(mesh.devices.reshape(dp, head // 2, 2), ("dp", "chip", "core"))
+    split, group, copied = P(("dp", "chip", "core"), None, None), P("dp"), P()
     return jax.shard_map(
         body,
         mesh=mesh,

time: 506 us -> 477 us (0.943)
  starting transfers between devices: 60.1 us -> 34 us
  Pallas kernels: 220 us -> 198 us
  waiting for transfers between devices: 107 us -> 122 us
  local copies, waits for them, and re-layouts: 34.4 us -> 22.1 us
  matrix products: 43.5 us -> 55.4 us
    ppermute x58 -> x48, waiting for transfers between devices: 79.7 us -> 122 us  [flip(): return lax.ppermute(values, axis_name, [(i, i ^ bit) for i in range(size)])]
    psum x1 -> x0, waiting for transfers between devices: 27.2 us -> none  [total(): return lax.psum(values, ('dp', 'head'))]
    ppermute x58 -> x48, starting transfers between devices: 60 us -> 34 us  [flip(): return lax.ppermute(values, axis_name, [(i, i ^ bit) for i in range(size)])]
    pallas_call x26 -> x15, Pallas kernels: 207 us -> 184 us  [the longest x5 134 us: images_call(): pl.pallas_call(run, grid_spec=pltpu.PrefetchScalarGridSpec(num_scalar_pre...]
    dot_general x7 -> x14, matrix products: 43.5 us -> 55.4 us  [row_product(): lax.dot_general(left.reshape(-1, left.shape[-1]), right.reshape(-1, right...]
    unnamed x145 -> x130, local copies, waits for them, and re-layouts: 21.4 us -> 10.5 us
    convert_element_type x2 -> x8, other arithmetic: 2.6 us -> 10.2 us  [the longest x7 8 us: total_of_pieces(): (one.astype(F32) + more.astype(F32)).astype(BF16)]
    dynamic_slice x0 -> x9, local copies, waits for them, and re-layouts: none -> 7.11 us  [the longest x6 6.38 us: total_of_pieces(): keep[m] = lax.dynamic_slice_in_dim(keep[m], b, 1, axis)]
  transfers between devices with their start and end apart: 59 -> 49, of which waited for: 25 -> 24; matrix products, arithmetic and copies ran while one was open for 11% -> 17% of each run, Pallas kernels for 27% -> 27%
where the time goes in v2:
time: 477 us; the launch traced here: 469 us
  Pallas kernels  198 us (42%)
  waiting for transfers between devices  122 us (26%)
  matrix products  55.4 us (12%)
  starting transfers between devices  34 us (7%)
  other arithmetic  23.2 us (5%)
  local copies, waits for them, and re-layouts  22.1 us (5%)
  between operations  14.9 us (3%)
    pallas_call x5, Pallas kernels, images_call(): pl.pallas_call(run, grid_spec=pltpu.PrefetchScalarGridSpec(num_scalar_pre...  134 us
    ppermute x48, waiting for transfers between devices, flip(): return lax.ppermute(values, axis_name, [(i, i ^ bit) for i in range(size)])  122 us
    dot_general x14, matrix products, row_product(): lax.dot_general(left.reshape(-1, left.shape[-1]), right.reshape(-1, right...  55.4 us
    pallas_call x9, Pallas kernels, plain_call(): pl.pallas_call(run, grid_spec=pltpu.PrefetchScalarGridSpec(num_scalar_pre...  40.3 us
    ppermute x48, starting transfers between devices, flip(): return lax.ppermute(values, axis_name, [(i, i ^ bit) for i in range(size)])  34 us
    pallas_call x2, Pallas kernels, take_call(): pl.pallas_call(take_images, grid_spec=pltpu.PrefetchScalarGridSpec(num_sc...  13.5 us
    unnamed x130, local copies, waits for them, and re-layouts  10.5 us
    pallas_call x1, Pallas kernels, total_of_pieces(): pl.pallas_call(take_own, grid=(count // chunk,), in_specs=[pl.BlockSpec((...  9.55 us
  transfers between devices with their start and end apart: 49, of which 24 were waited for; matrix products, arithmetic and copies ran while one was open for 17% of the time, Pallas kernels for 27%

profile of v2, /device:TPU:0, one launch (start us, length us, event | category | flops | bytes accessed | tf_op | source)
XLA Modules:
  0.0 469.0 jit_solution(234060383066394084)
XLA Ops:
  7.2 3.0 collective-permute-start
  13.2 25.0 %self_forward.1 = (bf16[8,136,768]{2,1,0:T(8,128)(2,1)}, bf16[8,136,2304]{2,1,0:T(8,128)(2,1)}, bf16[8,136,3072]{2,1,0:T(8,128)(2,1)}, bf16[8,136,768]{2,1,0:T(8...) custom-call(s32[8]{0:T(128)} %copy-done.49, ...), custom_call_target="tpu_custom_call" | custom-call | flops 1 | bytes 1 | tf_op jit(solution)/shard_map/self_forward/pallas_call | solution.py:453
  38.2 8.9 %collective-permute-done.refs_2_ = bf16[8,136,768]{2,1,0:T(8,128)(2,1)} collective-permute-done((bf16[8,136,768]{2,1,0:T(8,128)(2,1)}, bf16[8,136,768]{2,1,0:T(8,128)(2,1)}, u32[]{:S(2)}, u32[]{:S(2)}) %collective-permute-start) | collective-permute-done | bytes 1671200 | tf_op jit(solution)/shard_map/ppermute | solution.py:724
  53.4 6.8 %take_images.2.refs_4_ = bf16[8,136,768]{2,1,0:T(8,128)(2,1)} custom-call(s32[8]{0:T(128)} %get-tuple-element.209.source, s32[8]{0:T(128)} %get-tuple-element.184.place, bf16[8,136,768]{2,1,0:T(8,128)(2,1)} %refs_0_, bf16[8,136,768]{2,1,0:T(8,128)(2,1)} %collective-permute-done.1.refs_1_, bf16[8,136,768]{2,1,0:T(8,128)(2,1)} %collective-permute-done.refs_2_, ...), custom_call_target="tpu_custom_call" | custom-call | flops 1 | bytes 1 | tf_op jit(solution)/shard_map/take_images/pallas_call | solution.py:483
  60.1 53.3 %cross_and_mlp.1 = (bf16[8,136,768]{2,1,0:T(8,128)(2,1)}, bf16[8,136,1536]{2,1,0:T(8,128)(2,1)}, bf16[8,136,3072]{2,1,0:T(8,128)(2,1)}, bf16[8,136,768]{2,1,0:T(...) custom-call(s32[8]{0:T(128)} %copy-done.49, ...), custom_call_target="tpu_custom_call" | custom-call | flops 1 | bytes 1 | tf_op jit(solution)/shard_map/cross_and_mlp/pallas_call | solution.py:453
  113.4 7.2 %convolution_convert_fusion.3 = bf16[1536,768]{1,0:T(8,128)(2,1)} fusion(bf16[1088,768]{1,0:T(8,128)(2,1)} %bitcast.98, bf16[1088,3072]{1,0:T(8,128)(2,1)} %bitcast.89, s32[]{:T(128)S(6)} %select_n.280), kind=kOutput, calls=%fused_computation.7 | convolution fusion | flops 2568093696 | bytes 7372804 | tf_op jit(solution)/shard_map/dot_general | solution.py:745
  121.7 7.6 %convolution_convert_fusion.2 = bf16[384,3072]{1,0:T(8,128)(2,1)} fusion(bf16[1088,3072]{1,0:T(8,128)(2,1)} %bitcast.60, bf16[1088,768]{1,0:T(8,128)(2,1)S(1)} %bitcast.83, s32[]{:T(128)S(6)} %select_n.276), kind=kOutput, calls=%fused_computation.6 | convolution fusion | flops 2568093696 | bytes 9879556 | tf_op jit(solution)/shard_map/dot_general | solution.py:745
  129.3 6.6 %add_convert_fusion = bf16[1536,768]{1,0:T(8,128)(2,1)S(1)} fusion(bf16[1536,768]{1,0:T(8,128)(2,1)} %collective-permute-done.4, bf16[1088,768]{1,0:T(8,128)(2,1)} %bitcast.99, bf16[1088,3072]{1,0:T(8,128)(2,1)} %bitcast.90, s32[]{:T(128)S(6)} %select_n.279), kind=kOutput, calls=%fused_computation.2 | convolution fusion | flops 2570452992 | bytes 9732100 | tf_op jit(solution)/shard_map/dot_general | solution.py:745
  135.9 1.6 constant_dynamic-slice_fusion.10
  137.5 1.5 collective-permute-start.6
  139.1 4.8 %add_convert_fusion.1 = bf16[384,3072]{1,0:T(8,128)(2,1)S(1)} fusion(bf16[384,3072]{1,0:T(8,128)(2,1)} %collective-permute-done.3, bf16[1088,3072]{1,0:T(8,128)(2,1)S(1)} %bitcast.63, bf16[1088,768]{1,0:T(8,128)(2,1)S(1)} %bitcast.84, s32[]{:T(128)S(6)} %select_n.275), kind=kOutput, calls=%fused_computation.3 | convolution fusion | flops 2570452992 | bytes 12238852 | tf_op jit(solution)/shard_map/dot_general | solution.py:745
  146.3 25.5 %cross_back.1 = (bf16[8,136,768]{2,1,0:T(8,128)(2,1)}, bf16[8,136,768]{2,1,0:T(8,128)(2,1)}, bf16[8,136,1536]{2,1,0:T(8,128)(2,1)}, bf16[8,136,768]{2,1,0:T(8,12...) custom-call(s32[8]{0:T(128)} %copy-done.52, ...), custom_call_target="tpu_custom_call", output_to_operand_aliasing={{6}: (12, {}), {7}: (13, {})} | custom-call | flops 1 | bytes 1 | tf_op jit(solution)/shard_map/cross_back/pallas_call | solution.py:453
  171.8 2.2 convert_element_type.176
  174.2 1.8 convolution_convert_fusion.6.refs_17_.refs_8_.refs_20_.refs_32_.refs_44_.refs_56_.refs_68_
  176.0 1.8 convolution_convert_fusion.7.refs_16_
  177.8 1.7 collective-permute-start.9
  179.5 2.7 convolution_convert_fusion.4.refs_15_.refs_6_.refs_18_.refs_30_.refs_42_.refs_54_.refs_66_
  182.3 1.8 convolution_convert_fusion.8.refs_13_.refs_4_.refs_16_.refs_28_.refs_40_.refs_52_.refs_64_
  184.1 1.9 convolution_convert_fusion.9.refs_12_
  186.0 1.8 convolution_convert_fusion.10.refs_11_.refs_2_.refs_14_.refs_26_.refs_38_.refs_50_.refs_62_
  187.8 2.7 convolution_convert_fusion.5.refs_14_
  190.5 1.6 add_convert_fusion.2
  193.2 2.4 collective-permute-start.8
  195.7 1.7 add_convert_fusion.3
  199.5 1.8 convolution_convert_fusion.11.refs_10_
  201.3 15.1 %self_back.2 = (bf16[8,136,2304]{2,1,0:T(8,128)(2,1)}, bf16[8,136,768]{2,1,0:T(8,128)(2,1)}, f32[2,768]{1,0:T(2,128)}, bf16[2,2,1,1,24,3072]{5,4,3,2,1,0:T(8,128)(2,1)}, bf16[2,1,1,2,96,768]{5,4,3,2,1,0:T(8,128)(2,1)}) custom-call(s32[8]{0:T(128)} %copy-done.49, ...), custom_call_target="tpu_custom_call", output_to_operand_aliasing={{3}: (18, {}), {4}: (19, {})} | custom-call | flops 1 | bytes 1 | tf_op jit(solution)/shard_map/self_back/pallas_call | solution.py:453
  216.4 1.4 add_convert_fusion.4
  223.2 15.5 %self_back.3 = (bf16[8,136,2304]{2,1,0:T(8,128)(2,1)}, bf16[8,136,768]{2,1,0:T(8,128)(2,1)}, f32[2,768]{1,0:T(2,128)}, bf16[2,1,1,1,24,3072]{5,4,3,2,1,0:T(8,128)(2,1)}, bf16[1,1,1,2,96,768]{5,4,3,2,1,0:T(8,128)(2,1)}) custom-call(s32[8]{0:T(128)} %copy-done.49, ...), custom_call_target="tpu_custom_call", output_to_operand_aliasing={{0}: (11, {}), {1}: (12, {}), {3}: (13, {}), {4}: (14, {})} | custom-call | flops 1 | bytes 1 | tf_op jit(solution)/shard_map/self_back/pallas_call | solution.py:453
  239.8 1.3 collective-permute-start.38
  242.2 1.5 collective-permute-start.37
  243.6 2.7 collective-permute-done.38
  246.6 4.7 collective-permute-done.37
  252.2 6.4 %convolution_convert_fusion = bf16[384,2304]{1,0:T(8,128)(2,1)} fusion(bf16[1088,2304]{1,0:T(8,128)(2,1)} %bitcast.70, bf16[1088,768]{1,0:T(8,128)(2,1)} %bitcast.96, s32[]{:T(128)S(6)} %select_n.276), kind=kOutput, calls=%fused_computation.4 | convolution fusion | flops 1926070272 | bytes 7618564 | tf_op jit(solution)/shard_map/dot_general | solution.py:745
  260.3 3.6 collective-permute-done.15.refs_9_.refs_21_.refs_33_.refs_45_.refs_57_.refs_69_
  264.3 1.3 collective-permute-done.13.refs_5_.refs_17_.refs_29_.refs_41_.refs_53_.refs_65_
  267.1 6.4 %convolution_convert_fusion.1.refs_10_.refs_22_.refs_34_.refs_46_.refs_58_.refs_70_ = bf16[384,2304]{1,0:T(8,128)(2,1)} fusion(bf16[1088,2304]{1,0:T(8,128)(2,1)} %bitcast.71, bf16[1088,768]{1,0:T(8,128)(2,1)} %bitcast.97, s32[]{:T(128)S(6)} %select_n.275), kind=kOutput, calls=%fused_computation.5 | convolution fusion | flops 1926070272 | bytes 7618564 | tf_op jit(solution)/shard_map/dot_general | solution.py:745
  275.1 9.4 %split_first.1 = (bf16[8,8,6272]{2,1,0:T(8,128)(2,1)}, bf16[8,8,6272]{2,1,0:T(8,128)(2,1)}, bf16[8,8,6272]{2,1,0:T(8,128)(2,1)}, bf16[8,8,6272]{2,1,0:T(8,128)(2...) custom-call(s32[1]{0:T(128)} %bitcast.18.refs_0_, s32[3]{0:T(128)} %pad_add_fusion.refs_1_, ...), custom_call_target="tpu_custom_call" | custom-call | flops 1 | bytes 1 | tf_op jit(solution)/shard_map/split_first/pallas_call | solution.py:506
  286.1 1.6 sort.17
  289.5 6.7 %take_images.3.refs_14_ = bf16[8,136,768]{2,1,0:T(8,128)(2,1)} custom-call(s32[8]{0:T(128)} %fusion.39.source, s32[8]{0:T(128)} %get-tuple-element.182.place, bf16[8,136,768]{2,1,0:T(8,128)(2,1)} %get-tuple-element.124.refs_0_, bf16[8,136,768]{2,1,0:T(8,128)(2,1)} %collective-permute-done.10.refs_1_, bf16[8,136,768]{2,1,0:T(8,128)(2,1)} %copy-done.9, ...), custom_call_target="tpu_custom_call" | custom-call | flops 1 | bytes 1 | tf_op jit(solution)/shard_map/take_images/pallas_call | solution.py:483
  296.2 8.8 %collective-permute-done.20.refs_7_.refs_10_ = bf16[8,8,6272]{2,1,0:T(8,128)(2,1)S(1)} collective-permute-done((bf16[8,8,6272]{2,1,0:T(8,128)(2,1)}, bf16[8,8,6272]{2,1,0:T(8,128)(2,1)S(1)}, u32[]{:S(2)}, u32[]{:S(2)}) %collective-permute-start.20) | collective-permute-done | bytes 802848 | tf_op jit(solution)/shard_map/ppermute | solution.py:724
  305.4 15.1 %collective-permute-done.22.refs_9_.refs_12_ = bf16[8,8,6272]{2,1,0:T(8,128)(2,1)S(1)} collective-permute-done((bf16[8,8,6272]{2,1,0:T(8,128)(2,1)}, bf16[8,8,6272]{2,1,0:T(8,128)(2,1)S(1)}, u32[]{:S(2)}, u32[]{:S(2)}) %collective-permute-start.22) | collective-permute-done | bytes 802848 | tf_op jit(solution)/shard_map/ppermute | solution.py:724
  321.4 4.6 add_blocks.4
  327.1 7.0 %collective-permute-done.23.refs_7_.refs_10_ = bf16[4,8,6272]{2,1,0:T(8,128)(2,1)S(1)} collective-permute-done((bf16[4,8,6272]{2,1,0:T(8,128)(2,1)}, bf16[4,8,6272]{2,1,0:T(8,128)(2,1)S(1)}, u32[]{:S(2)}, u32[]{:S(2)}) %collective-permute-start.23) | collective-permute-done | bytes 401440 | tf_op jit(solution)/shard_map/ppermute | solution.py:724
  334.1 10.9 %collective-permute-done.24.refs_8_.refs_11_ = bf16[4,8,6272]{2,1,0:T(8,128)(2,1)S(1)} collective-permute-done((bf16[4,8,6272]{2,1,0:T(8,128)(2,1)}, bf16[4,8,6272]{2,1,0:T(8,128)(2,1)S(1)}, u32[]{:S(2)}, u32[]{:S(2)}) %collective-permute-start.24) | collective-permute-done | bytes 401440 | tf_op jit(solution)/shard_map/ppermute | solution.py:724
  345.9 3.4 add_blocks.5
  350.6 1.4 collective-permute-start.28
  352.0 3.2 collective-permute-done.26.refs_7_.refs_10_
  357.2 2.8 add_blocks.6
  361.1 2.7 collective-permute-start.29
  363.8 11.5 %collective-permute-done.29.refs_4_.refs_5_.refs_6_ = bf16[3,8,6272]{2,1,0:T(8,128)(2,1)S(1)} collective-permute-done((bf16[3,8,6272]{2,1,0:T(8,128)(2,1)S(1)}, bf16[3,8,6272]{2,1,0:T(8,128)(2,1)S(1)}, u32[]{:S(2)}, u32[]{:S(2)}) %collective-permute-start.29) | collective-permute-done | bytes 301088 | tf_op jit(solution)/shard_map/ppermute | solution.py:724
  376.0 1.9 add_blocks.7
  379.0 14.4 %collective-permute-done.30.refs_4_.refs_5_.refs_6_ = bf16[3,8,6272]{2,1,0:T(8,128)(2,1)S(1)} collective-permute-done((bf16[3,8,6272]{2,1,0:T(8,128)(2,1)S(1)}, bf16[3,8,6272]{2,1,0:T(8,128)(2,1)S(1)}, u32[]{:S(2)}, u32[]{:S(2)}) %collective-permute-start.30) | collective-permute-done | bytes 301088 | tf_op jit(solution)/shard_map/ppermute | solution.py:724
  394.1 2.7 merge_blocks.3
  397.4 6.5 %collective-permute-done.31.refs_4_ = bf16[2,8,6272]{2,1,0:T(8,128)(2,1)S(1)} collective-permute-done((bf16[2,8,6272]{2,1,0:T(8,128)(2,1)}, bf16[2,8,6272]{2,1,0:T(8,128)(2,1)S(1)}, u32[]{:S(2)}, u32[]{:S(2)}) %collective-permute-start.31) | collective-permute-done | bytes 200736 | tf_op jit(solution)/shard_map/ppermute | solution.py:724
  405.3 3.1 merge_blocks.4
  408.4 1.7 collective-permute-start.35
  410.1 1.3 collective-permute-start.36
  411.4 9.6 %take_own.1 = (bf16[32,24,3072]{2,1,0:T(8,128)(2,1)}, bf16[32,4,24,768]{3,2,1,0:T(8,128)(2,1)}) custom-call(bf16[32,2,24,3072]{3,2,1,0:T(8,128)(2,1)} %all-gather.2.cloned.1.call-done.refs_every), custom_call_target="tpu_custom_call" | custom-call | flops 1 | bytes 1 | tf_op jit(solution)/shard_map/take_own/pallas_call | solution.py:593
  422.0 3.8 merge_blocks.5
  426.5 2.0 collective-permute-start.40
  429.4 14.5 %collective-permute-done.39.refs_5_ = bf16[8,8,6272]{2,1,0:T(8,128)(2,1)S(1)} collective-permute-done((bf16[8,8,6272]{2,1,0:T(8,128)(2,1)}, bf16[8,8,6272]{2,1,0:T(8,128)(2,1)S(1)}, u32[]{:S(2)}, u32[]{:S(2)}) %collective-permute-start.39) | collective-permute-done | bytes 802848 | tf_op jit(solution)/shard_map/ppermute | solution.py:724
  444.6 1.4 collective-permute-done.41.refs_7_
  447.3 2.3 collective-permute-done.46.refs_12_
  450.6 8.5 %unpack_blocks.1 = (bf16[2,3,2,8,8,768]{5,4,3,2,1,0:T(8,128)(2,1)}, bf16[2,3,2,8,8,768]{5,4,3,2,1,0:T(8,128)(2,1)}, bf16[2,3,2,8,8,1536]{5,4,3,2,1,0:T(8,128)(2,...) custom-call(s32[1]{0:T(128)} %bitcast.18.refs_0_, ...), custom_call_target="tpu_custom_call" | custom-call | flops 1 | bytes 1 | tf_op jit(solution)/shard_map/unpack_blocks/pallas_call | solution.py:506
  (257 shorter events, 53.6 us)
Async XLA Ops:
  7.2 41.6 %copy-start = (s32[32,136]{1,0:T(8,128)S(1)}, s32[32,136]{1,0:T(8,128)}, u32[]{:S(2)}) copy-start(s32[32,136]{1,0:T(8,128)} %param.25) | copy-start | bytes 52228
  7.2 404.2 %all-gather.2.cloned.1.call-start = ((), (), s32[]{:S(2)}) async-start(), calls=%async_computation | async-start | bytes 9732096 | tf_op jit(solution)/shard_map/all_gather | solution.py:587
  7.2 39.9 %collective-permute-start = (bf16[8,136,768]{2,1,0:T(8,128)(2,1)}, bf16[8,136,768]{2,1,0:T(8,128)(2,1)}, u32[]{:S(2)}, u32[]{:S(2)}) collective-permute-start(bf16[8,136,768]{2,1,0:T(8,128)(2,1)} %refs_0_), channel_id=1, source_target_pairs={{0,2},{2,0},{1,3},{3,1},{4,6},{6,4},{5,7},{7,5},{8,10},{10,8},{9,1... | collective-permute-start | bytes 5013512 | tf_op jit(solution)/shard_map/ppermute | solution.py:724
  13.2 33.9 %copy-start.22 = (bf16[8,136,768]{2,1,0:T(8,128)(2,1)S(1)}, bf16[8,136,768]{2,1,0:T(8,128)(2,1)}, u32[]{:S(2)}) copy-start(bf16[8,136,768]{2,1,0:T(8,128)(2,1)} %refs_0_) | copy-start | bytes 5013508
  13.2 34.5 %copy-start.58 = (s32[32]{0:T(128)S(1)}, s32[32]{0:T(128)}, u32[]{:S(2)}) copy-start(s32[32]{0:T(128)} %param.26) | copy-start | bytes 388
  13.2 36.2 %copy-start.61 = (s32[32]{0:T(128)S(1)}, s32[32]{0:T(128)}, u32[]{:S(2)}) copy-start(s32[32]{0:T(128)} %param.23) | copy-start | bytes 388
  13.2 36.9 %copy-start.54 = (bf16[3072]{0:T(1024)(128)(2,1)S(1)}, bf16[3072]{0:T(1024)(128)(2,1)}, u32[]{:S(2)}) copy-start(bf16[3072]{0:T(1024)(128)(2,1)} %param.35) | copy-start | bytes 18436
  13.2 37.5 %copy-start.57 = (bf16[768]{0:T(1024)(128)(2,1)S(1)}, bf16[768]{0:T(1024)(128)(2,1)}, u32[]{:S(2)}) copy-start(bf16[768]{0:T(1024)(128)(2,1)} %param.37) | copy-start | bytes 4612
  47.1 6.0 %collective-permute-start.1 = (bf16[8,136,768]{2,1,0:T(8,128)(2,1)S(1)}, bf16[8,136,768]{2,1,0:T(8,128)(2,1)}, u32[]{:S(2)}, u32[]{:S(2)}) collective-permute-start(bf16[8,136,768]{2,1,0:T(8,128)(2,1)S(1)} %copy-done.22), channel_id=1, source_target_pairs={{0,1},{1,0},{2,3},{3,2},{4,5},{5,4},{6,7},{7,6},{8,9},{9,8},{10,11... | collective-permute-start | bytes 5013512 | tf_op jit(solution)/shard_map/ppermute | solution.py:724
  47.1 6.3 %collective-permute-start.2 = (bf16[8,136,768]{2,1,0:T(8,128)(2,1)}, bf16[8,136,768]{2,1,0:T(8,128)(2,1)}, u32[]{:S(2)}, u32[]{:S(2)}) collective-permute-start(bf16[8,136,768]{2,1,0:T(8,128)(2,1)} %collective-permute-done.refs_2_), channel_id=1, source_target_pairs={{0,1},{1,0},{2,3},{3,2},{4,5},{5,4},{6,7},{7,6},{8,9},{9,8},{10,11... | collective-permute-start | bytes 5013512 | tf_op jit(solution)/shard_map/ppermute | solution.py:724
  50.0 10.1 %copy-start.52 = (s32[8]{0:T(128)}, s32[8]{0:T(128)S(1)}, u32[]{:S(2)}) copy-start(s32[8]{0:T(128)S(1)} %gather_fusion) | copy-start | bytes 100
  120.7 8.6 %collective-permute-start.4 = (bf16[1536,768]{1,0:T(8,128)(2,1)}, bf16[1536,768]{1,0:T(8,128)(2,1)}, u32[]{:S(2)}, u32[]{:S(2)}) collective-permute-start(bf16[1536,768]{1,0:T(8,128)(2,1)} %convolution_convert_fusion.3), channel_id=1, source_target_pairs={{0,1},{1,0},{2,3},{3,2},{4,5},{5,4},{6,7},{7,6},{8,9},{9,8},{10,11... | collective-permute-start | bytes 7077896 | tf_op jit(solution)/shard_map/ppermute | solution.py:724
  129.3 9.8 %collective-permute-start.3 = (bf16[384,3072]{1,0:T(8,128)(2,1)}, bf16[384,3072]{1,0:T(8,128)(2,1)}, u32[]{:S(2)}, u32[]{:S(2)}) collective-permute-start(bf16[384,3072]{1,0:T(8,128)(2,1)} %convolution_convert_fusion.2), channel_id=1, source_target_pairs={{0,1},{1,0},{2,3},{3,2},{4,5},{5,4},{6,7},{7,6},{8,9},{9,8},{10,11... | collective-permute-start | bytes 7077896 | tf_op jit(solution)/shard_map/ppermute | solution.py:724
  137.5 53.0 %collective-permute-start.6 = (bf16[2,2,1,2,96,768]{5,4,3,2,1,0:T(8,128)(2,1)}, bf16[2,2,1,2,96,768]{5,4,3,2,1,0:T(8,128)(2,1)}, u32[]{:S(2)}, u32[]{:S(2)}) collective-permute-start(bf16[2,2,1,2,96,768]{5,4,3,2,1,0:T(8,128)(2,1)} %get-tuple-element.187.refs_11_), channel_id=1, source_target_pairs={{0,4},{4,0},{8,12},{12,8},{16,20},{20,16},{24,28},{28,24},{1,5},{5... | collective-permute-start | bytes 3538952 | tf_op jit(solution)/shard_map/ppermute | solution.py:724
  145.1 50.6 %collective-permute-start.5 = (bf16[2,2,2,1,24,3072]{5,4,3,2,1,0:T(8,128)(2,1)S(1)}, bf16[2,2,2,1,24,3072]{5,4,3,2,1,0:T(8,128)(2,1)}, u32[]{:S(2)}, u32[]{:S(2)}) collective-permute-start(bf16[2,2,2,1,24,3072]{5,4,3,2,1,0:T(8,128)(2,1)S(1)} %get-tuple-element.189.refs_10_), channel_id=1, source_target_pairs={{0,2},{2,0},{1,3},{3,1},{4,6},{6,4},{5,7},{7,5},{8,10},{10,8},{9,1... | collective-permute-start | bytes 3538952 | tf_op jit(solution)/shard_map/ppermute | solution.py:724
  177.8 44.2 %collective-permute-start.9 = (bf16[8,136,768]{2,1,0:T(8,128)(2,1)}, bf16[8,136,768]{2,1,0:T(8,128)(2,1)S(1)}, u32[]{:S(2)}, u32[]{:S(2)}) collective-permute-start(bf16[8,136,768]{2,1,0:T(8,128)(2,1)} %get-tuple-element.124.refs_0_), channel_id=1, source_target_pairs={{0,2},{2,0},{1,3},{3,1},{4,6},{6,4},{5,7},{7,5},{8,10},{10,8},{9,1... | collective-permute-start | bytes 5013512 | tf_op jit(solution)/shard_map/ppermute | solution.py:724
  193.2 23.2 %collective-permute-start.8 = (bf16[2,1,1,2,96,768]{5,4,3,2,1,0:T(8,128)(2,1)}, bf16[2,1,1,2,96,768]{5,4,3,2,1,0:T(8,128)(2,1)}, u32[]{:S(2)}, u32[]{:S(2)}) collective-permute-start(bf16[2,1,1,2,96,768]{5,4,3,2,1,0:T(8,128)(2,1)} %get-tuple-element.191.refs_9_), channel_id=1, source_target_pairs={{0,8},{4,12},{8,0},{12,4},{16,24},{20,28},{24,16},{28,20},{1,9},{5... | collective-permute-start | bytes 1769480 | tf_op jit(solution)/shard_map/ppermute | solution.py:724
  198.3 21.2 %collective-permute-start.7 = (bf16[2,2,1,1,24,3072]{5,4,3,2,1,0:T(8,128)(2,1)S(1)}, bf16[2,2,1,1,24,3072]{5,4,3,2,1,0:T(8,128)(2,1)}, u32[]{:S(2)}, u32[]{:S(2)}) collective-permute-start(bf16[2,2,1,1,24,3072]{5,4,3,2,1,0:T(8,128)(2,1)S(1)} %get-tuple-element.193.refs_8_), channel_id=1, source_target_pairs={{0,4},{4,0},{8,12},{12,8},{16,20},{20,16},{24,28},{28,24},{1,5},{5... | collective-permute-start | bytes 1769480 | tf_op jit(solution)/shard_map/ppermute | solution.py:724
  218.7 20.1 %collective-permute-start.19 = (bf16[1,1,1,2,96,768]{5,4,3,2,1,0:T(8,128)(2,1)S(1)}, bf16[1,1,1,2,96,768]{5,4,3,2,1,0:T(8,128)(2,1)S(1)}, u32[]{:S(2)}, u32[]{:S(2)}) collective-permute-start(bf16[1,1,1,2,96,768]{5,4,3,2,1,0:T(8,128)(2,1)S(1)} %get-tuple-element.195.refs_9_), channel_id=1, source_target_pairs={{0,16},{4,20},{8,24},{12,28},{16,0},{20,4},{24,8},{28,12},{1,17},{... | collective-permute-start | bytes 884744 | tf_op jit(solution)/shard_map/ppermute | solution.py:724
  221.4 19.6 %collective-permute-start.18 = (bf16[2,1,1,1,24,3072]{5,4,3,2,1,0:T(8,128)(2,1)S(1)}, bf16[2,1,1,1,24,3072]{5,4,3,2,1,0:T(8,128)(2,1)S(1)}, u32[]{:S(2)}, u32[]{:S(2)}) collective-permute-start(bf16[2,1,1,1,24,3072]{5,4,3,2,1,0:T(8,128)(2,1)S(1)} %get-tuple-element.197.refs_8_), channel_id=1, source_target_pairs={{0,8},{4,12},{8,0},{12,4},{16,24},{20,28},{24,16},{28,20},{1,9},{5... | collective-permute-start | bytes 884744 | tf_op jit(solution)/shard_map/ppermute | solution.py:724
  239.8 12.3 %copy-start.39 = (bf16[1,1,1,1,96,768]{5,4,3,2,1,0:T(8,128)(2,1)}, bf16[1,1,1,1,96,768]{5,4,3,2,1,0:T(8,128)(2,1)S(1)}, u32[]{:S(2)}) copy-start(bf16[1,1,1,1,96,768]{5,4,3,2,1,0:T(8,128)(2,1)S(1)} %constant_dynamic-slice_fusion.refs_75_) | copy-start | bytes 442372
  239.8 6.6 %collective-permute-start.38 = (bf16[1,1,1,1,96,768]{5,4,3,2,1,0:T(8,128)(2,1)S(1)}, bf16[1,1,1,1,96,768]{5,4,3,2,1,0:T(8,128)(2,1)S(1)}, u32[]{:S(2)}, u32[]{:S(2)}) collective-permute-start(bf16[1,1,1,1,96,768]{5,4,3,2,1,0:T(8,128)(2,1)S(1)} %constant_dynamic-slice_fusion.refs_75_), channel_id=1, source_target_pairs={{0,2},{2,0},{1,3},{3,1},{4,6},{6,4},{5,7},{7,5},{8,10},{10,8},{9,1... | collective-permute-start | bytes 442376 | tf_op jit(solution)/shard_map/ppermute | solution.py:724
  242.2 9.1 %collective-permute-start.37 = (bf16[1,1,1,1,24,3072]{5,4,3,2,1,0:T(8,128)(2,1)S(1)}, bf16[1,1,1,1,24,3072]{5,4,3,2,1,0:T(8,128)(2,1)S(1)}, u32[]{:S(2)}, u32[]{:S(2)}) collective-permute-start(bf16[1,1,1,1,24,3072]{5,4,3,2,1,0:T(8,128)(2,1)S(1)} %constant_dynamic-slice_fusion.1.refs_74_), channel_id=1, source_target_pairs={{0,16},{4,20},{8,24},{12,28},{16,0},{20,4},{24,8},{28,12},{1,17},{... | collective-permute-start | bytes 442376 | tf_op jit(solution)/shard_map/ppermute | solution.py:724
  252.1 13.9 %copy-start.55 = (f32[2,768]{1,0:T(2,128)S(1)}, f32[2,768]{1,0:T(2,128)}, u32[]{:S(2)}) copy-start(f32[2,768]{1,0:T(2,128)} %get-tuple-element.131) | copy-start | bytes 18436
  252.1 13.8 %copy-start.56 = (f32[2,768]{1,0:T(2,128)S(1)}, f32[2,768]{1,0:T(2,128)}, u32[]{:S(2)}) copy-start(f32[2,768]{1,0:T(2,128)} %get-tuple-element.132) | copy-start | bytes 18436
  258.6 14.9 %collective-permute-start.16 = (bf16[384,2304]{1,0:T(8,128)(2,1)}, bf16[384,2304]{1,0:T(8,128)(2,1)S(1)}, u32[]{:S(2)}, u32[]{:S(2)}) collective-permute-start(bf16[384,2304]{1,0:T(8,128)(2,1)} %convolution_convert_fusion), channel_id=1, source_target_pairs={{0,1},{1,0},{2,3},{3,2},{4,5},{5,4},{6,7},{7,6},{8,9},{9,8},{10,11... | collective-permute-start | bytes 5308424 | tf_op jit(solution)/shard_map/ppermute | solution.py:724
  258.6 5.3 %collective-permute-start.15 = (bf16[384,768]{1,0:T(8,128)(2,1)}, bf16[384,768]{1,0:T(8,128)(2,1)}, u32[]{:S(2)}, u32[]{:S(2)}) collective-permute-start(bf16[384,768]{1,0:T(8,128)(2,1)} %convolution_convert_fusion.7.refs_16_), channel_id=1, source_target_pairs={{0,1},{1,0},{2,3},{3,2},{4,5},{5,4},{6,7},{7,6},{8,9},{9,8},{10,11... | collective-permute-start | bytes 1769480 | tf_op jit(solution)/shard_map/ppermute | solution.py:724
  259.1 6.5 %collective-permute-start.13 = (bf16[384,768]{1,0:T(8,128)(2,1)}, bf16[384,768]{1,0:T(8,128)(2,1)}, u32[]{:S(2)}, u32[]{:S(2)}) collective-permute-start(bf16[384,768]{1,0:T(8,128)(2,1)} %convolution_convert_fusion.9.refs_12_), channel_id=1, source_target_pairs={{0,1},{1,0},{2,3},{3,2},{4,5},{5,4},{6,7},{7,6},{8,9},{9,8},{10,11... | collective-permute-start | bytes 1769480 | tf_op jit(solution)/shard_map/ppermute | solution.py:724
  259.1 14.4 %collective-permute-start.14 = (bf16[384,1536]{1,0:T(8,128)(2,1)}, bf16[384,1536]{1,0:T(8,128)(2,1)S(1)}, u32[]{:S(2)}, u32[]{:S(2)}) collective-permute-start(bf16[384,1536]{1,0:T(8,128)(2,1)} %convolution_convert_fusion.5.refs_14_), channel_id=1, source_target_pairs={{0,1},{1,0},{2,3},{3,2},{4,5},{5,4},{6,7},{7,6},{8,9},{9,8},{10,11... | collective-permute-start | bytes 3538952 | tf_op jit(solution)/shard_map/ppermute | solution.py:724
  259.6 7.3 %collective-permute-start.12 = (bf16[384,768]{1,0:T(8,128)(2,1)}, bf16[384,768]{1,0:T(8,128)(2,1)}, u32[]{:S(2)}, u32[]{:S(2)}) collective-permute-start(bf16[384,768]{1,0:T(8,128)(2,1)} %convolution_convert_fusion.11.refs_10_), channel_id=1, source_target_pairs={{0,1},{1,0},{2,3},{3,2},{4,5},{5,4},{6,7},{7,6},{8,9},{9,8},{10,11... | collective-permute-start | bytes 1769480 | tf_op jit(solution)/shard_map/ppermute | solution.py:724
  263.9 25.5 %collective-permute-start.10 = (bf16[8,136,768]{2,1,0:T(8,128)(2,1)}, bf16[8,136,768]{2,1,0:T(8,128)(2,1)}, u32[]{:S(2)}, u32[]{:S(2)}) collective-permute-start(bf16[8,136,768]{2,1,0:T(8,128)(2,1)} %get-tuple-element.124.refs_0_), channel_id=1, source_target_pairs={{0,1},{1,0},{2,3},{3,2},{4,5},{5,4},{6,7},{7,6},{8,9},{9,8},{10,11... | collective-permute-start | bytes 5013512 | tf_op jit(solution)/shard_map/ppermute | solution.py:724
  265.6 23.9 %collective-permute-start.11 = (bf16[8,136,768]{2,1,0:T(8,128)(2,1)}, bf16[8,136,768]{2,1,0:T(8,128)(2,1)}, u32[]{:S(2)}, u32[]{:S(2)}) collective-permute-start(bf16[8,136,768]{2,1,0:T(8,128)(2,1)} %copy-done.9), channel_id=1, source_target_pairs={{0,1},{1,0},{2,3},{3,2},{4,5},{5,4},{6,7},{7,6},{8,9},{9,8},{10,11... | collective-permute-start | bytes 5013512 | tf_op jit(solution)/shard_map/ppermute | solution.py:724
  266.9 6.6 %collective-permute-start.17 = (bf16[384,128]{1,0:T(8,128)(2,1)S(1)}, bf16[384,128]{1,0:T(8,128)(2,1)S(1)}, u32[]{:S(2)}, u32[]{:S(2)}) collective-permute-start(bf16[384,128]{1,0:T(8,128)(2,1)S(1)} %get-tuple-element.198), channel_id=1, source_target_pairs={{0,1},{1,0},{2,3},{3,2},{4,5},{5,4},{6,7},{7,6},{8,9},{9,8},{10,11... | collective-permute-start | bytes 294920 | tf_op jit(solution)/shard_map/ppermute | solution.py:724
  275.1 11.0 %copy-start.59 = (s32[32]{0:T(128)S(1)}, s32[32]{0:T(128)}, u32[]{:S(2)}) copy-start(s32[32]{0:T(128)} %param.26) | copy-start | bytes 388
  284.5 20.4 %collective-permute-start.20 = (bf16[8,8,6272]{2,1,0:T(8,128)(2,1)}, bf16[8,8,6272]{2,1,0:T(8,128)(2,1)S(1)}, u32[]{:S(2)}, u32[]{:S(2)}) collective-permute-start(bf16[8,8,6272]{2,1,0:T(8,128)(2,1)} %get-tuple-element.141), channel_id=1, source_target_pairs={{0,2},{2,0},{1,3},{3,1},{4,6},{6,4},{5,7},{7,5},{8,10},{10,8},{9,1... | collective-permute-start | bytes 2408456 | tf_op jit(solution)/shard_map/ppermute | solution.py:724
  285.3 20.1 %collective-permute-start.21 = (bf16[8,8,6272]{2,1,0:T(8,128)(2,1)}, bf16[8,8,6272]{2,1,0:T(8,128)(2,1)S(1)}, u32[]{:S(2)}, u32[]{:S(2)}) collective-permute-start(bf16[8,8,6272]{2,1,0:T(8,128)(2,1)} %get-tuple-element.142), channel_id=1, source_target_pairs={{0,4},{4,0},{8,12},{12,8},{16,20},{20,16},{24,28},{28,24},{1,5},{5... | collective-permute-start | bytes 2408456 | tf_op jit(solution)/shard_map/ppermute | solution.py:724
  285.8 34.7 %collective-permute-start.22 = (bf16[8,8,6272]{2,1,0:T(8,128)(2,1)}, bf16[8,8,6272]{2,1,0:T(8,128)(2,1)S(1)}, u32[]{:S(2)}, u32[]{:S(2)}) collective-permute-start(bf16[8,8,6272]{2,1,0:T(8,128)(2,1)} %get-tuple-element.143), channel_id=1, source_target_pairs={{0,8},{4,12},{8,0},{12,4},{16,24},{20,28},{24,16},{28,20},{1,9},{5... | collective-permute-start | bytes 2408456 | tf_op jit(solution)/shard_map/ppermute | solution.py:724
  305.0 15.6 %copy-start.13 = (bf16[8,8,6272]{2,1,0:T(8,128)(2,1)}, bf16[8,8,6272]{2,1,0:T(8,128)(2,1)S(1)}, u32[]{:S(2)}) copy-start(bf16[8,8,6272]{2,1,0:T(8,128)(2,1)S(1)} %collective-permute-done.20.refs_7_.refs_10_) | copy-start | bytes 2408452
  305.4 15.1 %copy-start.14 = (bf16[8,8,6272]{2,1,0:T(8,128)(2,1)}, bf16[8,8,6272]{2,1,0:T(8,128)(2,1)S(1)}, u32[]{:S(2)}) copy-start(bf16[8,8,6272]{2,1,0:T(8,128)(2,1)S(1)} %collective-permute-done.21.refs_8_.refs_11_) | copy-start | bytes 2408452
  326.0 8.1 %collective-permute-start.23 = (bf16[4,8,6272]{2,1,0:T(8,128)(2,1)}, bf16[4,8,6272]{2,1,0:T(8,128)(2,1)S(1)}, u32[]{:S(2)}, u32[]{:S(2)}) collective-permute-start(bf16[4,8,6272]{2,1,0:T(8,128)(2,1)} %get-tuple-element.147), channel_id=1, source_target_pairs={{0,4},{4,0},{8,12},{12,8},{16,20},{20,16},{24,28},{28,24},{1,5},{5... | collective-permute-start | bytes 1204232 | tf_op jit(solution)/shard_map/ppermute | solution.py:724
  326.1 18.9 %collective-permute-start.24 = (bf16[4,8,6272]{2,1,0:T(8,128)(2,1)}, bf16[4,8,6272]{2,1,0:T(8,128)(2,1)S(1)}, u32[]{:S(2)}, u32[]{:S(2)}) collective-permute-start(bf16[4,8,6272]{2,1,0:T(8,128)(2,1)} %get-tuple-element.148), channel_id=1, source_target_pairs={{0,8},{4,12},{8,0},{12,4},{16,24},{20,28},{24,16},{28,20},{1,9},{5... | collective-permute-start | bytes 1204232 | tf_op jit(solution)/shard_map/ppermute | solution.py:724
  326.1 18.9 %collective-permute-start.25 = (bf16[4,8,6272]{2,1,0:T(8,128)(2,1)}, bf16[4,8,6272]{2,1,0:T(8,128)(2,1)S(1)}, u32[]{:S(2)}, u32[]{:S(2)}) collective-permute-start(bf16[4,8,6272]{2,1,0:T(8,128)(2,1)} %get-tuple-element.149), channel_id=1, source_target_pairs={{0,2},{2,0},{1,3},{3,1},{4,6},{6,4},{5,7},{7,5},{8,10},{10,8},{9,1... | collective-permute-start | bytes 1204232 | tf_op jit(solution)/shard_map/ppermute | solution.py:724
  334.1 10.9 %copy-start.23 = (bf16[4,8,6272]{2,1,0:T(8,128)(2,1)}, bf16[4,8,6272]{2,1,0:T(8,128)(2,1)S(1)}, u32[]{:S(2)}) copy-start(bf16[4,8,6272]{2,1,0:T(8,128)(2,1)S(1)} %collective-permute-done.23.refs_7_.refs_10_) | copy-start | bytes 1204228
  349.3 5.9 %collective-permute-start.26 = (bf16[2,8,6272]{2,1,0:T(8,128)(2,1)}, bf16[2,8,6272]{2,1,0:T(8,128)(2,1)S(1)}, u32[]{:S(2)}, u32[]{:S(2)}) collective-permute-start(bf16[2,8,6272]{2,1,0:T(8,128)(2,1)} %get-tuple-element.153), channel_id=1, source_target_pairs={{0,8},{4,12},{8,0},{12,4},{16,24},{20,28},{24,16},{28,20},{1,9},{5... | collective-permute-start | bytes 602120 | tf_op jit(solution)/shard_map/ppermute | solution.py:724
  349.5 5.9 %collective-permute-start.27 = (bf16[2,8,6272]{2,1,0:T(8,128)(2,1)}, bf16[2,8,6272]{2,1,0:T(8,128)(2,1)S(1)}, u32[]{:S(2)}, u32[]{:S(2)}) collective-permute-start(bf16[2,8,6272]{2,1,0:T(8,128)(2,1)} %get-tuple-element.154), channel_id=1, source_target_pairs={{0,2},{2,0},{1,3},{3,1},{4,6},{6,4},{5,7},{7,5},{8,10},{10,8},{9,1... | collective-permute-start | bytes 602120 | tf_op jit(solution)/shard_map/ppermute | solution.py:724
  350.6 5.9 %collective-permute-start.28 = (bf16[2,8,6272]{2,1,0:T(8,128)(2,1)}, bf16[2,8,6272]{2,1,0:T(8,128)(2,1)S(1)}, u32[]{:S(2)}, u32[]{:S(2)}) collective-permute-start(bf16[2,8,6272]{2,1,0:T(8,128)(2,1)} %get-tuple-element.155), channel_id=1, source_target_pairs={{0,4},{4,0},{8,12},{12,8},{16,20},{20,16},{24,28},{28,24},{1,5},{5... | collective-permute-start | bytes 602120 | tf_op jit(solution)/shard_map/ppermute | solution.py:724
  361.1 14.2 %collective-permute-start.29 = (bf16[3,8,6272]{2,1,0:T(8,128)(2,1)S(1)}, bf16[3,8,6272]{2,1,0:T(8,128)(2,1)S(1)}, u32[]{:S(2)}, u32[]{:S(2)}) collective-permute-start(bf16[3,8,6272]{2,1,0:T(8,128)(2,1)S(1)} %pad_maximum_fusion), channel_id=1, source_target_pairs={{0,16},{4,20},{8,24},{12,28},{16,0},{20,4},{24,8},{28,12},{1,17},{... | collective-permute-start | bytes 903176 | tf_op jit(solution)/shard_map/ppermute | solution.py:724
  378.9 14.4 %collective-permute-start.30 = (bf16[3,8,6272]{2,1,0:T(8,128)(2,1)S(1)}, bf16[3,8,6272]{2,1,0:T(8,128)(2,1)S(1)}, u32[]{:S(2)}, u32[]{:S(2)}) collective-permute-start(bf16[3,8,6272]{2,1,0:T(8,128)(2,1)S(1)} %pad_maximum_fusion.1), channel_id=1, source_target_pairs={{0,16},{4,20},{8,24},{12,28},{16,0},{20,4},{24,8},{28,12},{1,17},{... | collective-permute-start | bytes 903176 | tf_op jit(solution)/shard_map/ppermute | solution.py:724
  396.7 7.1 %collective-permute-start.31 = (bf16[2,8,6272]{2,1,0:T(8,128)(2,1)}, bf16[2,8,6272]{2,1,0:T(8,128)(2,1)S(1)}, u32[]{:S(2)}, u32[]{:S(2)}) collective-permute-start(bf16[2,8,6272]{2,1,0:T(8,128)(2,1)} %get-tuple-element.165.refs_1_.refs_7_), channel_id=1, source_target_pairs={{0,8},{4,12},{8,0},{12,4},{16,24},{20,28},{24,16},{28,20},{1,9},{5... | collective-permute-start | bytes 602120 | tf_op jit(solution)/shard_map/ppermute | solution.py:724
  396.7 7.2 %collective-permute-start.32 = (bf16[2,8,6272]{2,1,0:T(8,128)(2,1)}, bf16[2,8,6272]{2,1,0:T(8,128)(2,1)S(1)}, u32[]{:S(2)}, u32[]{:S(2)}) collective-permute-start(bf16[2,8,6272]{2,1,0:T(8,128)(2,1)} %get-tuple-element.166.refs_2_), channel_id=1, source_target_pairs={{0,2},{2,0},{1,3},{3,1},{4,6},{6,4},{5,7},{7,5},{8,10},{10,8},{9,1... | collective-permute-start | bytes 602120 | tf_op jit(solution)/shard_map/ppermute | solution.py:724
  397.4 6.8 %collective-permute-start.33 = (bf16[2,8,6272]{2,1,0:T(8,128)(2,1)}, bf16[2,8,6272]{2,1,0:T(8,128)(2,1)S(1)}, u32[]{:S(2)}, u32[]{:S(2)}) collective-permute-start(bf16[2,8,6272]{2,1,0:T(8,128)(2,1)} %get-tuple-element.167.refs_3_), channel_id=1, source_target_pairs={{0,4},{4,0},{8,12},{12,8},{16,20},{20,16},{24,28},{28,24},{1,5},{5... | collective-permute-start | bytes 602120 | tf_op jit(solution)/shard_map/ppermute | solution.py:724
  408.4 12.6 %collective-permute-start.34 = (bf16[4,8,6272]{2,1,0:T(8,128)(2,1)}, bf16[4,8,6272]{2,1,0:T(8,128)(2,1)S(1)}, u32[]{:S(2)}, u32[]{:S(2)}) collective-permute-start(bf16[4,8,6272]{2,1,0:T(8,128)(2,1)} %get-tuple-element.168.refs_1_.refs_7_), channel_id=1, source_target_pairs={{0,4},{4,0},{8,12},{12,8},{16,20},{20,16},{24,28},{28,24},{1,5},{5... | collective-permute-start | bytes 1204232 | tf_op jit(solution)/shard_map/ppermute | solution.py:724
  408.4 12.6 %collective-permute-start.35 = (bf16[4,8,6272]{2,1,0:T(8,128)(2,1)}, bf16[4,8,6272]{2,1,0:T(8,128)(2,1)S(1)}, u32[]{:S(2)}, u32[]{:S(2)}) collective-permute-start(bf16[4,8,6272]{2,1,0:T(8,128)(2,1)} %get-tuple-element.169.refs_2_), channel_id=1, source_target_pairs={{0,8},{4,12},{8,0},{12,4},{16,24},{20,28},{24,16},{28,20},{1,9},{5... | collective-permute-start | bytes 1204232 | tf_op jit(solution)/shard_map/ppermute | solution.py:724
  410.1 10.9 %collective-permute-start.36 = (bf16[4,8,6272]{2,1,0:T(8,128)(2,1)}, bf16[4,8,6272]{2,1,0:T(8,128)(2,1)S(1)}, u32[]{:S(2)}, u32[]{:S(2)}) collective-permute-start(bf16[4,8,6272]{2,1,0:T(8,128)(2,1)} %get-tuple-element.170.refs_3_), channel_id=1, source_target_pairs={{0,2},{2,0},{1,3},{3,1},{4,6},{6,4},{5,7},{7,5},{8,10},{10,8},{9,1... | collective-permute-start | bytes 1204232 | tf_op jit(solution)/shard_map/ppermute | solution.py:724
  425.8 18.0 %collective-permute-start.39 = (bf16[8,8,6272]{2,1,0:T(8,128)(2,1)}, bf16[8,8,6272]{2,1,0:T(8,128)(2,1)S(1)}, u32[]{:S(2)}, u32[]{:S(2)}) collective-permute-start(bf16[8,8,6272]{2,1,0:T(8,128)(2,1)} %get-tuple-element.172.refs_2_.refs_14_), channel_id=1, source_target_pairs={{0,2},{2,0},{1,3},{3,1},{4,6},{6,4},{5,7},{7,5},{8,10},{10,8},{9,1... | collective-permute-start | bytes 2408456 | tf_op jit(solution)/shard_map/ppermute | solution.py:724
  426.5 18.0 %collective-permute-start.40 = (bf16[8,8,6272]{2,1,0:T(8,128)(2,1)}, bf16[8,8,6272]{2,1,0:T(8,128)(2,1)S(1)}, u32[]{:S(2)}, u32[]{:S(2)}) collective-permute-start(bf16[8,8,6272]{2,1,0:T(8,128)(2,1)} %get-tuple-element.173.refs_3_), channel_id=1, source_target_pairs={{0,4},{4,0},{8,12},{12,8},{16,20},{20,16},{24,28},{28,24},{1,5},{5... | collective-permute-start | bytes 2408456 | tf_op jit(solution)/shard_map/ppermute | solution.py:724
  428.5 17.5 %collective-permute-start.41 = (bf16[8,8,6272]{2,1,0:T(8,128)(2,1)}, bf16[8,8,6272]{2,1,0:T(8,128)(2,1)S(1)}, u32[]{:S(2)}, u32[]{:S(2)}) collective-permute-start(bf16[8,8,6272]{2,1,0:T(8,128)(2,1)} %get-tuple-element.174.refs_4_), channel_id=1, source_target_pairs={{0,8},{4,12},{8,0},{12,4},{16,24},{20,28},{24,16},{28,20},{1,9},{5... | collective-permute-start | bytes 2408456 | tf_op jit(solution)/shard_map/ppermute | solution.py:724
  428.9 17.1 %collective-permute-start.42 = (bf16[8,8,6272]{2,1,0:T(8,128)(2,1)}, bf16[8,8,6272]{2,1,0:T(8,128)(2,1)S(1)}, u32[]{:S(2)}, u32[]{:S(2)}) collective-permute-start(bf16[8,8,6272]{2,1,0:T(8,128)(2,1)} %get-tuple-element.172.refs_2_.refs_14_), channel_id=1, source_target_pairs={{0,1},{1,0},{2,3},{3,2},{4,5},{5,4},{6,7},{7,6},{8,9},{9,8},{10,11... | collective-permute-start | bytes 2408456 | tf_op jit(solution)/shard_map/ppermute | solution.py:724
  428.9 17.6 %collective-permute-start.43 = (bf16[8,8,6272]{2,1,0:T(8,128)(2,1)}, bf16[8,8,6272]{2,1,0:T(8,128)(2,1)S(1)}, u32[]{:S(2)}, u32[]{:S(2)}) collective-permute-start(bf16[8,8,6272]{2,1,0:T(8,128)(2,1)} %get-tuple-element.173.refs_3_), channel_id=1, source_target_pairs={{0,1},{1,0},{2,3},{3,2},{4,5},{5,4},{6,7},{7,6},{8,9},{9,8},{10,11... | collective-permute-start | bytes 2408456 | tf_op jit(solution)/shard_map/ppermute | solution.py:724
  443.9 2.6 collective-permute-start.44
  444.6 2.8 collective-permute-start.45
  446.0 3.6 collective-permute-start.46
  446.0 4.5 collective-permute-start.47
  450.6 11.4 %copy-start.1 = (s32[32,136]{1,0:T(8,128)S(1)}, s32[32,136]{1,0:T(8,128)}, u32[]{:S(2)}) copy-start(s32[32,136]{1,0:T(8,128)} %param.25) | copy-start | bytes 52228
  (49 other events, 155.5 us)
Sparse Core Ops, SparseCore 0:
  252.2 92.8 all-gather.1

commit v3 on v2

--- a/solution.py
+++ b/solution.py
@@ -163,7 +163,7 @@
 
 
 def self_forward(
-    base, count, x_ref, pos_ref, gain_ref, shift_ref, qkv_w, out_w, q_w,
+    base, ready, count, x_ref, pos_ref, gain_ref, shift_ref, qkv_w, out_w, q_w,
     h1_ref, qkv_ref, p_ref, o_ref, x1_ref, h2_ref, q2_ref,
 ):
     step = pl.program_id(0)
@@ -185,6 +185,7 @@
                 i, keys, block(0), block(1), block(2), pos_ref[i], pos_ref[i], p_ref, o_ref
             ),
         )
+    ready()
     x1 = x + mm(rows_of(o_ref).astype(BF16), out_w[...])
     put_rows(x1_ref, x1)
     scaled, _ = norm(x1)
@@ -194,7 +195,7 @@
 
 
 def cross_and_mlp(
-    base, count, other_count, x1_ref, q2_ref, opt_ref, dy_ref, pos_ref, other_pos_ref, gain_ref, shift_ref,
+    base, ready, count, other_count, x1_ref, q2_ref, opt_ref, dy_ref, pos_ref, other_pos_ref, gain_ref, shift_ref,
     kv_w, out_w, in_w, in_b, mo_w, mo_b,
     mixed_ref, kv_ref, p_ref, o_ref, h3_ref, g_ref, du_ref, dm_ref, dx2_ref, sums_ref, in_sums_ref,
 ):
@@ -215,6 +216,7 @@
                 pos_ref[i], other_pos_ref[i], p_ref, o_ref,
             ),
         )
+    ready()
     x2 = rows_of(x1_ref) + mm(rows_of(o_ref).astype(BF16), out_w[...])
     scaled, inverse = norm(x2)
     gain = gain_ref[...].astype(F32)[2:3]
@@ -258,7 +260,7 @@
 
 
 def cross_back(
-    base, other_count, dx2_ref, x1_ref, q2_ref, kv_ref, p_ref, gain_ref, out_w, q_w, kv_w,
+    base, ready, other_count, dx2_ref, x1_ref, q2_ref, kv_ref, p_ref, gain_ref, out_w, q_w, kv_w,
     da2_ref, dq2_ref, dkv_ref, og_ref, dx1_ref, sums_ref, do_ref,
 ):
     step = pl.program_id(0)
@@ -286,6 +288,7 @@
                 p_ref, put(dq2_ref, 0), put(dkv_ref, 0), put(dkv_ref, 1), slots,
             ),
         )
+    ready()
     put_rows(og_ref, mm_t(rows_of(dkv_ref).astype(BF16), kv_w[...]))
     dh2 = mm_t(rows_of(dq2_ref).astype(BF16), q_w[...])
     scaled, inverse = norm(rows_of(x1_ref))
@@ -302,7 +305,7 @@
 
 
 def self_back(
-    base, count, dx1_ref, x_ref, qkv_ref, p_ref, gain_ref, out_w, qkv_w,
+    base, ready, count, dx1_ref, x_ref, qkv_ref, p_ref, gain_ref, out_w, qkv_w,
     dqkv_ref, dx_ref, sums_ref, do_ref,
 ):
     step = pl.program_id(0)
@@ -329,6 +332,7 @@
                 p_ref, put(dqkv_ref, 0), put(dqkv_ref, 1), put(dqkv_ref, 2), slots,
             ),
         )
+    ready()
     dh1 = mm_t(rows_of(dqkv_ref).astype(BF16), qkv_w[...])
     scaled, inverse = norm(rows_of(x_ref))
     put_rows(dx_ref, dx1 + norm_back(dh1, scaled, inverse, gain_ref[...].astype(F32)[0:1]))
@@ -344,12 +348,16 @@
 
 
 def take_images(source, place, *refs):
-    j = pl.program_id(0)
-    for r, ref in enumerate(refs[:-1]):
-
-        @pl.when(source[j] == r)
-        def _(ref=ref):
-            refs[-1][...] = ref[...]
+    out = refs[-1]
+    together = out.shape[0]
+    each = (len(refs) - 1) // together
+    for k in range(together):
+        chosen = source[pl.program_id(0) * together + k]
+        for r in range(each):
+
+            @pl.when(chosen == r)
+            def _(ref=refs[k * each + r], k=k):
+                out[k] = ref[0]
 
 
 def split_first(core, bits, *refs):
@@ -421,7 +429,7 @@
     return waits, through, hand_back
 
 
-def images_call(kernel, scalars, arrays, whole, outs, sums, scratch, flops, name, part=(0, 1), into=None, after=()):
+def images_call(kernel, scalars, arrays, whole, outs, sums, scratch, flops, name, part=(0, 1), into=None, after=(), late=()):
     images = arrays[0].shape[0]
     pair = PAIR if images % PAIR == 0 else 1
     steps = images // pair // part[1]
@@ -444,9 +452,33 @@
     n_outs = len(out_shapes) + len(sum_shapes)
     shapes = out_shapes + sum_shapes + [jax.ShapeDtypeStruct(x.shape, x.dtype) for x in through]
 
+    scratch_shapes = [pltpu.VMEM((pair,) + tail, dtype) for tail, dtype in scratch]
+    scratch_shapes += [pltpu.VMEM(whole[k].shape, whole[k].dtype) for k in late]
+    scratch_shapes += [pltpu.SemaphoreType.DMA((max(1, len(late)),))]
+
     def run(*refs):
-        refs, rest = refs[:n_used], refs[n_used + len(free) :]
-        kernel(first * pair, *refs, *rest[:n_outs], *rest[n_outs + len(through) :])
+        refs, rest = list(refs[:n_used]), refs[n_used + len(free) :]
+        outs_, scratch_ = rest[:n_outs], rest[n_outs + len(through) :]
+        sem, held = scratch_[-1], scratch_[len(scratch) : -1]
+        begin = pl.program_id(0) == 0
+        copies = []
+        for k, (w, inside) in enumerate(zip(late, held)):
+            place = len(scalars) + len(arrays) + w
+            copies.append(pltpu.make_async_copy(refs[place], inside, sem.at[k]))
+            refs[place] = inside
+
+        @pl.when(begin)
+        def _():
+            for copy in copies:
+                copy.start()
+
+        def ready():
+            @pl.when(begin)
+            def _():
+                for copy in copies:
+                    copy.wait()
+
+        kernel(first * pair, ready, *refs, *outs_, *scratch_[: len(scratch)])
 
     aliases = {n_used + len(waits) + k: k for k in range(len(into))}
     aliases |= {n_used + len(waits) + len(into) + k: n_outs + k for k in range(len(through))}
@@ -456,12 +488,14 @@
             num_scalar_prefetch=len(scalars),
             grid=(steps,),
             in_specs=[split_spec(a.shape) for a in arrays]
-            + [whole_spec(a.shape) for a in whole]
+            + [
+                pl.BlockSpec(memory_space=pl.ANY) if k in late else whole_spec(a.shape) for k, a in enumerate(whole)
+            ]
             + [pl.BlockSpec(memory_space=pl.ANY)] * len(free),
             out_specs=[split_spec(o.shape) for o in out_shapes]
             + [pl.BlockSpec(s.shape, lambda i, *_: (0, 0)) for s in sum_shapes]
             + [pl.BlockSpec(memory_space=pl.ANY)] * len(through),
-            scratch_shapes=[pltpu.VMEM((pair,) + tail, dtype) for tail, dtype in scratch],
+            scratch_shapes=scratch_shapes,
         ),
         out_shape=shapes,
         input_output_aliases=aliases,
@@ -475,23 +509,28 @@
 
 def take_call(source, place, sources):
     shape = sources[0].shape
-    block = (1,) + shape[1:]
-
-    def spec(r):
-        return pl.BlockSpec(block, lambda j, source, place: (jnp.where(source[j] == r, place[j], 0), 0, 0))
+    together = TOGETHER if shape[0] % TOGETHER == 0 else 1
+
+    def spec(k, r):
+        def index(j, source, place):
+            image = j * together + k
+            return (jnp.where(source[image] == r, place[image], 0), 0, 0)
+
+        return pl.BlockSpec((1,) + shape[1:], index)
 
     return pl.pallas_call(
         take_images,
         grid_spec=pltpu.PrefetchScalarGridSpec(
             num_scalar_prefetch=2,
-            grid=(shape[0],),
-            in_specs=[spec(r) for r in range(len(sources))],
-            out_specs=pl.BlockSpec(block, lambda j, source, place: (j, 0, 0)),
+            grid=(shape[0] // together,),
+            in_specs=[spec(k, r) for k in range(together) for r in range(len(sources))],
+            out_specs=pl.BlockSpec((together,) + shape[1:], lambda j, source, place: (j, 0, 0)),
         ),
+        compiler_params=pltpu.CompilerParams(vmem_limit_bytes=VMEM_BYTES),
         out_shape=jax.ShapeDtypeStruct(shape, sources[0].dtype),
         cost_estimate=SMALL_COST,
         name="take_images",
-    )(source, place, *sources)
+    )(source, place, *(sources * together))
 
 
 def plain_call(kernel, scalars, grid, ins, outs, name, after=()):
@@ -533,6 +572,7 @@
 
 
 PARTS = 3
+TOGETHER = 4
 
 
 def sum_links(turn):
@@ -796,6 +836,7 @@
         [],
         2 * rows * width * width * 5 + 2 * attention,
         "self_forward",
+        late=(3, 4),
     )
     far, x1 = lax.optimization_barrier((gather_far(optical), x1))
     optical_blocks = gather_near(far)
@@ -823,6 +864,7 @@
         [],
         2 * rows * width * (3 * width + 4 * hidden) + 2 * attention,
         "cross_and_mlp",
+        late=(3, 4, 6),
     )
     first = total_of_pieces((half_of_rows(h3, du), half_of_rows(g, dm)))
     before_cross = next(first)
@@ -842,6 +884,7 @@
         [((slots, width), BF16)],
         2 * rows * width * width * 4 + 4 * attention,
         "cross_back",
+        late=(2, 3),
         after=before_cross,
     )
     second = [
@@ -860,7 +903,7 @@
     made = None
     for part in range(2):
         *made, sums = images_call(
-            self_back, scalars, arrays, whole, outs, [(2, width)], [((slots, width), BF16)], 0, "self_back",
+            self_back, scalars, arrays, whole, outs, [(2, width)], [((slots, width), BF16)], 0, "self_back", late=(2,),
             part=(part, 2), into=made, after=begun + (sum(halves, ()) if part == 0 else ()) + (tuple(og_far[r] for r in og_far if r) if part == 1 else ()),
         )
         sums1 = sums if part == 0 else sums1 + sums

time: 477 us -> 471 us (0.987)
  Pallas kernels: 198 us -> 188 us
    pallas_call x5, Pallas kernels: 134 us -> 129 us  [images_call(): pl.pallas_call(run, grid_spec=pltpu.PrefetchScalarGridSpec(num_scalar_pre...]
  transfers between devices with their start and end apart: 49 -> 49, of which waited for: 24 -> 25; matrix products, arithmetic and copies ran while one was open for 17% -> 17% of each run, Pallas kernels for 27% -> 26%
where the time goes in v3:
time: 471 us; the launch traced here: 464 us
  Pallas kernels  188 us (40%)
  waiting for transfers between devices  123 us (26%)
  matrix products  55.4 us (12%)
  starting transfers between devices  37.4 us (8%)
  other arithmetic  23.2 us (5%)
  local copies, waits for them, and re-layouts  21.8 us (5%)
  between operations  15 us (3%)
    pallas_call x5, Pallas kernels, images_call(): pl.pallas_call(run, grid_spec=pltpu.PrefetchScalarGridSpec(num_scalar_pre...  129 us
    ppermute x48, waiting for transfers between devices, flip(): return lax.ppermute(values, axis_name, [(i, i ^ bit) for i in range(size)])  123 us
    dot_general x14, matrix products, row_product(): lax.dot_general(left.reshape(-1, left.shape[-1]), right.reshape(-1, right...  55.4 us
    pallas_call x9, Pallas kernels, plain_call(): pl.pallas_call(run, grid_spec=pltpu.PrefetchScalarGridSpec(num_scalar_pre...  40.5 us
    ppermute x48, starting transfers between devices, flip(): return lax.ppermute(values, axis_name, [(i, i ^ bit) for i in range(size)])  37.3 us
    unnamed x130, local copies, waits for them, and re-layouts  10.2 us
    pallas_call x2, Pallas kernels, take_call(): pl.pallas_call(take_images, grid_spec=pltpu.PrefetchScalarGridSpec(num_sc...  9.59 us
    pallas_call x1, Pallas kernels, total_of_pieces(): pl.pallas_call(take_own, grid=(count // chunk,), in_specs=[pl.BlockSpec((...  9.55 us
  transfers between devices with their start and end apart: 49, of which 25 were waited for; matrix products, arithmetic and copies ran while one was open for 17% of the time, Pallas kernels for 26%

profile of v3, /device:TPU:0, one launch (start us, length us, event | category | flops | bytes accessed | tf_op | source)
XLA Modules:
  0.0 464.2 jit_solution(5080089665704354641)
XLA Ops:
  7.2 3.0 collective-permute-start
  13.2 24.3 %self_forward.1 = (bf16[8,136,768]{2,1,0:T(8,128)(2,1)}, bf16[8,136,2304]{2,1,0:T(8,128)(2,1)}, bf16[8,136,3072]{2,1,0:T(8,128)(2,1)}, bf16[8,136,768]{2,1,0:T(8...) custom-call(s32[8]{0:T(128)} %copy-done.49, ...), custom_call_target="tpu_custom_call" | custom-call | flops 1 | bytes 1 | tf_op jit(solution)/shard_map/self_forward/pallas_call | solution.py:485
  37.5 9.6 %collective-permute-done.refs_2_.refs_6_.refs_10_.refs_14_ = bf16[8,136,768]{2,1,0:T(8,128)(2,1)} collective-permute-done((bf16[8,136,768]{2,1,0:T(8,128)(2,1)}, bf16[8,136,768]{2,1,0:T(8,128)(2,1)}, u32[]{:S(2)}, u32[]{:S(2)}) %collective-permute-start) | collective-permute-done | bytes 1671200 | tf_op jit(solution)/shard_map/ppermute | solution.py:764
  53.4 4.8 %take_images.2.refs_4_ = bf16[8,136,768]{2,1,0:T(8,128)(2,1)} custom-call(s32[8]{0:T(128)} %get-tuple-element.209.source, s32[8]{0:T(128)} %get-tuple-element.184.place, bf16[8,136,768]{2,1,0:T(8,128)(2,1)} %refs_12_.1, bf16[8,136,768]{2,1,0:T(8,128)(2,1)} %collective-permute-done.1.refs_1_.refs_5_.refs_9_.refs_13_, ...), custom_call_target="tpu_custom_call" | custom-call | flops 1 | bytes 1 | tf_op jit(solution)/shard_map/take_images/pallas_call | solution.py:521
  58.2 51.5 %cross_and_mlp.1 = (bf16[8,136,768]{2,1,0:T(8,128)(2,1)}, bf16[8,136,1536]{2,1,0:T(8,128)(2,1)}, bf16[8,136,3072]{2,1,0:T(8,128)(2,1)}, bf16[8,136,768]{2,1,0:T(...) custom-call(s32[8]{0:T(128)} %copy-done.49, ...), custom_call_target="tpu_custom_call" | custom-call | flops 1 | bytes 1 | tf_op jit(solution)/shard_map/cross_and_mlp/pallas_call | solution.py:485
  109.7 7.2 %convolution_convert_fusion.3 = bf16[1536,768]{1,0:T(8,128)(2,1)} fusion(bf16[1088,768]{1,0:T(8,128)(2,1)} %bitcast.98, bf16[1088,3072]{1,0:T(8,128)(2,1)} %bitcast.89, s32[]{:T(128)S(6)} %select_n.280), kind=kOutput, calls=%fused_computation.7 | convolution fusion | flops 2568093696 | bytes 7372804 | tf_op jit(solution)/shard_map/dot_general | solution.py:785
  116.9 7.6 %convolution_convert_fusion.2 = bf16[384,3072]{1,0:T(8,128)(2,1)} fusion(bf16[1088,3072]{1,0:T(8,128)(2,1)} %bitcast.60, bf16[1088,768]{1,0:T(8,128)(2,1)S(1)} %bitcast.83, s32[]{:T(128)S(6)} %select_n.276), kind=kOutput, calls=%fused_computation.6 | convolution fusion | flops 2568093696 | bytes 9879556 | tf_op jit(solution)/shard_map/dot_general | solution.py:785
  125.0 6.6 %add_convert_fusion = bf16[1536,768]{1,0:T(8,128)(2,1)S(1)} fusion(bf16[1536,768]{1,0:T(8,128)(2,1)} %collective-permute-done.4, bf16[1088,768]{1,0:T(8,128)(2,1)} %bitcast.99, bf16[1088,3072]{1,0:T(8,128)(2,1)} %bitcast.90, s32[]{:T(128)S(6)} %select_n.279), kind=kOutput, calls=%fused_computation.2 | convolution fusion | flops 2570452992 | bytes 9732100 | tf_op jit(solution)/shard_map/dot_general | solution.py:785
  131.6 1.6 constant_dynamic-slice_fusion.10
  133.2 1.5 collective-permute-start.6
  134.8 4.8 %add_convert_fusion.1 = bf16[384,3072]{1,0:T(8,128)(2,1)S(1)} fusion(bf16[384,3072]{1,0:T(8,128)(2,1)} %collective-permute-done.3, bf16[1088,3072]{1,0:T(8,128)(2,1)S(1)} %bitcast.63, bf16[1088,768]{1,0:T(8,128)(2,1)S(1)} %bitcast.84, s32[]{:T(128)S(6)} %select_n.275), kind=kOutput, calls=%fused_computation.3 | convolution fusion | flops 2570452992 | bytes 12238852 | tf_op jit(solution)/shard_map/dot_general | solution.py:785
  139.6 1.2 constant_dynamic-slice_fusion.11
  140.8 2.0 collective-permute-start.5
  142.8 24.4 %cross_back.1 = (bf16[8,136,768]{2,1,0:T(8,128)(2,1)}, bf16[8,136,768]{2,1,0:T(8,128)(2,1)}, bf16[8,136,1536]{2,1,0:T(8,128)(2,1)}, bf16[8,136,768]{2,1,0:T(8,12...) custom-call(s32[8]{0:T(128)} %copy-done.52, ...), custom_call_target="tpu_custom_call", output_to_operand_aliasing={{6}: (12, {}), {7}: (13, {})} | custom-call | flops 1 | bytes 1 | tf_op jit(solution)/shard_map/cross_back/pallas_call | solution.py:485
  167.2 2.2 convert_element_type.176
  169.7 1.8 convolution_convert_fusion.6.refs_17_.refs_8_.refs_20_.refs_32_.refs_44_.refs_56_.refs_68_
  171.5 1.8 convolution_convert_fusion.7.refs_16_
  174.3 2.7 convolution_convert_fusion.4.refs_15_.refs_6_.refs_18_.refs_30_.refs_42_.refs_54_.refs_66_
  177.0 1.8 convolution_convert_fusion.8.refs_13_.refs_4_.refs_16_.refs_28_.refs_40_.refs_52_.refs_64_
  178.9 1.9 convolution_convert_fusion.9.refs_12_
  180.7 1.8 convolution_convert_fusion.10.refs_11_.refs_2_.refs_14_.refs_26_.refs_38_.refs_50_.refs_62_
  182.5 2.7 convolution_convert_fusion.5.refs_14_
  185.3 1.6 add_convert_fusion.2
  188.0 2.9 collective-permute-start.8
  190.9 1.7 add_convert_fusion.3
  194.7 1.8 convolution_convert_fusion.11.refs_10_
  196.5 14.1 %self_back.2 = (bf16[8,136,2304]{2,1,0:T(8,128)(2,1)}, bf16[8,136,768]{2,1,0:T(8,128)(2,1)}, f32[2,768]{1,0:T(2,128)}, bf16[2,2,1,1,24,3072]{5,4,3,2,1,0:T(8,128)(2,1)}, bf16[2,1,1,2,96,768]{5,4,3,2,1,0:T(8,128)(2,1)}) custom-call(s32[8]{0:T(128)} %copy-done.49, ...), custom_call_target="tpu_custom_call", output_to_operand_aliasing={{3}: (18, {}), {4}: (19, {})} | custom-call | flops 1 | bytes 1 | tf_op jit(solution)/shard_map/self_back/pallas_call | solution.py:485
  210.6 1.4 add_convert_fusion.4
  212.8 2.4 collective-permute-start.19
  218.5 14.4 %self_back.3 = (bf16[8,136,2304]{2,1,0:T(8,128)(2,1)}, bf16[8,136,768]{2,1,0:T(8,128)(2,1)}, f32[2,768]{1,0:T(2,128)}, bf16[2,1,1,1,24,3072]{5,4,3,2,1,0:T(8,128)(2,1)}, bf16[1,1,1,2,96,768]{5,4,3,2,1,0:T(8,128)(2,1)}) custom-call(s32[8]{0:T(128)} %copy-done.49, ...), custom_call_target="tpu_custom_call", output_to_operand_aliasing={{0}: (11, {}), {1}: (12, {}), {3}: (13, {}), {4}: (14, {})} | custom-call | flops 1 | bytes 1 | tf_op jit(solution)/shard_map/self_back/pallas_call | solution.py:485
  236.4 3.3 collective-permute-done.38
  239.9 5.5 %collective-permute-done.37 = bf16[1,1,1,1,24,3072]{5,4,3,2,1,0:T(8,128)(2,1)S(1)} collective-permute-done((bf16[1,1,1,1,24,3072]{5,4,3,2,1,0:T(8,128)(2,1)S(1)}, bf16[1,1,1,1,24,3072]{5,4,3,2,1,0:T(8,128)(2,1)S(1)}, u32[]{:S(2)}, u32[]{:S(2)}) %collective-permute-start.37) | collective-permute-done | bytes 147488 | tf_op jit(solution)/shard_map/ppermute | solution.py:764
  246.3 6.4 %convolution_convert_fusion = bf16[384,2304]{1,0:T(8,128)(2,1)} fusion(bf16[1088,2304]{1,0:T(8,128)(2,1)} %bitcast.70, bf16[1088,768]{1,0:T(8,128)(2,1)} %bitcast.96, s32[]{:T(128)S(6)} %select_n.276), kind=kOutput, calls=%fused_computation.4 | convolution fusion | flops 1926070272 | bytes 7618564 | tf_op jit(solution)/shard_map/dot_general | solution.py:785
  254.5 3.6 collective-permute-done.15.refs_9_.refs_21_.refs_33_.refs_45_.refs_57_.refs_69_
  258.5 1.3 collective-permute-done.13.refs_5_.refs_17_.refs_29_.refs_41_.refs_53_.refs_65_
  261.2 6.4 %convolution_convert_fusion.1.refs_10_.refs_22_.refs_34_.refs_46_.refs_58_.refs_70_ = bf16[384,2304]{1,0:T(8,128)(2,1)} fusion(bf16[1088,2304]{1,0:T(8,128)(2,1)} %bitcast.71, bf16[1088,768]{1,0:T(8,128)(2,1)} %bitcast.97, s32[]{:T(128)S(6)} %select_n.275), kind=kOutput, calls=%fused_computation.5 | convolution fusion | flops 1926070272 | bytes 7618564 | tf_op jit(solution)/shard_map/dot_general | solution.py:785
  269.3 9.4 %split_first.1 = (bf16[8,8,6272]{2,1,0:T(8,128)(2,1)}, bf16[8,8,6272]{2,1,0:T(8,128)(2,1)}, bf16[8,8,6272]{2,1,0:T(8,128)(2,1)}, bf16[8,8,6272]{2,1,0:T(8,128)(2...) custom-call(s32[1]{0:T(128)} %bitcast.18.refs_0_, s32[3]{0:T(128)} %pad_add_fusion.refs_1_, ...), custom_call_target="tpu_custom_call" | custom-call | flops 1 | bytes 1 | tf_op jit(solution)/shard_map/split_first/pallas_call | solution.py:545
  280.5 1.6 sort.17
  283.9 4.8 %take_images.3.refs_14_ = bf16[8,136,768]{2,1,0:T(8,128)(2,1)} custom-call(s32[8]{0:T(128)} %fusion.39.source, s32[8]{0:T(128)} %get-tuple-element.182.place, bf16[8,136,768]{2,1,0:T(8,128)(2,1)} %get-tuple-element.124.refs_0_.refs_4_.refs_8_.refs_12_, bf16[8,136,768]{2,1,0:T(8,128)(2,1)} %collective-permute-done.10.refs_1_.refs_5_.refs_9_.refs_13_, ...), custom_call_target="tpu_custom_call" | custom-call | flops 1 | bytes 1 | tf_op jit(solution)/shard_map/take_images/pallas_call | solution.py:521
  288.7 10.4 %collective-permute-done.20.refs_7_.refs_10_ = bf16[8,8,6272]{2,1,0:T(8,128)(2,1)S(1)} collective-permute-done((bf16[8,8,6272]{2,1,0:T(8,128)(2,1)}, bf16[8,8,6272]{2,1,0:T(8,128)(2,1)S(1)}, u32[]{:S(2)}, u32[]{:S(2)}) %collective-permute-start.20) | collective-permute-done | bytes 802848 | tf_op jit(solution)/shard_map/ppermute | solution.py:764
  300.0 15.0 %collective-permute-done.22.refs_9_.refs_12_ = bf16[8,8,6272]{2,1,0:T(8,128)(2,1)S(1)} collective-permute-done((bf16[8,8,6272]{2,1,0:T(8,128)(2,1)}, bf16[8,8,6272]{2,1,0:T(8,128)(2,1)S(1)}, u32[]{:S(2)}, u32[]{:S(2)}) %collective-permute-start.22) | collective-permute-done | bytes 802848 | tf_op jit(solution)/shard_map/ppermute | solution.py:764
  315.9 4.6 add_blocks.4
  320.6 3.5 collective-permute-start.25
  324.7 5.6 %collective-permute-done.23.refs_7_.refs_10_ = bf16[4,8,6272]{2,1,0:T(8,128)(2,1)S(1)} collective-permute-done((bf16[4,8,6272]{2,1,0:T(8,128)(2,1)}, bf16[4,8,6272]{2,1,0:T(8,128)(2,1)S(1)}, u32[]{:S(2)}, u32[]{:S(2)}) %collective-permute-start.23) | collective-permute-done | bytes 401440 | tf_op jit(solution)/shard_map/ppermute | solution.py:764
  330.3 9.2 %collective-permute-done.24.refs_8_.refs_11_ = bf16[4,8,6272]{2,1,0:T(8,128)(2,1)S(1)} collective-permute-done((bf16[4,8,6272]{2,1,0:T(8,128)(2,1)}, bf16[4,8,6272]{2,1,0:T(8,128)(2,1)S(1)}, u32[]{:S(2)}, u32[]{:S(2)}) %collective-permute-start.24) | collective-permute-done | bytes 401440 | tf_op jit(solution)/shard_map/ppermute | solution.py:764
  340.4 3.4 add_blocks.5
  344.2 1.5 collective-permute-start.27
  346.4 3.7 collective-permute-done.26.refs_7_.refs_10_
  350.2 1.4 collective-permute-done.28.refs_9_.refs_12_
  352.3 2.8 add_blocks.6
  356.2 1.8 collective-permute-start.29
  358.0 11.5 %collective-permute-done.29.refs_4_.refs_5_.refs_6_ = bf16[3,8,6272]{2,1,0:T(8,128)(2,1)S(1)} collective-permute-done((bf16[3,8,6272]{2,1,0:T(8,128)(2,1)S(1)}, bf16[3,8,6272]{2,1,0:T(8,128)(2,1)S(1)}, u32[]{:S(2)}, u32[]{:S(2)}) %collective-permute-start.29) | collective-permute-done | bytes 301088 | tf_op jit(solution)/shard_map/ppermute | solution.py:764
  370.2 1.9 add_blocks.7
  373.2 14.5 %collective-permute-done.30.refs_4_.refs_5_.refs_6_ = bf16[3,8,6272]{2,1,0:T(8,128)(2,1)S(1)} collective-permute-done((bf16[3,8,6272]{2,1,0:T(8,128)(2,1)S(1)}, bf16[3,8,6272]{2,1,0:T(8,128)(2,1)S(1)}, u32[]{:S(2)}, u32[]{:S(2)}) %collective-permute-start.30) | collective-permute-done | bytes 301088 | tf_op jit(solution)/shard_map/ppermute | solution.py:764
  388.4 2.7 merge_blocks.3
  393.0 5.1 %collective-permute-done.31.refs_4_ = bf16[2,8,6272]{2,1,0:T(8,128)(2,1)S(1)} collective-permute-done((bf16[2,8,6272]{2,1,0:T(8,128)(2,1)}, bf16[2,8,6272]{2,1,0:T(8,128)(2,1)S(1)}, u32[]{:S(2)}, u32[]{:S(2)}) %collective-permute-start.31) | collective-permute-done | bytes 200736 | tf_op jit(solution)/shard_map/ppermute | solution.py:764
  399.8 3.3 merge_blocks.4
  403.9 1.7 collective-permute-start.35
  406.6 9.6 %take_own.1 = (bf16[32,24,3072]{2,1,0:T(8,128)(2,1)}, bf16[32,4,24,768]{3,2,1,0:T(8,128)(2,1)}) custom-call(bf16[32,2,24,3072]{3,2,1,0:T(8,128)(2,1)} %all-gather.2.cloned.1.call-done.refs_every), custom_call_target="tpu_custom_call" | custom-call | flops 1 | bytes 1 | tf_op jit(solution)/shard_map/take_own/pallas_call | solution.py:633
  417.1 3.8 merge_blocks.5
  422.0 1.2 collective-permute-start.40
  424.1 14.8 %collective-permute-done.39.refs_5_ = bf16[8,8,6272]{2,1,0:T(8,128)(2,1)S(1)} collective-permute-done((bf16[8,8,6272]{2,1,0:T(8,128)(2,1)}, bf16[8,8,6272]{2,1,0:T(8,128)(2,1)S(1)}, u32[]{:S(2)}, u32[]{:S(2)}) %collective-permute-start.39) | collective-permute-done | bytes 802848 | tf_op jit(solution)/shard_map/ppermute | solution.py:764
  442.4 2.3 collective-permute-done.46.refs_12_
  445.7 8.5 %unpack_blocks.1 = (bf16[2,3,2,8,8,768]{5,4,3,2,1,0:T(8,128)(2,1)}, bf16[2,3,2,8,8,768]{5,4,3,2,1,0:T(8,128)(2,1)}, bf16[2,3,2,8,8,1536]{5,4,3,2,1,0:T(8,128)(2,...) custom-call(s32[1]{0:T(128)} %bitcast.18.refs_0_, ...), custom_call_target="tpu_custom_call" | custom-call | flops 1 | bytes 1 | tf_op jit(solution)/shard_map/unpack_blocks/pallas_call | solution.py:545
  (257 shorter events, 55.6 us)
Async XLA Ops:
  7.2 41.6 %copy-start = (s32[32,136]{1,0:T(8,128)S(1)}, s32[32,136]{1,0:T(8,128)}, u32[]{:S(2)}) copy-start(s32[32,136]{1,0:T(8,128)} %param.25) | copy-start | bytes 52228
  7.2 399.4 %all-gather.2.cloned.1.call-start = ((), (), s32[]{:S(2)}) async-start(), calls=%async_computation | async-start | bytes 9732096 | tf_op jit(solution)/shard_map/all_gather | solution.py:627
  7.2 39.9 %collective-permute-start = (bf16[8,136,768]{2,1,0:T(8,128)(2,1)}, bf16[8,136,768]{2,1,0:T(8,128)(2,1)}, u32[]{:S(2)}, u32[]{:S(2)}) collective-permute-start(bf16[8,136,768]{2,1,0:T(8,128)(2,1)} %refs_12_.1), channel_id=1, source_target_pairs={{0,2},{2,0},{1,3},{3,1},{4,6},{6,4},{5,7},{7,5},{8,10},{10,8},{9,1... | collective-permute-start | bytes 5013512 | tf_op jit(solution)/shard_map/ppermute | solution.py:764
  13.2 33.9 %copy-start.5 = (bf16[8,136,768]{2,1,0:T(8,128)(2,1)S(1)}, bf16[8,136,768]{2,1,0:T(8,128)(2,1)}, u32[]{:S(2)}) copy-start(bf16[8,136,768]{2,1,0:T(8,128)(2,1)} %refs_12_.1) | copy-start | bytes 5013508
  13.2 34.5 %copy-start.58 = (s32[32]{0:T(128)S(1)}, s32[32]{0:T(128)}, u32[]{:S(2)}) copy-start(s32[32]{0:T(128)} %param.26) | copy-start | bytes 388
  13.2 36.2 %copy-start.61 = (s32[32]{0:T(128)S(1)}, s32[32]{0:T(128)}, u32[]{:S(2)}) copy-start(s32[32]{0:T(128)} %param.23) | copy-start | bytes 388
  13.2 36.9 %copy-start.54 = (bf16[3072]{0:T(1024)(128)(2,1)S(1)}, bf16[3072]{0:T(1024)(128)(2,1)}, u32[]{:S(2)}) copy-start(bf16[3072]{0:T(1024)(128)(2,1)} %param.35) | copy-start | bytes 18436
  13.2 37.5 %copy-start.57 = (bf16[768]{0:T(1024)(128)(2,1)S(1)}, bf16[768]{0:T(1024)(128)(2,1)}, u32[]{:S(2)}) copy-start(bf16[768]{0:T(1024)(128)(2,1)} %param.37) | copy-start | bytes 4612
  47.1 6.0 %collective-permute-start.1 = (bf16[8,136,768]{2,1,0:T(8,128)(2,1)S(1)}, bf16[8,136,768]{2,1,0:T(8,128)(2,1)}, u32[]{:S(2)}, u32[]{:S(2)}) collective-permute-start(bf16[8,136,768]{2,1,0:T(8,128)(2,1)S(1)} %copy-done.5), channel_id=1, source_target_pairs={{0,1},{1,0},{2,3},{3,2},{4,5},{5,4},{6,7},{7,6},{8,9},{9,8},{10,11... | collective-permute-start | bytes 5013512 | tf_op jit(solution)/shard_map/ppermute | solution.py:764
  47.1 6.3 %collective-permute-start.2 = (bf16[8,136,768]{2,1,0:T(8,128)(2,1)}, bf16[8,136,768]{2,1,0:T(8,128)(2,1)}, u32[]{:S(2)}, u32[]{:S(2)}) collective-permute-start(bf16[8,136,768]{2,1,0:T(8,128)(2,1)} %collective-permute-done.refs_2_.refs_6_.refs_10_.refs_14_), channel_id=1, source_target_pairs={{0,1},{1,0},{2,3},{3,2},{4,5},{5,4},{6,7},{7,6},{8,9},{9,8},{10,11... | collective-permute-start | bytes 5013512 | tf_op jit(solution)/shard_map/ppermute | solution.py:764
  116.9 8.1 %collective-permute-start.4 = (bf16[1536,768]{1,0:T(8,128)(2,1)}, bf16[1536,768]{1,0:T(8,128)(2,1)}, u32[]{:S(2)}, u32[]{:S(2)}) collective-permute-start(bf16[1536,768]{1,0:T(8,128)(2,1)} %convolution_convert_fusion.3), channel_id=1, source_target_pairs={{0,1},{1,0},{2,3},{3,2},{4,5},{5,4},{6,7},{7,6},{8,9},{9,8},{10,11... | collective-permute-start | bytes 7077896 | tf_op jit(solution)/shard_map/ppermute | solution.py:764
  124.5 10.2 %collective-permute-start.3 = (bf16[384,3072]{1,0:T(8,128)(2,1)}, bf16[384,3072]{1,0:T(8,128)(2,1)}, u32[]{:S(2)}, u32[]{:S(2)}) collective-permute-start(bf16[384,3072]{1,0:T(8,128)(2,1)} %convolution_convert_fusion.2), channel_id=1, source_target_pairs={{0,1},{1,0},{2,3},{3,2},{4,5},{5,4},{6,7},{7,6},{8,9},{9,8},{10,11... | collective-permute-start | bytes 7077896 | tf_op jit(solution)/shard_map/ppermute | solution.py:764
  125.0 9.8 %slice-start.1 = ((s8[6684672]{0:T(1024)(128)(4,1)}), s8[4194304]{0:T(1024)(128)(4,1)S(1)}, s32[]{:S(2)}) async-start(s8[6684672]{0:T(1024)(128)(4,1)} %bitcast.61), calls=%async_computation.2 | async-start | bytes 8388608
  133.2 52.0 %collective-permute-start.6 = (bf16[2,2,1,2,96,768]{5,4,3,2,1,0:T(8,128)(2,1)}, bf16[2,2,1,2,96,768]{5,4,3,2,1,0:T(8,128)(2,1)}, u32[]{:S(2)}, u32[]{:S(2)}) collective-permute-start(bf16[2,2,1,2,96,768]{5,4,3,2,1,0:T(8,128)(2,1)} %get-tuple-element.187.refs_11_), channel_id=1, source_target_pairs={{0,4},{4,0},{8,12},{12,8},{16,20},{20,16},{24,28},{28,24},{1,5},{5... | collective-permute-start | bytes 3538952 | tf_op jit(solution)/shard_map/ppermute | solution.py:764
  140.8 50.1 %collective-permute-start.5 = (bf16[2,2,2,1,24,3072]{5,4,3,2,1,0:T(8,128)(2,1)S(1)}, bf16[2,2,2,1,24,3072]{5,4,3,2,1,0:T(8,128)(2,1)}, u32[]{:S(2)}, u32[]{:S(2)}) collective-permute-start(bf16[2,2,2,1,24,3072]{5,4,3,2,1,0:T(8,128)(2,1)S(1)} %get-tuple-element.189.refs_10_), channel_id=1, source_target_pairs={{0,2},{2,0},{1,3},{3,1},{4,6},{6,4},{5,7},{7,5},{8,10},{10,8},{9,1... | collective-permute-start | bytes 3538952 | tf_op jit(solution)/shard_map/ppermute | solution.py:764
  173.3 43.9 %collective-permute-start.9 = (bf16[8,136,768]{2,1,0:T(8,128)(2,1)}, bf16[8,136,768]{2,1,0:T(8,128)(2,1)S(1)}, u32[]{:S(2)}, u32[]{:S(2)}) collective-permute-start(bf16[8,136,768]{2,1,0:T(8,128)(2,1)} %get-tuple-element.124.refs_0_.refs_4_.refs_8_.refs_12_), channel_id=1, source_target_pairs={{0,2},{2,0},{1,3},{3,1},{4,6},{6,4},{5,7},{7,5},{8,10},{10,8},{9,1... | collective-permute-start | bytes 5013512 | tf_op jit(solution)/shard_map/ppermute | solution.py:764
  188.0 22.6 %collective-permute-start.8 = (bf16[2,1,1,2,96,768]{5,4,3,2,1,0:T(8,128)(2,1)}, bf16[2,1,1,2,96,768]{5,4,3,2,1,0:T(8,128)(2,1)}, u32[]{:S(2)}, u32[]{:S(2)}) collective-permute-start(bf16[2,1,1,2,96,768]{5,4,3,2,1,0:T(8,128)(2,1)} %get-tuple-element.191.refs_9_), channel_id=1, source_target_pairs={{0,8},{4,12},{8,0},{12,4},{16,24},{20,28},{24,16},{28,20},{1,9},{5... | collective-permute-start | bytes 1769480 | tf_op jit(solution)/shard_map/ppermute | solution.py:764
  193.5 21.7 %collective-permute-start.7 = (bf16[2,2,1,1,24,3072]{5,4,3,2,1,0:T(8,128)(2,1)S(1)}, bf16[2,2,1,1,24,3072]{5,4,3,2,1,0:T(8,128)(2,1)}, u32[]{:S(2)}, u32[]{:S(2)}) collective-permute-start(bf16[2,2,1,1,24,3072]{5,4,3,2,1,0:T(8,128)(2,1)S(1)} %get-tuple-element.193.refs_8_), channel_id=1, source_target_pairs={{0,4},{4,0},{8,12},{12,8},{16,20},{20,16},{24,28},{28,24},{1,5},{5... | collective-permute-start | bytes 1769480 | tf_op jit(solution)/shard_map/ppermute | solution.py:764
  212.8 20.1 %collective-permute-start.19 = (bf16[1,1,1,2,96,768]{5,4,3,2,1,0:T(8,128)(2,1)S(1)}, bf16[1,1,1,2,96,768]{5,4,3,2,1,0:T(8,128)(2,1)S(1)}, u32[]{:S(2)}, u32[]{:S(2)}) collective-permute-start(bf16[1,1,1,2,96,768]{5,4,3,2,1,0:T(8,128)(2,1)S(1)} %get-tuple-element.195.refs_9_), channel_id=1, source_target_pairs={{0,16},{4,20},{8,24},{12,28},{16,0},{20,4},{24,8},{28,12},{1,17},{... | collective-permute-start | bytes 884744 | tf_op jit(solution)/shard_map/ppermute | solution.py:764
  217.2 17.7 %collective-permute-start.18 = (bf16[2,1,1,1,24,3072]{5,4,3,2,1,0:T(8,128)(2,1)S(1)}, bf16[2,1,1,1,24,3072]{5,4,3,2,1,0:T(8,128)(2,1)S(1)}, u32[]{:S(2)}, u32[]{:S(2)}) collective-permute-start(bf16[2,1,1,1,24,3072]{5,4,3,2,1,0:T(8,128)(2,1)S(1)} %get-tuple-element.197.refs_8_), channel_id=1, source_target_pairs={{0,8},{4,12},{8,0},{12,4},{16,24},{20,28},{24,16},{28,20},{1,9},{5... | collective-permute-start | bytes 884744 | tf_op jit(solution)/shard_map/ppermute | solution.py:764
  234.0 12.3 %copy-start.39 = (bf16[1,1,1,1,96,768]{5,4,3,2,1,0:T(8,128)(2,1)}, bf16[1,1,1,1,96,768]{5,4,3,2,1,0:T(8,128)(2,1)S(1)}, u32[]{:S(2)}) copy-start(bf16[1,1,1,1,96,768]{5,4,3,2,1,0:T(8,128)(2,1)S(1)} %constant_dynamic-slice_fusion.refs_75_) | copy-start | bytes 442372
  234.0 5.7 %collective-permute-start.38 = (bf16[1,1,1,1,96,768]{5,4,3,2,1,0:T(8,128)(2,1)S(1)}, bf16[1,1,1,1,96,768]{5,4,3,2,1,0:T(8,128)(2,1)S(1)}, u32[]{:S(2)}, u32[]{:S(2)}) collective-permute-start(bf16[1,1,1,1,96,768]{5,4,3,2,1,0:T(8,128)(2,1)S(1)} %constant_dynamic-slice_fusion.refs_75_), channel_id=1, source_target_pairs={{0,2},{2,0},{1,3},{3,1},{4,6},{6,4},{5,7},{7,5},{8,10},{10,8},{9,1... | collective-permute-start | bytes 442376 | tf_op jit(solution)/shard_map/ppermute | solution.py:764
  236.0 10.3 %copy-start.40 = (bf16[1,1,1,1,24,3072]{5,4,3,2,1,0:T(8,128)(2,1)}, bf16[1,1,1,1,24,3072]{5,4,3,2,1,0:T(8,128)(2,1)S(1)}, u32[]{:S(2)}) copy-start(bf16[1,1,1,1,24,3072]{5,4,3,2,1,0:T(8,128)(2,1)S(1)} %constant_dynamic-slice_fusion.1.refs_74_) | copy-start | bytes 442372
  236.0 9.5 %collective-permute-start.37 = (bf16[1,1,1,1,24,3072]{5,4,3,2,1,0:T(8,128)(2,1)S(1)}, bf16[1,1,1,1,24,3072]{5,4,3,2,1,0:T(8,128)(2,1)S(1)}, u32[]{:S(2)}, u32[]{:S(2)}) collective-permute-start(bf16[1,1,1,1,24,3072]{5,4,3,2,1,0:T(8,128)(2,1)S(1)} %constant_dynamic-slice_fusion.1.refs_74_), channel_id=1, source_target_pairs={{0,16},{4,20},{8,24},{12,28},{16,0},{20,4},{24,8},{28,12},{1,17},{... | collective-permute-start | bytes 442376 | tf_op jit(solution)/shard_map/ppermute | solution.py:764
  246.3 13.8 %copy-start.55 = (f32[2,768]{1,0:T(2,128)S(1)}, f32[2,768]{1,0:T(2,128)}, u32[]{:S(2)}) copy-start(f32[2,768]{1,0:T(2,128)} %get-tuple-element.131) | copy-start | bytes 18436
  246.3 13.8 %copy-start.56 = (f32[2,768]{1,0:T(2,128)S(1)}, f32[2,768]{1,0:T(2,128)}, u32[]{:S(2)}) copy-start(f32[2,768]{1,0:T(2,128)} %get-tuple-element.132) | copy-start | bytes 18436
  252.8 14.9 %collective-permute-start.16 = (bf16[384,2304]{1,0:T(8,128)(2,1)}, bf16[384,2304]{1,0:T(8,128)(2,1)S(1)}, u32[]{:S(2)}, u32[]{:S(2)}) collective-permute-start(bf16[384,2304]{1,0:T(8,128)(2,1)} %convolution_convert_fusion), channel_id=1, source_target_pairs={{0,1},{1,0},{2,3},{3,2},{4,5},{5,4},{6,7},{7,6},{8,9},{9,8},{10,11... | collective-permute-start | bytes 5308424 | tf_op jit(solution)/shard_map/ppermute | solution.py:764
  252.8 5.3 %collective-permute-start.15 = (bf16[384,768]{1,0:T(8,128)(2,1)}, bf16[384,768]{1,0:T(8,128)(2,1)}, u32[]{:S(2)}, u32[]{:S(2)}) collective-permute-start(bf16[384,768]{1,0:T(8,128)(2,1)} %convolution_convert_fusion.7.refs_16_), channel_id=1, source_target_pairs={{0,1},{1,0},{2,3},{3,2},{4,5},{5,4},{6,7},{7,6},{8,9},{9,8},{10,11... | collective-permute-start | bytes 1769480 | tf_op jit(solution)/shard_map/ppermute | solution.py:764
  253.3 6.5 %collective-permute-start.13 = (bf16[384,768]{1,0:T(8,128)(2,1)}, bf16[384,768]{1,0:T(8,128)(2,1)}, u32[]{:S(2)}, u32[]{:S(2)}) collective-permute-start(bf16[384,768]{1,0:T(8,128)(2,1)} %convolution_convert_fusion.9.refs_12_), channel_id=1, source_target_pairs={{0,1},{1,0},{2,3},{3,2},{4,5},{5,4},{6,7},{7,6},{8,9},{9,8},{10,11... | collective-permute-start | bytes 1769480 | tf_op jit(solution)/shard_map/ppermute | solution.py:764
  253.3 14.4 %collective-permute-start.14 = (bf16[384,1536]{1,0:T(8,128)(2,1)}, bf16[384,1536]{1,0:T(8,128)(2,1)S(1)}, u32[]{:S(2)}, u32[]{:S(2)}) collective-permute-start(bf16[384,1536]{1,0:T(8,128)(2,1)} %convolution_convert_fusion.5.refs_14_), channel_id=1, source_target_pairs={{0,1},{1,0},{2,3},{3,2},{4,5},{5,4},{6,7},{7,6},{8,9},{9,8},{10,11... | collective-permute-start | bytes 3538952 | tf_op jit(solution)/shard_map/ppermute | solution.py:764
  253.8 7.3 %collective-permute-start.12 = (bf16[384,768]{1,0:T(8,128)(2,1)}, bf16[384,768]{1,0:T(8,128)(2,1)}, u32[]{:S(2)}, u32[]{:S(2)}) collective-permute-start(bf16[384,768]{1,0:T(8,128)(2,1)} %convolution_convert_fusion.11.refs_10_), channel_id=1, source_target_pairs={{0,1},{1,0},{2,3},{3,2},{4,5},{5,4},{6,7},{7,6},{8,9},{9,8},{10,11... | collective-permute-start | bytes 1769480 | tf_op jit(solution)/shard_map/ppermute | solution.py:764
  258.1 25.8 %collective-permute-start.10 = (bf16[8,136,768]{2,1,0:T(8,128)(2,1)}, bf16[8,136,768]{2,1,0:T(8,128)(2,1)}, u32[]{:S(2)}, u32[]{:S(2)}) collective-permute-start(bf16[8,136,768]{2,1,0:T(8,128)(2,1)} %get-tuple-element.124.refs_0_.refs_4_.refs_8_.refs_12_), channel_id=1, source_target_pairs={{0,1},{1,0},{2,3},{3,2},{4,5},{5,4},{6,7},{7,6},{8,9},{9,8},{10,11... | collective-permute-start | bytes 5013512 | tf_op jit(solution)/shard_map/ppermute | solution.py:764
  259.8 24.1 %collective-permute-start.11 = (bf16[8,136,768]{2,1,0:T(8,128)(2,1)}, bf16[8,136,768]{2,1,0:T(8,128)(2,1)}, u32[]{:S(2)}, u32[]{:S(2)}) collective-permute-start(bf16[8,136,768]{2,1,0:T(8,128)(2,1)} %copy-done.4), channel_id=1, source_target_pairs={{0,1},{1,0},{2,3},{3,2},{4,5},{5,4},{6,7},{7,6},{8,9},{9,8},{10,11... | collective-permute-start | bytes 5013512 | tf_op jit(solution)/shard_map/ppermute | solution.py:764
  261.1 6.6 %collective-permute-start.17 = (bf16[384,128]{1,0:T(8,128)(2,1)S(1)}, bf16[384,128]{1,0:T(8,128)(2,1)S(1)}, u32[]{:S(2)}, u32[]{:S(2)}) collective-permute-start(bf16[384,128]{1,0:T(8,128)(2,1)S(1)} %get-tuple-element.198), channel_id=1, source_target_pairs={{0,1},{1,0},{2,3},{3,2},{4,5},{5,4},{6,7},{7,6},{8,9},{9,8},{10,11... | collective-permute-start | bytes 294920 | tf_op jit(solution)/shard_map/ppermute | solution.py:764
  269.3 11.2 %copy-start.59 = (s32[32]{0:T(128)S(1)}, s32[32]{0:T(128)}, u32[]{:S(2)}) copy-start(s32[32]{0:T(128)} %param.26) | copy-start | bytes 388
  278.7 20.4 %collective-permute-start.20 = (bf16[8,8,6272]{2,1,0:T(8,128)(2,1)}, bf16[8,8,6272]{2,1,0:T(8,128)(2,1)S(1)}, u32[]{:S(2)}, u32[]{:S(2)}) collective-permute-start(bf16[8,8,6272]{2,1,0:T(8,128)(2,1)} %get-tuple-element.141), channel_id=1, source_target_pairs={{0,2},{2,0},{1,3},{3,1},{4,6},{6,4},{5,7},{7,5},{8,10},{10,8},{9,1... | collective-permute-start | bytes 2408456 | tf_op jit(solution)/shard_map/ppermute | solution.py:764
  279.8 20.2 %collective-permute-start.21 = (bf16[8,8,6272]{2,1,0:T(8,128)(2,1)}, bf16[8,8,6272]{2,1,0:T(8,128)(2,1)S(1)}, u32[]{:S(2)}, u32[]{:S(2)}) collective-permute-start(bf16[8,8,6272]{2,1,0:T(8,128)(2,1)} %get-tuple-element.142), channel_id=1, source_target_pairs={{0,4},{4,0},{8,12},{12,8},{16,20},{20,16},{24,28},{28,24},{1,5},{5... | collective-permute-start | bytes 2408456 | tf_op jit(solution)/shard_map/ppermute | solution.py:764
  280.5 34.5 %collective-permute-start.22 = (bf16[8,8,6272]{2,1,0:T(8,128)(2,1)}, bf16[8,8,6272]{2,1,0:T(8,128)(2,1)S(1)}, u32[]{:S(2)}, u32[]{:S(2)}) collective-permute-start(bf16[8,8,6272]{2,1,0:T(8,128)(2,1)} %get-tuple-element.143), channel_id=1, source_target_pairs={{0,8},{4,12},{8,0},{12,4},{16,24},{20,28},{24,16},{28,20},{1,9},{5... | collective-permute-start | bytes 2408456 | tf_op jit(solution)/shard_map/ppermute | solution.py:764
  299.1 15.9 %copy-start.14 = (bf16[8,8,6272]{2,1,0:T(8,128)(2,1)}, bf16[8,8,6272]{2,1,0:T(8,128)(2,1)S(1)}, u32[]{:S(2)}) copy-start(bf16[8,8,6272]{2,1,0:T(8,128)(2,1)S(1)} %collective-permute-done.20.refs_7_.refs_10_) | copy-start | bytes 2408452
  300.0 15.0 %copy-start.15 = (bf16[8,8,6272]{2,1,0:T(8,128)(2,1)}, bf16[8,8,6272]{2,1,0:T(8,128)(2,1)S(1)}, u32[]{:S(2)}) copy-start(bf16[8,8,6272]{2,1,0:T(8,128)(2,1)S(1)} %collective-permute-done.21.refs_8_.refs_11_) | copy-start | bytes 2408452
  320.5 9.8 %collective-permute-start.23 = (bf16[4,8,6272]{2,1,0:T(8,128)(2,1)}, bf16[4,8,6272]{2,1,0:T(8,128)(2,1)S(1)}, u32[]{:S(2)}, u32[]{:S(2)}) collective-permute-start(bf16[4,8,6272]{2,1,0:T(8,128)(2,1)} %get-tuple-element.147), channel_id=1, source_target_pairs={{0,4},{4,0},{8,12},{12,8},{16,20},{20,16},{24,28},{28,24},{1,5},{5... | collective-permute-start | bytes 1204232 | tf_op jit(solution)/shard_map/ppermute | solution.py:764
  320.5 19.0 %collective-permute-start.24 = (bf16[4,8,6272]{2,1,0:T(8,128)(2,1)}, bf16[4,8,6272]{2,1,0:T(8,128)(2,1)S(1)}, u32[]{:S(2)}, u32[]{:S(2)}) collective-permute-start(bf16[4,8,6272]{2,1,0:T(8,128)(2,1)} %get-tuple-element.148), channel_id=1, source_target_pairs={{0,8},{4,12},{8,0},{12,4},{16,24},{20,28},{24,16},{28,20},{1,9},{5... | collective-permute-start | bytes 1204232 | tf_op jit(solution)/shard_map/ppermute | solution.py:764
  320.6 18.9 %collective-permute-start.25 = (bf16[4,8,6272]{2,1,0:T(8,128)(2,1)}, bf16[4,8,6272]{2,1,0:T(8,128)(2,1)S(1)}, u32[]{:S(2)}, u32[]{:S(2)}) collective-permute-start(bf16[4,8,6272]{2,1,0:T(8,128)(2,1)} %get-tuple-element.149), channel_id=1, source_target_pairs={{0,2},{2,0},{1,3},{3,1},{4,6},{6,4},{5,7},{7,5},{8,10},{10,8},{9,1... | collective-permute-start | bytes 1204232 | tf_op jit(solution)/shard_map/ppermute | solution.py:764
  343.8 6.3 %collective-permute-start.26 = (bf16[2,8,6272]{2,1,0:T(8,128)(2,1)}, bf16[2,8,6272]{2,1,0:T(8,128)(2,1)S(1)}, u32[]{:S(2)}, u32[]{:S(2)}) collective-permute-start(bf16[2,8,6272]{2,1,0:T(8,128)(2,1)} %get-tuple-element.153), channel_id=1, source_target_pairs={{0,8},{4,12},{8,0},{12,4},{16,24},{20,28},{24,16},{28,20},{1,9},{5... | collective-permute-start | bytes 602120 | tf_op jit(solution)/shard_map/ppermute | solution.py:764
  344.2 6.0 %collective-permute-start.27 = (bf16[2,8,6272]{2,1,0:T(8,128)(2,1)}, bf16[2,8,6272]{2,1,0:T(8,128)(2,1)S(1)}, u32[]{:S(2)}, u32[]{:S(2)}) collective-permute-start(bf16[2,8,6272]{2,1,0:T(8,128)(2,1)} %get-tuple-element.154), channel_id=1, source_target_pairs={{0,2},{2,0},{1,3},{3,1},{4,6},{6,4},{5,7},{7,5},{8,10},{10,8},{9,1... | collective-permute-start | bytes 602120 | tf_op jit(solution)/shard_map/ppermute | solution.py:764
  345.7 5.9 %collective-permute-start.28 = (bf16[2,8,6272]{2,1,0:T(8,128)(2,1)}, bf16[2,8,6272]{2,1,0:T(8,128)(2,1)S(1)}, u32[]{:S(2)}, u32[]{:S(2)}) collective-permute-start(bf16[2,8,6272]{2,1,0:T(8,128)(2,1)} %get-tuple-element.155), channel_id=1, source_target_pairs={{0,4},{4,0},{8,12},{12,8},{16,20},{20,16},{24,28},{28,24},{1,5},{5... | collective-permute-start | bytes 602120 | tf_op jit(solution)/shard_map/ppermute | solution.py:764
  356.2 13.3 %collective-permute-start.29 = (bf16[3,8,6272]{2,1,0:T(8,128)(2,1)S(1)}, bf16[3,8,6272]{2,1,0:T(8,128)(2,1)S(1)}, u32[]{:S(2)}, u32[]{:S(2)}) collective-permute-start(bf16[3,8,6272]{2,1,0:T(8,128)(2,1)S(1)} %pad_maximum_fusion), channel_id=1, source_target_pairs={{0,16},{4,20},{8,24},{12,28},{16,0},{20,4},{24,8},{28,12},{1,17},{... | collective-permute-start | bytes 903176 | tf_op jit(solution)/shard_map/ppermute | solution.py:764
  373.1 14.5 %collective-permute-start.30 = (bf16[3,8,6272]{2,1,0:T(8,128)(2,1)S(1)}, bf16[3,8,6272]{2,1,0:T(8,128)(2,1)S(1)}, u32[]{:S(2)}, u32[]{:S(2)}) collective-permute-start(bf16[3,8,6272]{2,1,0:T(8,128)(2,1)S(1)} %pad_maximum_fusion.1), channel_id=1, source_target_pairs={{0,16},{4,20},{8,24},{12,28},{16,0},{20,4},{24,8},{28,12},{1,17},{... | collective-permute-start | bytes 903176 | tf_op jit(solution)/shard_map/ppermute | solution.py:764
  391.0 7.1 %collective-permute-start.31 = (bf16[2,8,6272]{2,1,0:T(8,128)(2,1)}, bf16[2,8,6272]{2,1,0:T(8,128)(2,1)S(1)}, u32[]{:S(2)}, u32[]{:S(2)}) collective-permute-start(bf16[2,8,6272]{2,1,0:T(8,128)(2,1)} %get-tuple-element.165.refs_1_.refs_7_), channel_id=1, source_target_pairs={{0,8},{4,12},{8,0},{12,4},{16,24},{20,28},{24,16},{28,20},{1,9},{5... | collective-permute-start | bytes 602120 | tf_op jit(solution)/shard_map/ppermute | solution.py:764
  391.0 7.2 %collective-permute-start.32 = (bf16[2,8,6272]{2,1,0:T(8,128)(2,1)}, bf16[2,8,6272]{2,1,0:T(8,128)(2,1)S(1)}, u32[]{:S(2)}, u32[]{:S(2)}) collective-permute-start(bf16[2,8,6272]{2,1,0:T(8,128)(2,1)} %get-tuple-element.166.refs_2_), channel_id=1, source_target_pairs={{0,2},{2,0},{1,3},{3,1},{4,6},{6,4},{5,7},{7,5},{8,10},{10,8},{9,1... | collective-permute-start | bytes 602120 | tf_op jit(solution)/shard_map/ppermute | solution.py:764
  392.3 6.8 %collective-permute-start.33 = (bf16[2,8,6272]{2,1,0:T(8,128)(2,1)}, bf16[2,8,6272]{2,1,0:T(8,128)(2,1)S(1)}, u32[]{:S(2)}, u32[]{:S(2)}) collective-permute-start(bf16[2,8,6272]{2,1,0:T(8,128)(2,1)} %get-tuple-element.167.refs_3_), channel_id=1, source_target_pairs={{0,4},{4,0},{8,12},{12,8},{16,20},{20,16},{24,28},{28,24},{1,5},{5... | collective-permute-start | bytes 602120 | tf_op jit(solution)/shard_map/ppermute | solution.py:764
  403.1 13.0 %collective-permute-start.34 = (bf16[4,8,6272]{2,1,0:T(8,128)(2,1)}, bf16[4,8,6272]{2,1,0:T(8,128)(2,1)S(1)}, u32[]{:S(2)}, u32[]{:S(2)}) collective-permute-start(bf16[4,8,6272]{2,1,0:T(8,128)(2,1)} %get-tuple-element.168.refs_1_.refs_7_), channel_id=1, source_target_pairs={{0,4},{4,0},{8,12},{12,8},{16,20},{20,16},{24,28},{28,24},{1,5},{5... | collective-permute-start | bytes 1204232 | tf_op jit(solution)/shard_map/ppermute | solution.py:764
  403.9 12.2 %collective-permute-start.35 = (bf16[4,8,6272]{2,1,0:T(8,128)(2,1)}, bf16[4,8,6272]{2,1,0:T(8,128)(2,1)S(1)}, u32[]{:S(2)}, u32[]{:S(2)}) collective-permute-start(bf16[4,8,6272]{2,1,0:T(8,128)(2,1)} %get-tuple-element.169.refs_2_), channel_id=1, source_target_pairs={{0,8},{4,12},{8,0},{12,4},{16,24},{20,28},{24,16},{28,20},{1,9},{5... | collective-permute-start | bytes 1204232 | tf_op jit(solution)/shard_map/ppermute | solution.py:764
  405.6 10.5 %collective-permute-start.36 = (bf16[4,8,6272]{2,1,0:T(8,128)(2,1)}, bf16[4,8,6272]{2,1,0:T(8,128)(2,1)S(1)}, u32[]{:S(2)}, u32[]{:S(2)}) collective-permute-start(bf16[4,8,6272]{2,1,0:T(8,128)(2,1)} %get-tuple-element.170.refs_3_), channel_id=1, source_target_pairs={{0,2},{2,0},{1,3},{3,1},{4,6},{6,4},{5,7},{7,5},{8,10},{10,8},{9,1... | collective-permute-start | bytes 1204232 | tf_op jit(solution)/shard_map/ppermute | solution.py:764
  421.0 18.0 %collective-permute-start.39 = (bf16[8,8,6272]{2,1,0:T(8,128)(2,1)}, bf16[8,8,6272]{2,1,0:T(8,128)(2,1)S(1)}, u32[]{:S(2)}, u32[]{:S(2)}) collective-permute-start(bf16[8,8,6272]{2,1,0:T(8,128)(2,1)} %get-tuple-element.172.refs_2_.refs_14_), channel_id=1, source_target_pairs={{0,2},{2,0},{1,3},{3,1},{4,6},{6,4},{5,7},{7,5},{8,10},{10,8},{9,1... | collective-permute-start | bytes 2408456 | tf_op jit(solution)/shard_map/ppermute | solution.py:764
  422.0 17.4 %collective-permute-start.40 = (bf16[8,8,6272]{2,1,0:T(8,128)(2,1)}, bf16[8,8,6272]{2,1,0:T(8,128)(2,1)S(1)}, u32[]{:S(2)}, u32[]{:S(2)}) collective-permute-start(bf16[8,8,6272]{2,1,0:T(8,128)(2,1)} %get-tuple-element.173.refs_3_), channel_id=1, source_target_pairs={{0,4},{4,0},{8,12},{12,8},{16,20},{20,16},{24,28},{28,24},{1,5},{5... | collective-permute-start | bytes 2408456 | tf_op jit(solution)/shard_map/ppermute | solution.py:764
  423.3 17.2 %collective-permute-start.41 = (bf16[8,8,6272]{2,1,0:T(8,128)(2,1)}, bf16[8,8,6272]{2,1,0:T(8,128)(2,1)S(1)}, u32[]{:S(2)}, u32[]{:S(2)}) collective-permute-start(bf16[8,8,6272]{2,1,0:T(8,128)(2,1)} %get-tuple-element.174.refs_4_), channel_id=1, source_target_pairs={{0,8},{4,12},{8,0},{12,4},{16,24},{20,28},{24,16},{28,20},{1,9},{5... | collective-permute-start | bytes 2408456 | tf_op jit(solution)/shard_map/ppermute | solution.py:764
  423.6 16.9 %collective-permute-start.42 = (bf16[8,8,6272]{2,1,0:T(8,128)(2,1)}, bf16[8,8,6272]{2,1,0:T(8,128)(2,1)S(1)}, u32[]{:S(2)}, u32[]{:S(2)}) collective-permute-start(bf16[8,8,6272]{2,1,0:T(8,128)(2,1)} %get-tuple-element.172.refs_2_.refs_14_), channel_id=1, source_target_pairs={{0,1},{1,0},{2,3},{3,2},{4,5},{5,4},{6,7},{7,6},{8,9},{9,8},{10,11... | collective-permute-start | bytes 2408456 | tf_op jit(solution)/shard_map/ppermute | solution.py:764
  423.6 17.4 %collective-permute-start.43 = (bf16[8,8,6272]{2,1,0:T(8,128)(2,1)}, bf16[8,8,6272]{2,1,0:T(8,128)(2,1)S(1)}, u32[]{:S(2)}, u32[]{:S(2)}) collective-permute-start(bf16[8,8,6272]{2,1,0:T(8,128)(2,1)} %get-tuple-element.173.refs_3_), channel_id=1, source_target_pairs={{0,1},{1,0},{2,3},{3,2},{4,5},{5,4},{6,7},{7,6},{8,9},{9,8},{10,11... | collective-permute-start | bytes 2408456 | tf_op jit(solution)/shard_map/ppermute | solution.py:764
  439.0 2.5 collective-permute-start.44
  439.5 3.0 collective-permute-start.45
  440.5 4.2 collective-permute-start.46
  440.6 5.1 %collective-permute-start.47 = (bf16[8,8,6272]{2,1,0:T(8,128)(2,1)S(1)}, bf16[8,8,6272]{2,1,0:T(8,128)(2,1)}, u32[]{:S(2)}, u32[]{:S(2)}) collective-permute-start(bf16[8,8,6272]{2,1,0:T(8,128)(2,1)S(1)} %collective-permute-done.41.refs_7_), channel_id=1, source_target_pairs={{0,1},{1,0},{2,3},{3,2},{4,5},{5,4},{6,7},{7,6},{8,9},{9,8},{10,11... | collective-permute-start | bytes 2408456 | tf_op jit(solution)/shard_map/ppermute | solution.py:764
  445.7 11.4 %copy-start.1 = (s32[32,136]{1,0:T(8,128)S(1)}, s32[32,136]{1,0:T(8,128)}, u32[]{:S(2)}) copy-start(s32[32,136]{1,0:T(8,128)} %param.25) | copy-start | bytes 52228
  (49 other events, 157.8 us)
Sparse Core Ops, SparseCore 0:
  246.4 91.7 all-gather.1
